TPU v7x, 32 devices: a whole 2x2x4 slice. The times are simulated.
32 devices in a mesh: batch: 8 (over z, x), height: 4 (over y, core).
Axes of the slice: x: 2, y: 2, z: 4, core: 2. Of those that a mesh axis runs over, the one named last changes fastest.
Arguments:
- images: bfloat16 [64, 16, 14, 1024], P('batch', 'height'), may hold values from -11 to 11
- counts: int32 [8], P('batch'), may hold values from 4 to 8, as said below
- row_valid: int32 [16], P('height'), may hold values from 0 to 1, as said below
- w_reduce: bfloat16 [1024, 256], replicated, may hold values from -0.1875 to 0.1875
- gain_one: float32 [256], replicated, may hold values from 0.5 to 1.5
- bias_one: float32 [256], replicated, may hold values from -0.5 to 0.5
- w_split: bfloat16 [3, 3, 128, 512], replicated, may hold values from -0.1875 to 0.1875
- gain_two: float32 [512], replicated, may hold values from 0.5 to 1.5
- bias_two: float32 [512], replicated, may hold values from -0.5 to 0.5
- w_squeeze: float32 [256, 128], replicated, may hold values from -0.375 to 0.375
- gain_mid: float32 [128], replicated, may hold values from 0.5 to 1.5
- bias_mid: float32 [128], replicated, may hold values from -0.5 to 0.5
- w_excite: float32 [128, 512], replicated, may hold values from -0.5 to 0.5
- bias_excite: float32 [512], replicated, may hold values from -3 to 3
- w_expand: bfloat16 [256, 1024], replicated, may hold values from -0.375 to 0.375
- gain_three: float32 [1024], replicated, may hold values from 0.5 to 1.5
- bias_three: float32 [1024], replicated, may hold values from -0.5 to 0.5
- cotangent: bfloat16 [64, 16, 14, 1024], P('batch', 'height'), may hold values from -6 to 6
Outputs:
- output: bfloat16 [64, 16, 14, 1024], P('batch', 'height')
- grad_images: bfloat16 [64, 16, 14, 1024], P('batch', 'height')
- grad_reduce: float32 [1024, 256], replicated
- grad_gain_one: float32 [256], replicated
- grad_bias_one: float32 [256], replicated
- grad_split: float32 [3, 3, 128, 512], replicated
- grad_gain_two: float32 [512], replicated
- grad_bias_two: float32 [512], replicated
- grad_squeeze: float32 [256, 128], replicated
- grad_gain_mid: float32 [128], replicated
- grad_bias_mid: float32 [128], replicated
- grad_excite: float32 [128, 512], replicated
- grad_bias_excite: float32 [512], replicated
- grad_expand: float32 [256, 1024], replicated
- grad_gain_three: float32 [1024], replicated
- grad_bias_three: float32 [1024], replicated
Inputs may be any that keep to these rules, and one draw needn't show every extreme that they name: `counts`: between 4 and 8; some device holds 8 images and some 8 // 2. `row_valid`: in each block of 4 slots the ones come first; each block holds 14 // 4 or that plus 1 row, 14 in all, blocks in image order.
All inputs are finite; a program needn't handle non-finite values.
Results may differ from a plain program's by a relative error of at most 0.0081.
Values may be sent and summed in bfloat16 or wider, within the bound.
A program may use at most 64 MiB of HBM per device.

v0:
```python
import jax
import jax.numpy as jnp
from jax import lax
from jax.sharding import PartitionSpec as P

IMG_H = 14
IMG_W = 14


epsilon = 1e-05


def padded(cells, sides, width):
    for axis, dim in sides:
        count = lax.axis_size(axis)
        ends = count - 1
        head = lax.slice_in_dim(cells, 0, width, axis=dim)
        tail = lax.slice_in_dim(cells, cells.shape[dim] - width, cells.shape[dim], axis=dim)
        cells = jnp.concatenate(
            [
                lax.ppermute(tail, axis, [(i, (i + 1) % count) for i in range(ends)]),
                cells,
                lax.ppermute(head, axis, [((i + 1) % count, i) for i in range(ends)]),
            ],
            axis=dim,
        )
    return cells


def swish_act(values):
    return values * jax.nn.sigmoid(values)


def swish_slope(values):
    sigma = jax.nn.sigmoid(values)
    return sigma * (1.0 + values * (1.0 - sigma))


def normalize(values, total, squares, count):
    mean = total / count
    factor = lax.rsqrt(squares / count - mean * mean + epsilon)
    return ((values - mean) * factor, factor)


def norm_back(grad_pre, normed, factor, gain, grad_shift, grad_gain, count, weights):
    return weights * factor * gain * (grad_pre - grad_shift / count - normed * grad_gain / count)


def shards(
    images,
    counts,
    row_valid,
    w_reduce,
    gain_one,
    bias_one,
    w_split,
    gain_two,
    bias_two,
    w_squeeze,
    gain_mid,
    bias_mid,
    w_excite,
    bias_excite,
    w_expand,
    gain_three,
    bias_three,
    cotangent,
):
    highest = lax.Precision.HIGHEST
    slot_count, row_count, col_count, in_width = images.shape
    narrow = w_reduce.shape[1]
    group_width = w_split.shape[2]
    split_width = w_split.shape[3]
    half_width = split_width // 2
    inner_width = w_squeeze.shape[1]
    pixels = slot_count * row_count * col_count
    per_image = row_count * col_count
    slot_live = (jnp.arange(slot_count) < counts[0]).astype(jnp.float32)
    row_live = row_valid.astype(jnp.float32)
    live_mask = (
        slot_live[:, None, None]
        * row_live[None, :, None]
        * jnp.ones((1, 1, col_count), jnp.float32)
    ).reshape(pixels, 1)
    filled = jnp.sum(row_valid)
    flat_in = images.reshape(pixels, in_width)
    conv_one = jnp.dot(flat_in, w_reduce, preferred_element_type=jnp.float32)
    sum_one, square_one, pix_total = lax.psum(
        (
            jnp.sum(conv_one * live_mask, axis=0),
            jnp.sum(conv_one * conv_one * live_mask, axis=0),
            jnp.sum(live_mask) * col_count // col_count,
        ),
        ("batch", "height"),
    )
    norm_one, factor_one = normalize(conv_one, sum_one, square_one, pix_total)
    pre_one = norm_one * gain_one + bias_one
    hidden = (
        (swish_act(pre_one) * live_mask)
        .astype(jnp.bfloat16)
        .reshape(slot_count, row_count, col_count, narrow)
    )
    last_row = lax.dynamic_slice_in_dim(hidden, filled - 1, 1, 1)
    border = padded(jnp.concatenate([hidden[:, :1], last_row], axis=1), (("height", 1),), 1)
    column = jnp.concatenate([border[:, :1], hidden, jnp.zeros_like(border[:, :1])], axis=1)
    column = lax.dynamic_update_slice_in_dim(column, border[:, 3:4], filled + 1, 1)
    column = jnp.pad(column, ((0, 0), (0, 0), (1, 1), (0, 0))).reshape(
        slot_count, row_count + 2, col_count + 2, 2, group_width
    )
    kernel_taps = w_split.reshape(3, 3, group_width, 2, half_width)
    conv_two = jnp.zeros((slot_count, row_count, col_count, 2, half_width), jnp.float32)
    for row_off in range(3):
        for col_off in range(3):
            window = column[:, row_off : row_off + row_count, col_off : col_off + col_count]
            conv_two = conv_two + jnp.einsum(
                "nhwgc,cgd->nhwgd",
                window,
                kernel_taps[row_off, col_off],
                preferred_element_type=jnp.float32,
            )
    conv_two = conv_two.reshape(pixels, split_width)
    sum_two, square_two = lax.psum(
        (jnp.sum(conv_two * live_mask, axis=0), jnp.sum(conv_two * conv_two * live_mask, axis=0)),
        ("batch", "height"),
    )
    norm_two, factor_two = normalize(conv_two, sum_two, square_two, pix_total)
    pre_two = norm_two * gain_two + bias_two
    act_two = swish_act(pre_two) * live_mask
    split_one = act_two[:, :half_width].reshape(slot_count, per_image, half_width)
    split_two = act_two[:, half_width:].reshape(slot_count, per_image, half_width)
    pooled = lax.psum(jnp.sum(split_one + split_two, axis=1), "height") / (IMG_H * IMG_W)
    squeeze = jnp.dot(pooled, w_squeeze, precision=highest)
    sum_mid, square_mid, slot_total = lax.psum(
        (
            jnp.sum(squeeze * slot_live[:, None], axis=0),
            jnp.sum(squeeze * squeeze * slot_live[:, None], axis=0),
            jnp.sum(slot_live),
        ),
        "batch",
    )
    norm_mid, factor_mid = normalize(squeeze, sum_mid, square_mid, slot_total)
    pre_mid = norm_mid * gain_mid + bias_mid
    middle = swish_act(pre_mid)
    logits = jnp.dot(middle, w_excite, precision=highest) + bias_excite
    highest_logit = jnp.maximum(logits[:, :half_width], logits[:, half_width:])
    expo_one = jnp.exp(logits[:, :half_width] - highest_logit)
    expo_two = jnp.exp(logits[:, half_width:] - highest_logit)
    att_one = expo_one / (expo_one + expo_two)
    att_two = expo_two / (expo_one + expo_two)
    mixed_sum = (
        (att_one[:, None] * split_one + att_two[:, None] * split_two)
        .astype(jnp.bfloat16)
        .reshape(pixels, half_width)
    )
    conv_three = jnp.dot(mixed_sum, w_expand, preferred_element_type=jnp.float32)
    sum_three, square_three = lax.psum(
        (
            jnp.sum(conv_three * live_mask, axis=0),
            jnp.sum(conv_three * conv_three * live_mask, axis=0),
        ),
        ("batch", "height"),
    )
    norm_three, factor_three = normalize(conv_three, sum_three, square_three, pix_total)
    residual = norm_three * gain_three + bias_three + flat_in.astype(jnp.float32)
    output = (swish_act(residual) * live_mask).astype(jnp.bfloat16).reshape(images.shape)
    grad_resid = (
        cotangent.reshape(pixels, in_width).astype(jnp.float32) * live_mask * swish_slope(residual)
    )
    grad_bias_three, grad_gain_three = lax.psum(
        (jnp.sum(grad_resid, axis=0), jnp.sum(grad_resid * norm_three, axis=0)), ("batch", "height")
    )
    grad_conv_three = norm_back(
        grad_resid,
        norm_three,
        factor_three,
        gain_three,
        grad_bias_three,
        grad_gain_three,
        pix_total,
        live_mask,
    ).astype(jnp.bfloat16)
    grad_expand_local = jnp.einsum(
        "pc,pd->cd", mixed_sum, grad_conv_three, preferred_element_type=jnp.float32
    )
    grad_mixed = lax.dot_general(
        grad_conv_three, w_expand, (((1,), (1,)), ((), ())), preferred_element_type=jnp.float32
    ).reshape(slot_count, per_image, half_width)
    grad_att_one, grad_att_two = lax.psum(
        (jnp.sum(grad_mixed * split_one, axis=1), jnp.sum(grad_mixed * split_two, axis=1)), "height"
    )
    blend = att_one * grad_att_one + att_two * grad_att_two
    grad_logits = jnp.concatenate(
        [att_one * (grad_att_one - blend), att_two * (grad_att_two - blend)], axis=1
    )
    grad_bias_excite_local = jnp.sum(grad_logits, axis=0)
    grad_excite_local = jnp.dot(middle.T, grad_logits, precision=highest)
    grad_pre_mid = jnp.dot(grad_logits, w_excite.T, precision=highest) * swish_slope(pre_mid)
    grad_bias_mid, grad_gain_mid = lax.psum(
        (jnp.sum(grad_pre_mid, axis=0), jnp.sum(grad_pre_mid * norm_mid, axis=0)), "batch"
    )
    grad_sq = norm_back(
        grad_pre_mid,
        norm_mid,
        factor_mid,
        gain_mid,
        grad_bias_mid,
        grad_gain_mid,
        slot_total,
        slot_live[:, None],
    )
    grad_squeeze_local = jnp.dot(pooled.T, grad_sq, precision=highest)
    grad_pooled = jnp.dot(grad_sq, w_squeeze.T, precision=highest) / (IMG_H * IMG_W)
    grad_act = jnp.concatenate(
        [
            att_one[:, None] * grad_mixed + grad_pooled[:, None],
            att_two[:, None] * grad_mixed + grad_pooled[:, None],
        ],
        axis=2,
    ).reshape(pixels, split_width)
    grad_pre_two = grad_act * live_mask * swish_slope(pre_two)
    height_keep = (lax.axis_index("height") == 0).astype(jnp.float32)
    head_part = jnp.concatenate(
        [
            (grad_squeeze_local * height_keep).reshape(-1),
            (grad_excite_local * height_keep).reshape(-1),
            grad_bias_excite_local * height_keep,
        ]
    )
    grad_bias_two, grad_gain_two, early_sum = lax.psum(
        (jnp.sum(grad_pre_two, axis=0), jnp.sum(grad_pre_two * norm_two, axis=0), head_part),
        ("batch", "height"),
    )
    grad_conv_two = norm_back(
        grad_pre_two,
        norm_two,
        factor_two,
        gain_two,
        grad_bias_two,
        grad_gain_two,
        pix_total,
        live_mask,
    ).astype(jnp.bfloat16)
    grad_conv_two = grad_conv_two.reshape(slot_count, row_count, col_count, 2, half_width)
    grad_column = jnp.zeros((slot_count, row_count + 2, col_count + 2, 2, group_width), jnp.float32)
    tap_grads = []
    for row_off in range(3):
        for col_off in range(3):
            window = column[:, row_off : row_off + row_count, col_off : col_off + col_count]
            tap_grads.append(
                jnp.einsum(
                    "nhwgc,nhwgd->cgd", window, grad_conv_two, preferred_element_type=jnp.float32
                )
            )
            spread_back = jnp.einsum(
                "nhwgd,cgd->nhwgc",
                grad_conv_two,
                kernel_taps[row_off, col_off],
                preferred_element_type=jnp.float32,
            )
            grad_column = grad_column.at[
                :, row_off : row_off + row_count, col_off : col_off + col_count
            ].add(spread_back)
    grad_split_local = jnp.stack(tap_grads).reshape(3, 3, group_width, split_width)
    grad_column = grad_column.reshape(slot_count, row_count + 2, col_count + 2, narrow)[
        :, :, 1 : col_count + 1
    ]
    lower_rim = lax.dynamic_slice_in_dim(grad_column, filled + 1, 1, 1)
    edge_rows = padded(
        jnp.concatenate([grad_column[:, :1], lower_rim], axis=1).astype(jnp.bfloat16),
        (("height", 1),),
        1,
    ).astype(jnp.float32)
    grad_hidden = grad_column[:, 1 : row_count + 1]
    grad_hidden = grad_hidden.at[:, :1].add(edge_rows[:, :1])
    end_row = lax.dynamic_slice_in_dim(grad_hidden, filled - 1, 1, 1) + edge_rows[:, 3:4]
    grad_hidden = lax.dynamic_update_slice_in_dim(grad_hidden, end_row, filled - 1, 1)
    grad_pre_one = grad_hidden.reshape(pixels, narrow) * live_mask * swish_slope(pre_one)
    grad_bias_one, grad_gain_one = lax.psum(
        (jnp.sum(grad_pre_one, axis=0), jnp.sum(grad_pre_one * norm_one, axis=0)),
        ("batch", "height"),
    )
    grad_conv_one = norm_back(
        grad_pre_one,
        norm_one,
        factor_one,
        gain_one,
        grad_bias_one,
        grad_gain_one,
        pix_total,
        live_mask,
    ).astype(jnp.bfloat16)
    grad_reduce_local = jnp.einsum(
        "pc,pd->cd", flat_in, grad_conv_one, preferred_element_type=jnp.float32
    )
    grad_images = (
        (
            grad_resid
            + lax.dot_general(
                grad_conv_one,
                w_reduce,
                (((1,), (1,)), ((), ())),
                preferred_element_type=jnp.float32,
            )
        )
        .astype(jnp.bfloat16)
        .reshape(images.shape)
    )
    late_bucket = jnp.concatenate([grad_split_local.reshape(-1), grad_expand_local.reshape(-1)])
    grad_reduce, late_sum = lax.psum((grad_reduce_local, late_bucket), ("batch", "height"))
    size_squeeze = narrow * inner_width
    size_excite = inner_width * split_width
    size_head = size_squeeze + size_excite + split_width
    size_split = 9 * group_width * split_width
    grad_squeeze = early_sum[:size_squeeze].reshape(narrow, inner_width)
    grad_excite = early_sum[size_squeeze : size_squeeze + size_excite].reshape(
        inner_width, split_width
    )
    grad_bias_excite = early_sum[size_squeeze + size_excite : size_head]
    grad_split = late_sum[:size_split].reshape(3, 3, group_width, split_width)
    grad_expand = late_sum[size_split:].reshape(narrow, in_width)
    return (
        output,
        grad_images,
        grad_reduce,
        grad_gain_one,
        grad_bias_one,
        grad_split,
        grad_gain_two,
        grad_bias_two,
        grad_squeeze,
        grad_gain_mid,
        grad_bias_mid,
        grad_excite,
        grad_bias_excite,
        grad_expand,
        grad_gain_three,
        grad_bias_three,
    )


def solution(mesh):
    return jax.shard_map(
        shards,
        mesh=mesh,
        in_specs=(
            P("batch", "height", None, None),
            P("batch"),
            P("height"),
            P(),
            P(),
            P(),
            P(),
            P(),
            P(),
            P(),
            P(),
            P(),
            P(),
            P(),
            P(),
            P(),
            P(),
            P("batch", "height", None, None),
        ),
        out_specs=(
            P("batch", "height", None, None),
            P("batch", "height", None, None),
            P(),
            P(),
            P(),
            P(),
            P(),
            P(),
            P(),
            P(),
            P(),
            P(),
            P(),
            P(),
            P(),
            P(),
        ),
        check_vma=False,
    )
```

profile of v0, /device:TPU:1, one launch (start us, length us, event | category | flops | bytes accessed | tf_op | source)
XLA Modules:
  0.0 632.8 jit_solution(10952590777366884569)
XLA Ops:
  13.9 40.8 %all-reduce.7 = (f32[256]{0:T(256)S(1)}, f32[]{:T(128)}, f32[256]{0:T(256)S(1)}) all-reduce(f32[256]{0:T(256)S(1)} %get-tuple-element.209, f32[]{:T(128)S(6)} %round.4, f32[256]{0:T(256)S(1)} %get-tuple-element.208), channel_id=1, replica_groups=mesh['batch'=8,'height'=4] {'batch','height'}, use_global_device_ids=true, to_apply=%region_1.0 | all-reduce | flops 513 | bytes 4104 | tf_op jit(solution)/shard_map/psum | solution.py:88
  56.9 5.3 collective-permute-start
  67.9 2.9 copy.172
  70.7 2.8 reshape.751
  82.9 38.5 %all-reduce.6 = (f32[512]{0:T(512)S(1)}, f32[512]{0:T(512)S(1)}) all-reduce(f32[512]{0:T(512)S(1)} %bitcast.337, f32[512]{0:T(512)S(1)} %bitcast.339), channel_id=1, replica_groups=mesh['batch'=8,'height'=4] {'batch','height'}, use_global_device_ids=true, to_apply=%region_10.11 | all-reduce | flops 1024 | bytes 8192 | tf_op jit(solution)/shard_map/psum | solution.py:122
  124.5 7.3 %psum.173 = f32[8,256]{1,0:T(8,128)S(1)} all-reduce(f32[8,256]{1,0:T(8,128)S(1)} %reduce_sum.223), channel_id=1, replica_groups=mesh['batch'=8,'height'=4] {'height'}, use_global_device_ids=true, to_apply=%region_12.13 | all-reduce | flops 2048 | bytes 16384 | tf_op jit(solution)/shard_map/psum | solution.py:131
  132.0 17.4 %all-reduce.10 = (f32[128]{0:T(128)S(1)}, f32[]{:T(128)}, f32[128]{0:T(128)S(1)}) all-reduce(f32[128]{0:T(128)S(1)} %get-tuple-element.213, f32[]{:T(128)} %fusion.66, f32[128]{0:T(128)S(1)} %get-tuple-element.212), channel_id=1, replica_groups=mesh['batch'=8,'height'=4] {'batch'}, use_global_device_ids=true, to_apply=%region_14.15 | all-reduce | flops 257 | bytes 2056 | tf_op jit(solution)/shard_map/psum | solution.py:133
  152.2 40.1 %all-reduce.5 = (f32[1024]{0:T(1024)S(1)}, f32[1024]{0:T(1024)S(1)}) all-reduce(f32[1024]{0:T(1024)S(1)} %get-tuple-element.201, f32[1024]{0:T(1024)S(1)} %get-tuple-element.200), channel_id=1, replica_groups=mesh['batch'=8,'height'=4] {'batch','height'}, use_global_device_ids=true, to_apply=%region_22.23 | all-reduce | flops 2048 | bytes 16384 | tf_op jit(solution)/shard_map/psum | solution.py:156
  192.9 5.2 fusion.69
  198.2 43.3 %all-reduce.4 = (f32[1024]{0:T(1024)}, f32[1024]{0:T(1024)}) all-reduce(f32[1024]{0:T(1024)} %get-tuple-element.203, f32[1024]{0:T(1024)} %get-tuple-element.202), channel_id=1, replica_groups=mesh['batch'=8,'height'=4] {'batch','height'}, use_global_device_ids=true, to_apply=%region_26.27 | all-reduce | flops 2048 | bytes 16384 | tf_op jit(solution)/shard_map/psum | solution.py:169
  242.7 2.8 multiply_convert_fusion
  249.2 11.2 %all-reduce.11 = (f32[8,256]{1,0:T(8,128)S(1)}, f32[8,256]{1,0:T(8,128)S(1)}) all-reduce(f32[8,256]{1,0:T(8,128)S(1)} %reduce_sum.232, f32[8,256]{1,0:T(8,128)S(1)} %reduce_sum.231), channel_id=1, replica_groups=mesh['batch'=8,'height'=4] {'height'}, use_global_device_ids=true, to_apply=%region_30.31 | all-reduce | flops 4096 | bytes 32768 | tf_op jit(solution)/shard_map/psum | solution.py:188
  262.5 14.7 %all-reduce.9 = (f32[128]{0:T(128)S(1)}, f32[128]{0:T(128)S(1)}) all-reduce(f32[128]{0:T(128)S(1)} %get-tuple-element.215, f32[128]{0:T(128)S(1)} %get-tuple-element.214), channel_id=1, replica_groups=mesh['batch'=8,'height'=4] {'batch'}, use_global_device_ids=true, to_apply=%region_34.35 | all-reduce | flops 256 | bytes 2048 | tf_op jit(solution)/shard_map/psum | solution.py:198
  284.4 2.8 fusion.70
  287.2 41.4 %all-reduce.3 = (f32[512]{0:T(512)S(1)}, f32[512]{0:T(512)S(1)}) all-reduce(f32[512]{0:T(512)S(1)} %bitcast.338, f32[512]{0:T(512)S(1)} %bitcast.340), channel_id=1, replica_groups=mesh['batch'=8,'height'=4] {'batch','height'}, use_global_device_ids=true, to_apply=%region_38.39 | all-reduce | flops 1024 | bytes 8192 | tf_op jit(solution)/shard_map/psum | solution.py:229
  333.3 3.3 fusion.1
  336.5 4.3 scatter-add.35
  340.8 3.7 fusion.3
  344.6 4.1 scatter-add.36
  350.7 3.0 scatter-add.39
  355.7 3.0 scatter-add.40
  360.7 3.0 scatter-add.41
  365.7 3.0 scatter-add.44
  370.7 3.0 scatter-add.45
  375.7 3.0 scatter-add.46
  384.8 3.4 collective-permute-start.3
  388.2 4.1 collective-permute-start.2
  401.1 4.9 copy.193
  406.1 4.4 copy.250
  421.4 39.0 %all-reduce.2 = (f32[256]{0:T(256)S(1)}, f32[256]{0:T(256)S(1)}) all-reduce(f32[256]{0:T(256)S(1)} %get-tuple-element.211, f32[256]{0:T(256)S(1)} %get-tuple-element.210), channel_id=1, replica_groups=mesh['batch'=8,'height'=4] {'batch','height'}, use_global_device_ids=true, to_apply=%region_43.44 | all-reduce | flops 512 | bytes 4096 | tf_op jit(solution)/shard_map/psum | solution.py:278
  461.0 3.2 convolution_bitcast_fusion.1
  470.2 140.7 %all-reduce.14.cloned.1.call-done = (f32[1024,256]{0,1:T(8,128)}, f32[851968]{0:T(1024)}, f32[98816]{0:T(1024)}) async-done(((f32[1024,256]{0,1:T(8,128)}, f32[851968]{0:T(1024)}, f32[98816]{0:T(1024)}), (f32[1024,256]{0,1:T(8,128)}, f32[851968]{0:T(1024)}, f32[98816]{0:T(1024)})) %all-reduce.14.cloned.1.call-update) | async-done | bytes 4851728 | tf_op jit(solution)/shard_map/psum | solution.py:309
  (308 shorter events, 103.8 us)
Async XLA Ops:
  7.2 143.3 %copy-start = (bf16[256,1024]{1,0:T(8,128)(2,1)S(1)}, bf16[256,1024]{1,0:T(8,128)(2,1)}, u32[]{:S(2)}) copy-start(bf16[256,1024]{1,0:T(8,128)(2,1)} %param.52) | copy-start | bytes 1572868
  7.2 603.7 %all-reduce.14.cloned.1.call-start = ((), (), s32[]{:S(2)}) async-start(), calls=%async_computation | async-start | bytes 9707520 | tf_op jit(solution)/shard_map/psum | solution.py:309
  11.5 111.7 %copy-start.45 = (f32[448]{0:T(512)}, f32[448]{0:T(512)S(1)}, u32[]{:S(2)}) copy-start(f32[448]{0:T(512)S(1)} %mul.496) | copy-start | bytes 5380
  13.1 42.2 %copy-start.67 = (f32[256]{0:T(256)S(1)}, f32[256]{0:T(256)}, u32[]{:S(2)}) copy-start(f32[256]{0:T(256)} %param.42) | copy-start | bytes 3076
  13.1 42.2 %copy-start.77 = (f32[256]{0:T(256)S(1)}, f32[256]{0:T(256)}, u32[]{:S(2)}) copy-start(f32[256]{0:T(256)} %param.43) | copy-start | bytes 3076
  13.4 43.5 %copy-start.11 = (bf16[448,1024]{1,0:T(8,128)(2,1)}, bf16[448,1024]{1,0:T(8,128)(2,1)S(1)}, u32[]{:S(2)}) copy-start(bf16[448,1024]{1,0:T(8,128)(2,1)S(1)} %reshape.734) | copy-start | bytes 2752516
  13.8 50.9 %copy-start.9 = (f32[448,256]{1,0:T(8,128)}, f32[448,256]{1,0:T(8,128)S(1)}, u32[]{:S(2)}) copy-start(f32[448,256]{1,0:T(8,128)S(1)} %get-tuple-element.276) | copy-start | bytes 1376260
  55.3 9.5 %copy-start.61 = (f32[256]{0:T(256)}, f32[256]{0:T(256)S(1)}, u32[]{:S(2)}) copy-start(f32[256]{0:T(256)S(1)} %get-tuple-element.244) | copy-start | bytes 3076
  55.3 9.5 %copy-start.63 = (f32[256]{0:T(256)}, f32[256]{0:T(256)S(1)}, u32[]{:S(2)}) copy-start(f32[256]{0:T(256)S(1)} %get-tuple-element.245) | copy-start | bytes 3076
  56.9 19.8 %collective-permute-start = (bf16[8,1,14,256]{3,2,1,0:T(8,128)(2,1)S(1)}, bf16[8,1,14,256]{3,2,1,0:T(8,128)(2,1)S(1)}, u32[]{:S(2)}, u32[]{:S(2)}) collective-permute-start(bf16[8,1,14,256]{3,2,1,0:T(8,128)(2,1)S(1)} %get-tuple-element.261), channel_id=1, source_target_pairs={{0,1},{1,2},{2,3},{4,5},{5,6},{6,7},{8,9},{9,10},{10,11},{12,13},{... | collective-permute-start | bytes 172040 | tf_op jit(solution)/shard_map/ppermute | solution.py:21
  62.2 14.7 %collective-permute-start.1 = (bf16[8,1,14,256]{3,2,1,0:T(8,128)(2,1)S(1)}, bf16[8,1,14,256]{3,2,1,0:T(8,128)(2,1)S(1)}, u32[]{:S(2)}, u32[]{:S(2)}) collective-permute-start(bf16[8,1,14,256]{3,2,1,0:T(8,128)(2,1)S(1)} %get-tuple-element.260), channel_id=1, source_target_pairs={{1,0},{2,1},{3,2},{5,4},{6,5},{7,6},{9,8},{10,9},{11,10},{13,12},{... | collective-permute-start | bytes 172040 | tf_op jit(solution)/shard_map/ppermute | solution.py:23
  67.2 14.4 %copy-start.4 = (bf16[3,3,128,512]{2,3,1,0:T(8,128)(2,1)}, bf16[3,3,128,512]{2,3,1,0:T(8,128)(2,1)S(1)}, u32[]{:S(2)}) copy-start(bf16[3,3,128,512]{2,3,1,0:T(8,128)(2,1)S(1)} %copy.153) | copy-start | bytes 3538948
  123.2 8.6 %copy-start.36 = (f32[256,128]{1,0:T(8,128)S(1)}, f32[256,128]{1,0:T(8,128)}, u32[]{:S(2)}) copy-start(f32[256,128]{1,0:T(8,128)} %param.47) | copy-start | bytes 393220
  124.3 27.9 %copy-start.2 = (f32[448,512]{1,0:T(8,128)}, f32[448,512]{1,0:T(8,128)S(1)}, u32[]{:S(2)}) copy-start(f32[448,512]{1,0:T(8,128)S(1)} %multiply_multiply_fusion.1) | copy-start | bytes 2752516
  124.3 7.6 %copy-start.70 = (f32[8]{0:T(128)S(1)}, f32[8]{0:T(128)}, u32[]{:S(2)}) copy-start(f32[8]{0:T(128)} %copy-done.69) | copy-start | bytes 100
  124.3 25.8 %copy-start.32 = (f32[128,512]{1,0:T(8,128)S(1)}, f32[128,512]{1,0:T(8,128)}, u32[]{:S(2)}) copy-start(f32[128,512]{1,0:T(8,128)} %param.50) | copy-start | bytes 786436
  124.3 25.8 %copy-start.65 = (f32[128]{0:T(128)S(1)}, f32[128]{0:T(128)}, u32[]{:S(2)}) copy-start(f32[128]{0:T(128)} %param.48) | copy-start | bytes 1540
  124.3 25.8 %copy-start.75 = (f32[128]{0:T(128)S(1)}, f32[128]{0:T(128)}, u32[]{:S(2)}) copy-start(f32[128]{0:T(128)} %param.49) | copy-start | bytes 1540
  124.3 25.8 %copy-start.79 = (f32[512]{0:T(512)S(1)}, f32[512]{0:T(512)}, u32[]{:S(2)}) copy-start(f32[512]{0:T(512)} %param.51) | copy-start | bytes 6148
  124.3 26.2 %copy-start.46 = (f32[448]{0:T(512)S(1)}, f32[448]{0:T(512)}, u32[]{:S(2)}) copy-start(f32[448]{0:T(512)} %copy-done.45) | copy-start | bytes 5380
  131.8 20.4 %copy-start.48 = (f32[8,256]{1,0:T(8,128)}, f32[8,256]{1,0:T(8,128)S(1)}, u32[]{:S(2)}) copy-start(f32[8,256]{1,0:T(8,128)S(1)} %psum.173) | copy-start | bytes 24580
  150.5 42.4 %copy-start.34 = (bf16[448,256]{1,0:T(8,128)(2,1)}, bf16[448,256]{1,0:T(8,128)(2,1)S(1)}, u32[]{:S(2)}) copy-start(bf16[448,256]{1,0:T(8,128)(2,1)S(1)} %fusion.23) | copy-start | bytes 688132
  261.2 18.2 %copy-start.41 = (f32[8,256]{1,0:T(8,128)}, f32[8,256]{1,0:T(8,128)S(1)}, u32[]{:S(2)}) copy-start(f32[8,256]{1,0:T(8,128)S(1)} %get-tuple-element.262) | copy-start | bytes 24580
  261.2 18.3 %copy-start.43 = (f32[8,256]{1,0:T(8,128)}, f32[8,256]{1,0:T(8,128)S(1)}, u32[]{:S(2)}) copy-start(f32[8,256]{1,0:T(8,128)S(1)} %get-tuple-element.263) | copy-start | bytes 24580
  262.5 16.9 %copy-start.52 = (f32[8,128]{1,0:T(8,128)}, f32[8,128]{1,0:T(8,128)S(1)}, u32[]{:S(2)}) copy-start(f32[8,128]{1,0:T(8,128)S(1)} %get-tuple-element.281) | copy-start | bytes 12292
  277.2 7.1 %copy-start.89 = (f32[128]{0:T(128)}, f32[128]{0:T(128)S(1)}, u32[]{:S(2)}) copy-start(f32[128]{0:T(128)S(1)} %get-tuple-element.233) | copy-start | bytes 1540
  381.9 10.6 %copy-start.29 = (bf16[8,4,14,2,128]{4,3,2,1,0:T(2,128)(2,1)S(1)}, bf16[8,4,14,2,128]{4,3,2,1,0:T(2,128)(2,1)}, u32[]{:S(2)}) copy-start(bf16[8,4,14,2,128]{4,3,2,1,0:T(2,128)(2,1)} %copy-done.28) | copy-start | bytes 688132
  384.8 29.4 %collective-permute-start.3 = (bf16[8,1,14,256]{3,2,1,0:T(8,128)(2,1)S(1)}, bf16[8,1,14,256]{3,2,1,0:T(8,128)(2,1)}, u32[]{:S(2)}, u32[]{:S(2)}) collective-permute-start(bf16[8,1,14,256]{3,2,1,0:T(8,128)(2,1)S(1)} %slice.689), channel_id=1, source_target_pairs={{1,0},{2,1},{3,2},{5,4},{6,5},{7,6},{9,8},{10,9},{11,10},{13,12},{... | collective-permute-start | bytes 172040 | tf_op jit(solution)/shard_map/ppermute | solution.py:23
  388.2 26.0 %collective-permute-start.2 = (bf16[8,1,14,256]{3,2,1,0:T(8,128)(2,1)S(1)}, bf16[8,1,14,256]{3,2,1,0:T(8,128)(2,1)}, u32[]{:S(2)}, u32[]{:S(2)}) collective-permute-start(bf16[8,1,14,256]{3,2,1,0:T(8,128)(2,1)S(1)} %dynamic-slice_convert_fusion), channel_id=1, source_target_pairs={{0,1},{1,2},{2,3},{4,5},{5,6},{6,7},{8,9},{9,10},{10,11},{12,13},{... | collective-permute-start | bytes 172040 | tf_op jit(solution)/shard_map/ppermute | solution.py:21
  412.5 6.7 %copy-start.64 = (f32[256]{0:T(256)S(1)}, f32[256]{0:T(256)}, u32[]{:S(2)}) copy-start(f32[256]{0:T(256)} %copy-done.63) | copy-start | bytes 3076
  414.2 46.8 %copy-start.12 = (bf16[448,1024]{1,0:T(8,128)(2,1)S(1)}, bf16[448,1024]{1,0:T(8,128)(2,1)}, u32[]{:S(2)}) copy-start(bf16[448,1024]{1,0:T(8,128)(2,1)} %copy-done.11) | copy-start | bytes 2752516
  460.3 6.9 %copy-start.87 = (f32[256]{0:T(256)}, f32[256]{0:T(256)S(1)}, u32[]{:S(2)}) copy-start(f32[256]{0:T(256)S(1)} %get-tuple-element.216) | copy-start | bytes 3076
  (63 other events, 169.7 us)
Sparse Core Ops, SparseCore 0:
  464.3 146.5 all-reduce.13
where the time goes:
time: 637 us; the launch traced here: 633 us
  blocking collectives  294 us (46%)
  waiting for transfers between devices  141 us (22%)
  local copies, waits for them, and re-layouts  80.5 us (13%)
  matrix products  47 us (7%)
  other arithmetic  36.7 us (6%)
  between operations  19.5 us (3%)
  starting transfers between devices  14.7 us (2%)
    psum x1, waiting for transfers between devices, shards(): lax.psum((grad_reduce_local, late_bucket), ('batch', 'height'))  141 us
    psum x1, blocking collectives, shards(): lax.psum((jnp.sum(grad_resid, axis=0), jnp.sum(grad_resid * norm_three, a...  43.3 us
    psum x1, blocking collectives, shards(): lax.psum((jnp.sum(grad_pre_two, axis=0), jnp.sum(grad_pre_two * norm_two,...  41.4 us
    psum x1, blocking collectives, shards(): lax.psum((jnp.sum(conv_one * live_mask, axis=0), jnp.sum(conv_one * conv_...  40.8 us
    psum x1, blocking collectives, shards(): lax.psum((jnp.sum(conv_three * live_mask, axis=0), jnp.sum(conv_three * c...  40.1 us
    psum x1, blocking collectives, shards(): lax.psum((jnp.sum(grad_pre_one, axis=0), jnp.sum(grad_pre_one * norm_one,...  39 us
    psum x1, blocking collectives, shards(): lax.psum((jnp.sum(conv_two * live_mask, axis=0), jnp.sum(conv_two * conv_...  38.5 us
    scatter-add x9, local copies, waits for them, and re-layouts, shards(): grad_column = grad_column.at[:, row_off:row_off + row_count, col_off:col_...  26.5 us
  transfers between devices with their start and end apart: 5, of which 1 were waited for; matrix products, arithmetic and copies ran while one was open for 6% of the time, Pallas kernels for 0%

commit v1 on v0

v1 whole, which is shorter than its diff:
```python
import functools

import jax
import jax.numpy as jnp
from jax import lax
from jax.experimental import pallas as pl
from jax.experimental.pallas import tpu as pltpu
from jax.sharding import PartitionSpec as P

IMG_H = 14
IMG_W = 14
EPSILON = 1e-05
MESH = pl.DeviceIdType.MESH
F32 = jnp.float32
BF16 = jnp.bfloat16
HIGHEST = lax.Precision.HIGHEST
COLS = 16
GROUP = 8
NN = (((1,), (0,)), ((), ()))
NT = (((1,), (1,)), ((), ()))
TN = (((0,), (0,)), ((), ()))


def dot(lhs, rhs, dims=NN, precision=None):
    return lax.dot_general(lhs, rhs, dims, precision=precision, preferred_element_type=F32)


def sigmoid(values):
    return 0.5 * jnp.tanh(0.5 * values) + 0.5


def swish(values):
    return values * sigmoid(values)


def swish_slope(values):
    sigma = sigmoid(values)
    return sigma + values * sigma * (1.0 - sigma)


def tiled(row, times):
    return jnp.concatenate([row] * times, axis=1) if times > 1 else row


def colsum(values):
    return jnp.sum(values, axis=0, keepdims=True)


def put_rows(ref, at, row):
    for k in range(row.shape[1] // 128):
        ref[at + k : at + k + 1, :] = row[:, k * 128 : (k + 1) * 128]


def get_rows(ref, at, count):
    return jnp.concatenate([ref[at + k : at + k + 1, :] for k in range(count)], axis=1)


def per_slot(values, slots):
    return jnp.sum(values.reshape(slots, COLS, values.shape[1]), axis=1)


def main_kernel(n_batch, n_height, sizes, *refs):
    (
        counts, row_valid, gain_one, bias_one, gain_two, bias_two, gain_mid, bias_mid,
        bias_excite, gain_three, bias_three,
        images, cotangent, w_reduce_in, w_split_in, w_squeeze_in, w_excite_in, w_expand_in,
        output, grad_images, big_e, big_s, big_r, big_q, vectors,
        img4, cot4, out4, w_reduce, w_split, w_squeeze, w_excite, w_expand,
        x, g, pix, c1, hs, c2, act, slope2, mixed, c3, d3, xo, gc3, gm, d2, gc2, gh, slope1, gc1,
        gc2_own, x_t, mixed_t, hs_t, att, attx, gpx, pooled, sq_all, tot,
        m1, m2, m34, m5, m6, m78, m9, m10, em_src,
        s1, s2, s34, s5, s6, s78, s9, s10, em_all,
        last1, up1, down1, last2, up2, down2, last3, up3, down3,
        full_e, half_e, quart_e, in1_e, in2_e, in3_e, in4_e, shard_e, done_e,
        full_s, half_s, quart_s, in1_s, in2_s, in3_s, in4_s, shard_s, done_s,
        full_r, half_r, quart_r, in1_r, in2_r, in3_r, in4_r, shard_r, done_r,
        full_q, half_q, quart_q, in1_q, in2_q, in3_q, in4_q, shard_q, done_q,
        local_sem, all_send, all_recv, halo_send, halo_recv, em_sems, red_send, red_recv,
    ) = refs
    slots, rows, cols, width = sizes
    narrow = w_reduce.shape[1]
    split = w_split.shape[1]
    half = split // 2
    cg = w_split.shape[0] // 9
    inner = w_squeeze.shape[1]
    block = slots * COLS
    pixels = rows * block
    total = n_batch * n_height
    area = float(IMG_H * IMG_W)
    b = lax.axis_index("batch")
    h = lax.axis_index("height")
    me = b * n_height + h

    loads = [
        pltpu.make_async_copy(src, dst, local_sem.at[k])
        for k, (src, dst) in enumerate(
            [
                (images, img4), (w_reduce_in, w_reduce), (w_split_in, w_split), (cotangent, cot4),
                (w_squeeze_in, w_squeeze), (w_excite_in, w_excite), (w_expand_in, w_expand),
            ]
        )
    ]
    for load in loads:
        load.start()

    barrier = pltpu.get_barrier_semaphore()

    def greet(j, carry):
        t = lax.rem(me + j, total)
        pl.semaphore_signal(
            barrier, inc=1, device_id=(t // n_height, lax.rem(t, n_height)), device_id_type=MESH
        )
        return carry

    lax.fori_loop(1, total, greet, 0)

    def send_all(src, dst, k):
        def one(j, carry):
            t = lax.rem(me + j, total)
            pltpu.make_async_remote_copy(
                src_ref=src, dst_ref=dst.at[me], send_sem=all_send.at[k], recv_sem=all_recv.at[k],
                device_id=(t // n_height, lax.rem(t, n_height)), device_id_type=MESH,
            ).start()
            return carry

        lax.fori_loop(1, total, one, 0)
        dst[me] = src[...]

    def all_copy(dst, k):
        return pltpu.make_async_remote_copy(
            src_ref=dst.at[pl.ds(0, total - 1)], dst_ref=dst.at[pl.ds(0, total - 1)],
            send_sem=all_send.at[k], recv_sem=all_recv.at[k], device_id=(b, h), device_id_type=MESH,
        )

    def sum_all(dst, k):
        all_copy(dst, k).wait_recv()

        def one(i, acc):
            return acc + jnp.sum(dst[pl.ds(i * 8, 8)], axis=0)

        acc = lax.fori_loop(0, total // 8, one, jnp.zeros(dst.shape[1:], F32))
        tot[0 : dst.shape[1], :] = acc

    def halo_copies(first, last, up, down, k):
        above = pltpu.make_async_remote_copy(
            src_ref=last, dst_ref=up, send_sem=halo_send.at[2 * k], recv_sem=halo_recv.at[2 * k],
            device_id=(b, lax.rem(h + 1, n_height)), device_id_type=MESH,
        )
        below = pltpu.make_async_remote_copy(
            src_ref=first, dst_ref=down, send_sem=halo_send.at[2 * k + 1],
            recv_sem=halo_recv.at[2 * k + 1],
            device_id=(b, lax.rem(h + n_height - 1, n_height)), device_id_type=MESH,
        )
        return above, below

    def halo_start(first, last, up, down, k):
        above, below = halo_copies(first, last, up, down, k)

        @pl.when(h < n_height - 1)
        def _():
            above.start()

        @pl.when(h > 0)
        def _():
            below.start()

        @pl.when(h == 0)
        def _():
            up[...] = jnp.zeros(up.shape, F32)

        @pl.when(h == n_height - 1)
        def _():
            down[...] = jnp.zeros(down.shape, F32)

    def halo_wait(first, last, up, down, k):
        above, below = halo_copies(first, last, up, down, k)

        @pl.when(h > 0)
        def _():
            above.wait_recv()

        @pl.when(h < n_height - 1)
        def _():
            below.wait_recv()

    def halo_sent(first, last, up, down, k):
        above, below = halo_copies(first, last, up, down, k)

        @pl.when(h < n_height - 1)
        def _():
            above.wait_send()

        @pl.when(h > 0)
        def _():
            below.wait_send()

    count = counts[0]
    filled = row_valid[0]
    for r in range(1, rows):
        filled = filled + row_valid[r]

    def flag(cond):
        return jnp.where(cond, 1.0, 0.0).astype(F32)

    def own(at):
        return flag((at >= 1) & (at <= filled))

    def ext(at):
        return flag(
            ((at >= 1) & (at <= filled))
            | ((at == 0) & (h > 0))
            | ((at == filled + 1) & (h < n_height - 1))
        )

    def mask(scale, lanes, start=0, size=block):
        return tiled(pix[start : start + size, :] * scale, lanes // 128)

    def block_at(at):
        return pl.ds(at * block if isinstance(at, int) else pl.multiple_of(at * block, block), block)

    def set_last(src, last):
        value = jnp.zeros(last.shape, F32)
        for r in range(rows):
            value = value + src[block_at(r + 1), :] * flag(filled == r + 1)
        last[...] = value

    def patch(ref, up, down):
        ref[block_at(0), :] = up[...]
        ref[block_at(rows + 1), :] = down[...]
        whole = flag(filled == rows)
        ref[block_at(rows), :] = ref[block_at(rows), :] * whole + down[...] * (1.0 - whole)

    iota = lax.broadcasted_iota(jnp.int32, (block, 128), 0)
    pix[...] = jnp.where(((iota >> 4) < count) & ((iota & 15) < cols), 1.0, 0.0)

    def pad_in(src, dst):
        def one(i, carry):
            r, s = i // slots, lax.rem(i, slots)
            live = flag((s < count) & (r < filled))
            dst[i, 0:cols, :] = (src[s, r].astype(F32) * live).astype(BF16)
            dst[i, cols:COLS, :] = jnp.zeros((COLS - cols, width), BF16)
            return carry

        lax.fori_loop(0, rows * slots, one, 0)

    def pad_out(src, dst):
        def one(i, carry):
            r, s = i // slots, lax.rem(i, slots)
            dst[s, r] = src[i, 0:cols, :]
            return carry

        lax.fori_loop(0, rows * slots, one, 0)

    kh, kq = lax.rem(h, 2), h // 2
    pair_one = (b, h + 1 - 2 * kh)
    pair_two = (b, h + 2 - 4 * kq)
    gi = lax.rem(b, GROUP)
    g0 = b - gi
    n_groups = n_batch // GROUP
    g_at = b // GROUP

    class Bucket:
        def __init__(self, at, full, half_, quart, in1, in2, in3, in4, shard, done):
            self.at, self.full, self.half, self.quart = at, full, half_, quart
            self.in1, self.in2, self.in3, self.in4 = in1, in2, in3, in4
            self.shard, self.done = shard, done
            self.size = full.shape[0]
            self.u2, self.u4, self.u32 = self.size // 2, self.size // 4, self.size // (4 * GROUP)
            self.kind = full.dtype
            self.tile = 8 if self.kind == F32 else 16
            self.quarter_at = pl.multiple_of(kh * self.u2 + kq * self.u4, self.tile)
            self.shard_at = pl.multiple_of(self.quarter_at + gi * self.u32, self.tile)

        def remote(self, stage, src, dst, device):
            k = self.at * 8 + stage
            return pltpu.make_async_remote_copy(
                src_ref=src, dst_ref=dst, send_sem=red_send.at[k], recv_sem=red_recv.at[k],
                device_id=device, device_id_type=MESH,
            )

        def halves(self):
            return self.remote(
                0, self.full.at[pl.ds(pl.multiple_of((1 - kh) * self.u2, self.tile), self.u2)], self.in1, pair_one
            )

        def quarters(self):
            return self.remote(
                1, self.half.at[pl.ds(pl.multiple_of((1 - kq) * self.u4, self.tile), self.u4)], self.in2, pair_two
            )

        def start_one(self):
            self.halves().start()

        def start_two(self):
            self.halves().wait_recv()
            step = self.u2 // 4

            def one(i, carry):
                at = pl.multiple_of(i * step, self.tile)
                mine = self.full[pl.ds(pl.multiple_of(kh * self.u2 + at, self.tile), step), :].astype(F32)
                self.half[pl.ds(at, step), :] = (mine + self.in1[pl.ds(at, step), :].astype(F32)).astype(self.kind)
                return carry

            lax.fori_loop(0, 4, one, 0)
            self.quarters().start()

        def pieces(self, t):
            return self.remote(
                2, self.quart.at[pl.ds(pl.multiple_of(t * self.u32, self.tile), self.u32)], self.in3.at[gi], (g0 + t, h)
            )

        def pieces_all(self):
            many = self.in3.at[pl.ds(0, GROUP - 1)]
            return self.remote(2, many, many, (b, h))

        def start_three(self):
            self.quarters().wait_recv()
            step = self.u4 // GROUP

            def one(i, carry):
                at = pl.multiple_of(i * step, self.tile)
                mine = self.half[pl.ds(pl.multiple_of(kq * self.u4 + at, self.tile), step), :].astype(F32)
                self.quart[pl.ds(at, step), :] = (mine + self.in2[pl.ds(at, step), :].astype(F32)).astype(self.kind)
                return carry

            lax.fori_loop(0, GROUP, one, 0)

            def send(j, carry):
                self.pieces(lax.rem(gi + j, GROUP)).start()
                return carry

            lax.fori_loop(1, GROUP, send, 0)
            self.in3[gi] = self.quart[pl.ds(pl.multiple_of(gi * self.u32, self.tile), self.u32), :]

        def others(self, t):
            return self.remote(3, self.shard, self.in4.at[g_at], (t * GROUP + gi, h))

        def others_all(self):
            many = self.in4.at[pl.ds(0, n_groups - 1)]
            return self.remote(3, many, many, (b, h))

        def shards(self, t):
            return self.remote(4, self.done.at[pl.ds(self.shard_at, self.u32)],
                               self.done.at[pl.ds(self.shard_at, self.u32)], (g0 + t, h))

        def shards_all(self):
            many = self.done.at[pl.ds(0, (GROUP - 1) * self.u32)]
            return self.remote(4, many, many, (b, h))

        def start_four(self):
            self.pieces_all().wait_recv()
            value = self.in3[0].astype(F32)
            for t in range(1, GROUP):
                value = value + self.in3[t].astype(F32)
            if n_groups > 1:
                self.shard[...] = value.astype(self.kind)

                def send_group(j, carry):
                    self.others(lax.rem(g_at + j, n_groups)).start()
                    return carry

                lax.fori_loop(1, n_groups, send_group, 0)
                self.in4[g_at] = self.shard[...]
                self.others_all().wait_recv()
                value = self.in4[0].astype(F32)
                for t in range(1, n_groups):
                    value = value + self.in4[t].astype(F32)
            self.done[pl.ds(self.shard_at, self.u32), :] = value.astype(self.kind)

            def send(j, carry):
                self.shards(lax.rem(gi + j, GROUP)).start()
                return carry

            lax.fori_loop(1, GROUP, send, 0)

        def quarter_back(self):
            part = self.done.at[pl.ds(self.quarter_at, self.u4)]
            return self.remote(5, part, part, pair_two)

        def half_back(self):
            part = self.done.at[pl.ds(pl.multiple_of(kh * self.u2, self.tile), self.u2)]
            return self.remote(6, part, part, pair_one)

        def start_five(self):
            self.shards_all().wait_recv()
            self.quarter_back().start()

        def start_six(self):
            self.quarter_back().wait_recv()
            self.half_back().start()

        def finish(self):
            self.half_back().wait_recv()

        def sent(self):
            self.halves().wait_send()
            self.quarters().wait_send()
            self.pieces_all().wait_send()
            if n_groups > 1:
                self.others_all().wait_send()
            self.shards_all().wait_send()
            self.quarter_back().wait_send()
            self.half_back().wait_send()

    bucket_e = Bucket(0, full_e, half_e, quart_e, in1_e, in2_e, in3_e, in4_e, shard_e, done_e)
    bucket_s = Bucket(1, full_s, half_s, quart_s, in1_s, in2_s, in3_s, in4_s, shard_s, done_s)
    bucket_r = Bucket(2, full_r, half_r, quart_r, in1_r, in2_r, in3_r, in4_r, shard_r, done_r)
    bucket_q = Bucket(3, full_q, half_q, quart_q, in1_q, in2_q, in3_q, in4_q, shard_q, done_q)

    loads[0].wait()
    pad_in(img4, x)
    loads[1].wait()
    sum_one = jnp.zeros((1, narrow), F32)
    square_one = jnp.zeros((1, narrow), F32)
    for q in range(rows // 2):
        value = dot(x[pl.ds(q * 2 * slots, 2 * slots)].reshape(2 * block, width), w_reduce[...])
        c1[pl.ds((1 + 2 * q) * block, 2 * block), :] = value
        sum_one = sum_one + colsum(value)
        square_one = square_one + colsum(value * value)
    m1[...] = jnp.zeros(m1.shape, F32)
    put_rows(m1, 0, sum_one)
    put_rows(m1, narrow // 128, square_one)
    m1[4:5, :] = jnp.zeros((1, 128), F32) + count.astype(F32)
    pl.semaphore_wait(barrier, total - 1)
    send_all(m1, s1, 0)
    set_last(c1, last1)
    first1 = c1.at[block_at(1)]
    halo_start(first1, last1, up1, down1, 0)
    loads[3].wait()
    pad_in(cot4, g)

    sum_all(s1, 0)
    slot_total = tot[4:5, :] / n_height
    pix_total = slot_total * area
    m_one = tiled(pix_total, narrow // 128)
    mean = get_rows(tot, 0, narrow // 128) / m_one
    inv_one = lax.rsqrt(get_rows(tot, 2, narrow // 128) / m_one - mean * mean + EPSILON)
    shift_one = mean * inv_one
    scale = inv_one * gain_one[...]
    offset = bias_one[...] - mean * scale
    scale_one, offset_one = scale, offset
    halo_wait(first1, last1, up1, down1, 0)
    patch(c1, up1, down1)

    def hide(at, carry):
        value = c1[block_at(at), :] * scale_one + offset_one
        value = swish(value) * mask(ext(at), narrow)
        hs[0, block_at(at), :] = pltpu.roll(value, 1, axis=0).astype(BF16)
        hs[1, block_at(at), :] = value.astype(BF16)
        hs[2, block_at(at), :] = pltpu.roll(value, block - 1, axis=0).astype(BF16)
        return carry

    lax.fori_loop(0, rows + 2, hide, 0)

    loads[2].wait()
    for q in range(rows // 2):
        for gr in range(2):
            lhs = jnp.concatenate(
                [
                    hs[bb, (a + 2 * q) * block : (a + 2 * q + 2) * block, gr * cg : (gr + 1) * cg]
                    for a in range(3)
                    for bb in range(3)
                ],
                axis=1,
            )
            c2[(1 + 2 * q) * block : (3 + 2 * q) * block, gr * half : (gr + 1) * half] = dot(
                lhs, w_split[:, gr * half : (gr + 1) * half]
            )
    m2[...] = jnp.zeros(m2.shape, F32)
    for j in range(2):
        lanes = pl.ds(j * half, half)

        def moments(r, carry):
            value = c2[block_at(r), lanes] * mask(own(r), half)
            return carry[0] + colsum(value), carry[1] + colsum(value * value)

        zero = jnp.zeros((1, half), F32)
        sums = lax.fori_loop(1, rows + 1, moments, (zero, zero))
        put_rows(m2, j * (half // 128), sums[0])
        put_rows(m2, split // 128 + j * (half // 128), sums[1])
    send_all(m2, s2, 1)
    set_last(c2, last2)
    first2 = c2.at[block_at(1)]
    halo_start(first2, last2, up2, down2, 1)
    x_t[...] = x[...].reshape(pixels, width).T

    sum_all(s2, 1)
    m_two = tiled(pix_total, split // 128)
    mean = get_rows(tot, 0, split // 128) / m_two
    inv_two = lax.rsqrt(get_rows(tot, split // 128, split // 128) / m_two - mean * mean + EPSILON)
    shift_two = mean * inv_two
    scale_two = inv_two * gain_two[...]
    offset_two = bias_two[...] - mean * scale_two
    pool = jnp.zeros((slots, half), F32)
    for j in range(2):
        lanes = pl.ds(j * half, half)
        sc, of = scale_two[:, j * half : (j + 1) * half], offset_two[:, j * half : (j + 1) * half]

        def activate(r, acc):
            value = swish(c2[block_at(r), lanes] * sc + of) * mask(own(r), half)
            act[block_at(r - 1), lanes] = value
            return acc + value

        acc = lax.fori_loop(1, rows + 1, activate, jnp.zeros((block, half), F32))
        pool = pool + per_slot(acc, slots)
    pool = pool / area
    pooled[...] = pool
    loads[4].wait()
    m34[...] = dot(pool, w_squeeze[...], precision=HIGHEST)
    send_all(m34, s34, 2)
    for bb in range(3):
        hs_t[bb] = hs[bb].T

    loads[5].wait()
    all_copy(s34, 2).wait_recv()

    def gather(i, carry):
        value = jnp.sum(s34[pl.ds(i * n_height, n_height)], axis=0)
        sq_all[i] = value
        return carry[0] + colsum(value), carry[1] + colsum(value * value)

    zero = jnp.zeros((1, inner), F32)
    sum_mid, square_mid = lax.fori_loop(0, n_batch, gather, (zero, zero))
    mean = sum_mid / slot_total
    inv_mid = lax.rsqrt(square_mid / slot_total - mean * mean + EPSILON)
    norm_mid = (sq_all[b] - mean) * inv_mid
    pre_mid = norm_mid * gain_mid[...] + bias_mid[...]
    middle = swish(pre_mid)
    logits = dot(middle, w_excite[...], precision=HIGHEST) + bias_excite[...]
    top = jnp.maximum(logits[:, :half], logits[:, half:])
    expo_one = jnp.exp(logits[:, :half] - top)
    expo_two = jnp.exp(logits[:, half:] - top)
    att_one = expo_one / (expo_one + expo_two)
    att_two = expo_two / (expo_one + expo_two)
    att[:, 0:half] = att_one
    att[:, half:split] = att_two
    for s in range(slots):
        attx[s * COLS : (s + 1) * COLS, :] = jnp.broadcast_to(att[s : s + 1, :], (COLS, split))

    def mix(r, carry):
        at = block_at(r)
        mixed[at, :] = (
            attx[:, 0:half] * act[at, 0:half] + attx[:, half:split] * act[at, half:split]
        ).astype(BF16)
        return carry

    lax.fori_loop(0, rows, mix, 0)
    loads[6].wait()
    for j in range(width // 256):
        lanes = pl.ds(j * 256, 256)
        sums = jnp.zeros((1, 256), F32)
        squares = jnp.zeros((1, 256), F32)
        for q in range(rows // 2):
            at = pl.ds(q * 2 * block, 2 * block)
            value = dot(mixed[at, :], w_expand[:, lanes])
            c3[at, lanes] = value
            sums = sums + colsum(value)
            squares = squares + colsum(value * value)
        put_rows(m5, j * 2, sums)
        put_rows(m5, width // 128 + j * 2, squares)
    send_all(m5, s5, 3)
    mixed_t[...] = mixed[...].T
    halo_wait(first2, last2, up2, down2, 1)
    halo_sent(first2, last2, up2, down2, 1)
    patch(c2, up2, down2)
    for j in range(2):
        lanes = pl.ds(j * half, half)
        sc, of = scale_two[:, j * half : (j + 1) * half], offset_two[:, j * half : (j + 1) * half]

        def slopes(at, carry):
            value = swish_slope(c2[block_at(at), lanes] * sc + of)
            slope2[block_at(at), lanes] = value * mask(ext(at), half)
            return carry

        lax.fori_loop(0, rows + 2, slopes, 0)

    def slopes_one(r, carry):
        value = swish_slope(c1[block_at(r + 1), :] * scale_one + offset_one)
        slope1[block_at(r), :] = value * mask(own(r + 1), narrow)
        return carry

    lax.fori_loop(0, rows, slopes_one, 0)

    sum_all(s5, 3)
    wide = width // 128
    m_three = tiled(pix_total, wide)
    mean = get_rows(tot, 0, wide) / m_three
    inv_three = lax.rsqrt(get_rows(tot, wide, wide) / m_three - mean * mean + EPSILON)
    shift_three = mean * inv_three
    scale_three = inv_three * gain_three[...]
    offset_three = bias_three[...] - mean * scale_three
    part = block // 2
    for j in range(width // 256):
        lanes = pl.ds(j * 256, 256)
        cut = slice(j * 256, (j + 1) * 256)
        sc, of = scale_three[:, cut], offset_three[:, cut]
        iv, sh = inv_three[:, cut], shift_three[:, cut]

        def finish_row(i, carry):
            r, k = i // 2, lax.rem(i, 2)
            at = pl.ds(pl.multiple_of(i * part, part), part)
            images_at = pl.ds(i * (slots // 2), slots // 2)
            conv = c3[at, lanes]
            pre = conv * sc + of + x[images_at, :, lanes].reshape(part, 256).astype(F32)
            sigma = sigmoid(pre)
            value = pre * sigma
            live = tiled(pix[pl.ds(pl.multiple_of(k * part, part), part), :] * own(r + 1), 2)
            xo[images_at, :, lanes] = (value * live).astype(BF16).reshape(slots // 2, COLS, 256)
            slope = sigma + value * (1.0 - sigma)
            grad = g[images_at, :, lanes].reshape(part, 256).astype(F32) * slope
            d3[at, lanes] = grad
            return carry[0] + colsum(grad), carry[1] + colsum(grad * (conv * iv - sh))

        zero = jnp.zeros((1, 256), F32)
        sums = lax.fori_loop(0, 2 * rows, finish_row, (zero, zero))
        put_rows(m6, j * 2, sums[0])
        put_rows(m6, wide + j * 2, sums[1])
    send_all(m6, s6, 4)
    pad_out(xo, out4)
    out_copy = pltpu.make_async_copy(out4, output, local_sem.at[7])
    out_copy.start()

    sum_all(s6, 4)
    gb_three = get_rows(tot, 0, wide)
    gg_three = get_rows(tot, wide, wide)
    vectors[0:1, :] = gb_three
    vectors[1:2, :] = gg_three
    gg = gg_three / m_three
    k_one = scale_three
    k_three = k_one * inv_three * gg
    k_two = k_one * (gb_three / m_three - shift_three * gg)
    for j in range(width // 256):
        lanes = pl.ds(j * 256, 256)
        cut = slice(j * 256, (j + 1) * 256)
        ka, kb, kc = k_one[:, cut], k_two[:, cut], k_three[:, cut]

        def back_three(i, carry):
            at = pl.ds(pl.multiple_of(i * part, part), part)
            gc3[at, lanes] = (d3[at, lanes] * ka - kb - c3[at, lanes] * kc).astype(BF16)
            return carry

        lax.fori_loop(0, 2 * rows, back_three, 0)
    for q in range(rows // 2):
        gm[pl.ds((1 + 2 * q) * block, 2 * block), :] = dot(
            gc3[pl.ds(2 * q * block, 2 * block), :], w_expand[...], NT
        )
    set_last(gm, last3)
    first3 = gm.at[block_at(1)]
    halo_start(first3, last3, up3, down3, 2)
    grad_att = []
    for j in range(2):
        lanes = pl.ds(j * half, half)

        def attend(r, acc):
            return acc + gm[block_at(r + 1), :] * act[block_at(r), lanes]

        acc = lax.fori_loop(0, rows, attend, jnp.zeros((block, half), F32))
        grad_att.append(per_slot(acc, slots))
    blend = att_one * grad_att[0] + att_two * grad_att[1]
    grad_logits = jnp.concatenate(
        [att_one * (grad_att[0] - blend), att_two * (grad_att[1] - blend)], axis=1
    )
    em_part = dot(grad_logits, w_excite[...], NT, HIGHEST) * swish_slope(pre_mid)
    em_src[...] = em_part
    m78[0:1, :] = colsum(em_part)
    m78[1:2, :] = colsum(em_part * norm_mid)

    def em_copy(j):
        return pltpu.make_async_remote_copy(
            src_ref=em_src, dst_ref=em_all.at[h], send_sem=em_sems.at[0], recv_sem=em_sems.at[1],
            device_id=(b, lax.rem(h + j, n_height)), device_id_type=MESH,
        )

    for j in range(1, n_height):
        em_copy(j).start()
    em_all[h] = em_src[...]
    send_all(m78, s78, 5)
    for j in range(width // 256):
        full_e[j * narrow : (j + 1) * narrow, :] = dot(
            mixed_t[...], gc3[:, j * 256 : (j + 1) * 256]
        ).astype(BF16)
    bucket_e.start_one()
    grad_excite = dot(middle, grad_logits, TN, HIGHEST)
    base = 9 * cg * 2
    full_s[base : base + inner, :] = grad_excite[:, :half].astype(BF16)
    full_s[base + inner : base + 2 * inner, :] = grad_excite[:, half:].astype(BF16)
    bias_part = colsum(grad_logits)
    put_rows(m10, 2 * (narrow // 128), bias_part)
    bucket_e.start_two()

    sum_all(s78, 5)
    gb_mid, gg_mid = tot[0:1, :], tot[1:2, :]
    vectors[4:5, 0:128] = gb_mid
    vectors[4:5, 128:256] = gg_mid
    many = em_all.at[pl.ds(0, n_height - 1)]
    em_wait = pltpu.make_async_remote_copy(
        src_ref=many, dst_ref=many, send_sem=em_sems.at[0], recv_sem=em_sems.at[1],
        device_id=(b, h), device_id_type=MESH,
    )
    em_wait.wait_recv()
    em = jnp.sum(em_all[...], axis=0)
    slot_live = jnp.where(lax.broadcasted_iota(jnp.int32, (slots, inner), 0) < count, 1.0, 0.0)
    grad_sq = (
        slot_live * inv_mid * gain_mid[...]
        * (em - gb_mid / slot_total - norm_mid * gg_mid / slot_total)
    )
    grad_pooled = dot(grad_sq, w_squeeze[...], NT, HIGHEST) / area
    pooled_grad = dot(pooled[...], grad_sq, TN, HIGHEST)
    att[:, 0:half] = grad_pooled
    for s in range(slots):
        gpx[s * COLS : (s + 1) * COLS, :] = jnp.broadcast_to(att[s : s + 1, 0:half], (COLS, half))
    halo_wait(first3, last3, up3, down3, 2)
    halo_sent(first3, last3, up3, down3, 2)
    patch(gm, up3, down3)
    for j in range(2):
        lanes = pl.ds(j * half, half)
        iv, sh = inv_two[:, j * half : (j + 1) * half], shift_two[:, j * half : (j + 1) * half]

        def back_act(at, carry):
            value = (attx[:, lanes] * gm[block_at(at), :] + gpx[...]) * slope2[block_at(at), lanes]
            d2[block_at(at), lanes] = value
            value = value * own(at)
            norm = c2[block_at(at), lanes] * iv - sh
            return carry[0] + colsum(value), carry[1] + colsum(value * norm)

        zero = jnp.zeros((1, half), F32)
        sums = lax.fori_loop(0, rows + 2, back_act, (zero, zero))
        put_rows(m9, j * (half // 128), sums[0])
        put_rows(m9, split // 128 + j * (half // 128), sums[1])
    send_all(m9, s9, 6)
    full_q[...] = pooled_grad
    bucket_q.start_one()
    bucket_e.start_three()

    sum_all(s9, 6)
    gb_two = get_rows(tot, 0, split // 128)
    gg_two = get_rows(tot, split // 128, split // 128)
    vectors[2:3, 0:split] = gb_two
    vectors[2:3, split : 2 * split] = gg_two
    gg = gg_two / m_two
    k_one = scale_two
    k_three = k_one * inv_two * gg
    k_two = k_one * (gb_two / m_two - shift_two * gg)
    for j in range(2):
        lanes = pl.ds(j * half, half)
        cut = slice(j * half, (j + 1) * half)
        ka, kb, kc = k_one[:, cut], k_two[:, cut], k_three[:, cut]

        def back_two(at, carry):
            value = d2[block_at(at), lanes] * ka - kb - c2[block_at(at), lanes] * kc
            gc2[block_at(at), lanes] = (value * mask(ext(at), half)).astype(BF16)
            return carry

        lax.fori_loop(0, rows + 2, back_two, 0)
    gc2_own[...] = (gc2[block_at(rows), :].astype(F32) * own(rows)).astype(BF16)
    for gr in range(2):
        outs = []
        for bb in range(3):
            lhs = jnp.concatenate(
                [gc2[(2 - a) * block : (2 - a) * block + pixels, gr * half : (gr + 1) * half] for a in range(3)],
                axis=1,
            )
            rhs = jnp.concatenate(
                [
                    w_split[(a * 3 + bb) * cg : (a * 3 + bb + 1) * cg, gr * half : (gr + 1) * half]
                    for a in range(3)
                ],
                axis=1,
            )
            outs.append(dot(lhs, rhs, NT))
        gh[:, gr * cg : (gr + 1) * cg] = (
            outs[1] + pltpu.roll(outs[2], 1, axis=0) + pltpu.roll(outs[0], pixels - 1, axis=0)
        )

    def back_hidden(r, carry):
        value = gh[block_at(r), :] * slope1[block_at(r), :]
        gh[block_at(r), :] = value
        norm = c1[block_at(r + 1), :] * inv_one - shift_one
        return carry[0] + colsum(value), carry[1] + colsum(value * norm)

    zero = jnp.zeros((1, narrow), F32)
    sums = lax.fori_loop(0, rows, back_hidden, (zero, zero))
    put_rows(m10, 0, sums[0])
    put_rows(m10, narrow // 128, sums[1])
    send_all(m10, s10, 7)
    for gr in range(2):
        for bb in range(3):
            lhs = jnp.concatenate(
                [hs_t[bb, gr * cg : (gr + 1) * cg, a * block : a * block + pixels] for a in range(3)], axis=0
            )
            lanes = slice(gr * half, (gr + 1) * half)
            rhs = jnp.concatenate([gc2[block:pixels, lanes], gc2_own[:, lanes]], axis=0)
            value = dot(lhs, rhs)
            for a in range(3):
                at = gr * 9 * cg + (a * 3 + bb) * cg
                full_s[at : at + cg, :] = value[a * cg : (a + 1) * cg].astype(BF16)
    base = base + 2 * inner
    if base < full_s.shape[0]:
        full_s[base:, :] = jnp.zeros((full_s.shape[0] - base, 256), BF16)
    bucket_s.start_one()
    bucket_q.start_two()
    bucket_e.start_four()

    sum_all(s10, 7)
    gb_one = get_rows(tot, 0, narrow // 128)
    gg_one = get_rows(tot, narrow // 128, narrow // 128)
    vectors[3:4, 0:narrow] = gb_one
    vectors[3:4, narrow : 2 * narrow] = gg_one
    vectors[3:4, 2 * narrow : 2 * narrow + split] = get_rows(tot, 2 * (narrow // 128), split // 128)
    gg = gg_one / m_one
    k_one = scale_one
    k_three = k_one * inv_one * gg
    k_two = k_one * (gb_one / m_one - shift_one * gg)

    def back_one(r, carry):
        value = gh[block_at(r), :] * k_one - k_two - c1[block_at(r + 1), :] * k_three
        gc1[block_at(r), :] = (value * mask(own(r + 1), narrow)).astype(BF16)
        return carry

    lax.fori_loop(0, rows, back_one, 0)
    for q in range(2):
        at = q * (width // 2)
        full_r[at : at + width // 2, :] = dot(x_t[at : at + width // 2, :], gc1[...]).astype(BF16)
    bucket_r.start_one()
    bucket_s.start_two()
    bucket_q.start_three()
    bucket_r.start_two()
    bucket_e.start_five()
    out_copy.wait()

    def back_image(r, carry):
        value = d3[block_at(r), :] + dot(gc1[block_at(r), :], w_reduce[...], NT)
        xo[pl.ds(r * slots, slots)] = value.astype(BF16).reshape(slots, COLS, width)
        return carry

    lax.fori_loop(0, rows, back_image, 0)
    bucket_q.start_four()
    bucket_s.start_three()
    bucket_r.start_three()
    bucket_e.start_six()
    pad_out(xo, out4)
    image_copy = pltpu.make_async_copy(out4, grad_images, local_sem.at[7])
    image_copy.start()
    bucket_q.start_five()
    bucket_s.start_four()
    bucket_r.start_four()
    bucket_e.finish()
    copy_e = pltpu.make_async_copy(done_e, big_e, local_sem.at[0])
    copy_e.start()
    bucket_q.start_six()
    bucket_s.start_five()
    bucket_r.start_five()
    bucket_s.start_six()
    bucket_r.start_six()
    bucket_s.finish()
    copy_s = pltpu.make_async_copy(done_s, big_s, local_sem.at[1])
    copy_s.start()
    bucket_q.finish()
    copy_q = pltpu.make_async_copy(done_q, big_q, local_sem.at[3])
    copy_q.start()
    bucket_r.finish()
    copy_r = pltpu.make_async_copy(done_r, big_r, local_sem.at[2])
    copy_r.start()

    for k, dst in enumerate((s1, s2, s34, s5, s6, s78, s9, s10)):
        all_copy(dst, k).wait_send()
    halo_sent(first1, last1, up1, down1, 0)
    em_wait.wait_send()
    bucket_e.sent()
    bucket_s.sent()
    bucket_r.sent()
    bucket_q.sent()
    image_copy.wait()
    copy_e.wait()
    copy_s.wait()
    copy_r.wait()
    copy_q.wait()


def unpack_kernel(
    out_a, gimg_a, big_e, big_s, big_r, big_q, vectors,
    output, grad_images, grad_reduce, grad_gain_one, grad_bias_one, grad_split, grad_gain_two, grad_bias_two,
    grad_squeeze, grad_gain_mid, grad_bias_mid, grad_excite, grad_bias_excite, grad_expand, grad_gain_three,
    grad_bias_three, sems,
):
    one = pltpu.make_async_copy(out_a, output, sems.at[0])
    two = pltpu.make_async_copy(gimg_a, grad_images, sems.at[1])
    one.start()
    two.start()
    narrow = grad_expand.shape[0]
    taps, split = grad_split.shape
    half = split // 2
    inner = grad_excite.shape[0]
    for j in range(grad_expand.shape[1] // 256):
        grad_expand[:, j * 256 : (j + 1) * 256] = big_e[j * narrow : (j + 1) * narrow, :].astype(F32)
    for gr in range(2):
        grad_split[:, gr * half : (gr + 1) * half] = big_s[gr * taps : (gr + 1) * taps, :].astype(F32)
    base = 2 * taps
    for gr in range(2):
        grad_excite[:, gr * half : (gr + 1) * half] = big_s[
            base + gr * inner : base + (gr + 1) * inner, :
        ].astype(F32)
    grad_squeeze[...] = big_q[...]
    grad_reduce[...] = big_r[...].astype(F32)
    grad_bias_three[...] = vectors[0:1, :]
    grad_gain_three[...] = vectors[1:2, :]
    grad_bias_two[...] = vectors[2:3, 0:split]
    grad_gain_two[...] = vectors[2:3, split : 2 * split]
    grad_bias_one[...] = vectors[3:4, 0:narrow]
    grad_gain_one[...] = vectors[3:4, narrow : 2 * narrow]
    grad_bias_excite[...] = vectors[3:4, 2 * narrow : 2 * narrow + split]
    grad_bias_mid[...] = vectors[4:5, 0:inner]
    grad_gain_mid[...] = vectors[4:5, inner : 2 * inner]
    one.wait()
    two.wait()


def shards(
    n_batch, n_height,
    images, counts, row_valid, w_reduce, gain_one, bias_one, w_split, gain_two, bias_two, w_squeeze,
    gain_mid, bias_mid, w_excite, bias_excite, w_expand, gain_three, bias_three, cotangent,
):
    slots, rows, cols, width = images.shape
    narrow = w_reduce.shape[1]
    split = w_split.shape[3]
    taps = 9 * w_split.shape[2]
    inner = w_squeeze.shape[1]
    half = split // 2
    total = n_batch * n_height
    block = slots * COLS
    pixels = rows * block
    padded = pixels + 2 * block
    n_groups = n_batch // GROUP

    def row(v):
        return v.reshape(1, -1)

    unit = 4 * GROUP * 16
    size_e = width // 256 * narrow
    size_s = -(-(2 * taps + 2 * inner) // unit) * unit
    size_r = width

    def bucket(size, lanes=256, kind=BF16):
        cut = size // (4 * GROUP)
        shapes = [
            (size, lanes), (size // 2, lanes), (size // 4, lanes), (size // 2, lanes), (size // 4, lanes),
            (GROUP, cut, lanes), (n_groups, cut, lanes), (cut, lanes), (size, lanes),
        ]
        return [pltpu.VMEM(dims, kind) for dims in shapes]

    heights = [8, 8, 8, 16, 16, 2, 8, 8]
    vm = pltpu.VMEM
    scratch = (
        [vm(images.shape, BF16), vm(images.shape, BF16), vm(images.shape, BF16)]
        + [vm((width, narrow), BF16), vm((taps, split), BF16), vm((narrow, inner), F32), vm((inner, split), F32),
           vm((narrow, width), BF16)]
        + [vm((rows * slots, COLS, width), BF16), vm((rows * slots, COLS, width), BF16), vm((block, 128), F32)]
        + [vm((padded, narrow), F32), vm((3, padded, narrow), BF16), vm((padded, split), F32), vm((pixels, split), F32),
           vm((padded, split), F32), vm((pixels, half), BF16), vm((pixels, width), F32), vm((pixels, width), F32),
           vm((rows * slots, COLS, width), BF16), vm((pixels, width), BF16), vm((padded, half), F32),
           vm((padded, split), F32), vm((padded, split), BF16), vm((pixels, narrow), F32), vm((pixels, narrow), F32),
           vm((pixels, narrow), BF16), vm((block, split), BF16)]
        + [vm((width, pixels), BF16), vm((half, pixels), BF16), vm((3, narrow, padded), BF16), vm((slots, split), F32),
           vm((block, split), F32), vm((block, half), F32), vm((slots, half), F32), vm((n_batch, slots, inner), F32),
           vm((16, 128), F32)]
        + [vm((k, 128), F32) for k in heights] + [vm((slots, inner), F32)]
        + [vm((total, k, 128), F32) for k in heights] + [vm((n_height, slots, inner), F32)]
        + [vm((block, narrow), F32)] * 3 + [vm((block, split), F32)] * 3 + [vm((block, half), F32)] * 3
        + bucket(size_e) + bucket(size_s) + bucket(size_r) + bucket(narrow, inner, F32)
        + [pltpu.SemaphoreType.DMA((8,)), pltpu.SemaphoreType.DMA((8,)), pltpu.SemaphoreType.DMA((8,)),
           pltpu.SemaphoreType.DMA((6,)), pltpu.SemaphoreType.DMA((6,)), pltpu.SemaphoreType.DMA((2,)),
           pltpu.SemaphoreType.DMA((32,)), pltpu.SemaphoreType.DMA((32,))]
    )
    smem = pl.BlockSpec(memory_space=pltpu.SMEM)
    vmem = pl.BlockSpec(memory_space=pltpu.VMEM)
    hbm = pl.BlockSpec(memory_space=pl.ANY)
    shape = jax.ShapeDtypeStruct
    out_a, gimg_a, big_e, big_s, big_r, big_q, vectors = pl.pallas_call(
        functools.partial(main_kernel, n_batch, n_height, images.shape),
        out_shape=(
            shape(images.shape, BF16), shape(images.shape, BF16), shape((size_e, 256), BF16),
            shape((size_s, 256), BF16), shape((size_r, 256), BF16), shape((narrow, inner), F32),
            shape((8, width), F32),
        ),
        in_specs=[smem, smem] + [vmem] * 9 + [hbm] * 7,
        out_specs=[hbm] * 6 + [vmem],
        scratch_shapes=scratch,
        compiler_params=pltpu.CompilerParams(
            collective_id=0, has_side_effects=True, vmem_limit_bytes=58 * 1024 * 1024
        ),
    )(
        counts, row_valid, row(gain_one), row(bias_one), row(gain_two), row(bias_two), row(gain_mid), row(bias_mid),
        row(bias_excite), row(gain_three), row(bias_three),
        images, cotangent, w_reduce, w_split.reshape(taps, split), w_squeeze, w_excite, w_expand,
    )
    outs = pl.pallas_call(
        unpack_kernel,
        out_shape=(
            shape(images.shape, BF16), shape(images.shape, BF16), shape((width, narrow), F32),
            shape((1, narrow), F32), shape((1, narrow), F32), shape((taps, split), F32),
            shape((1, split), F32), shape((1, split), F32), shape((narrow, inner), F32),
            shape((1, inner), F32), shape((1, inner), F32), shape((inner, split), F32),
            shape((1, split), F32), shape((narrow, width), F32), shape((1, width), F32), shape((1, width), F32),
        ),
        in_specs=[hbm, hbm] + [vmem] * 5,
        out_specs=[hbm, hbm] + [vmem] * 14,
        scratch_shapes=[pltpu.SemaphoreType.DMA((2,))],
        compiler_params=pltpu.CompilerParams(vmem_limit_bytes=40 * 1024 * 1024),
    )(out_a, gimg_a, big_e, big_s, big_r, big_q, vectors)
    result = []
    for value, like in zip(outs, (
        None, None, None, gain_one, bias_one, w_split, gain_two, bias_two, None, gain_mid, bias_mid, None, bias_excite,
        None, gain_three, bias_three,
    )):
        result.append(value if like is None else value.reshape(like.shape))
    return tuple(result)


def solution(mesh):
    axes = mesh.shape
    split_in = P("batch", "height", None, None)
    return jax.shard_map(
        functools.partial(shards, axes["batch"], axes["height"]),
        mesh=mesh,
        in_specs=(split_in, P("batch"), P("height")) + (P(),) * 14 + (split_in,),
        out_specs=(split_in, split_in) + (P(),) * 14,
        check_vma=False,
    )
```

time: 637 us -> 128 us (0.20)
  blocking collectives: 294 us -> 0 us
  waiting for transfers between devices: 141 us -> 0 us
  Pallas kernels: 0 us -> 109 us
  local copies, waits for them, and re-layouts: 80.5 us -> 14.5 us
  matrix products: 47 us -> 0 us
  other arithmetic: 36.7 us -> 0 us
  between operations: 19.5 us -> 1.41 us
  starting transfers between devices: 14.7 us -> 0 us
    psum x10 -> x0, blocking collectives: 294 us -> none  [the longest x1 43.3 us: shards(): lax.psum((jnp.sum(grad_resid, axis=0), jnp.sum(grad_resid * norm_three, a...]
    psum x1 -> x0, waiting for transfers between devices: 141 us -> none  [shards(): lax.psum((grad_reduce_local, late_bucket), ('batch', 'height'))]
    pallas_call x0 -> x2, Pallas kernels: none -> 109 us  [the longest x1 107 us: shards(): pl.pallas_call(functools.partial(main_kernel, n_batch, n_height, images.s...]
    dot_general x39 -> x0, matrix products: 47 us -> none  [the longest x9 20.1 us: shards(): jnp.einsum('nhwgd,cgd->nhwgc', grad_conv_two, kernel_taps[row_off, col_of...]
    scatter-add x9 -> x0, local copies, waits for them, and re-layouts: 26.5 us -> none  [shards(): grad_column = grad_column.at[:, row_off:row_off + row_count, col_off:col_...]
    reduce_sum x10 -> x0, other arithmetic: 15 us -> none  [the longest x1 5.23 us: shards(): jnp.sum(grad_resid, axis=0)]
    ppermute x4 -> x0, starting transfers between devices: 14.6 us -> none  [the longest x2 9.34 us: padded(): lax.ppermute(tail, axis, [(i, (i + 1) % count) for i in range(ends)])]
    slice x13 -> x0, local copies, waits for them, and re-layouts: 13.7 us -> none  [the longest x2 4.64 us: shards(): grad_expand = late_sum[size_split:].reshape(narrow, in_width)]
  transfers between devices with their start and end apart: 5 -> 0, of which waited for: 1 -> 0; matrix products, arithmetic and copies ran while one was open for 6% -> 0% of each run, Pallas kernels for 0% -> 0%
where the time goes in v1:
time: 128 us; the launch traced here: 125 us
  Pallas kernels  109 us (85%)
  local copies, waits for them, and re-layouts  14.5 us (11%)
  between operations  1.41 us (1%)
    pallas_call x1, Pallas kernels, shards(): pl.pallas_call(functools.partial(main_kernel, n_batch, n_height, images.s...  107 us
    unnamed x20, local copies, waits for them, and re-layouts  14.5 us
    pallas_call x1, Pallas kernels, shards(): pl.pallas_call(unpack_kernel, out_shape=(shape(images.shape, BF16), shape...  2.73 us

profile of v1, /device:TPU:1, one launch (start us, length us, event | category | flops | bytes accessed | tf_op | source)
XLA Modules:
  0.0 125.4 jit_solution(15972152757726983714)
XLA Ops:
  0.6 0.0 copy-start.7
  1.4 2.5 %copy.34.refs_11_ = bf16[8,4,14,1024]{3,2,1,0:T(8,128)(2,1)} copy(bf16[8,4,14,1024]{3,1,2,0:T(4,128)(2,1)} %param.18) | data formatting | bytes 1835008 | tf_op args[0]
  3.9 0.0 copy-done.7
  3.9 1.3 %copy.35.refs_12_ = bf16[8,4,14,1024]{3,2,1,0:T(8,128)(2,1)} copy(bf16[8,4,14,1024]{3,1,2,0:T(4,128)(2,1)S(1)} %copy-done.7) | data formatting | bytes 1835008 | tf_op args[17]
  5.1 106.8 %shard_map.297 = (bf16[8,4,14,1024]{3,2,1,0:T(8,128)(2,1)}, bf16[8,4,14,1024]{3,2,1,0:T(8,128)(2,1)}, bf16[1024,256]{1,0:T(8,128)(2,1)}, bf16[2560,256]{1,0:T(8,...) custom-call(s32[1]{0:T(128)S(6)} %copy.38.refs_0_, s32[4]{0:T(128)} %refs_1_.1, ...), custom_call_target="tpu_custom_call" | custom-call | tf_op jit(solution)/shard_map/pallas_call | solution.py:978
  111.9 0.0 copy-start
  111.9 1.3 %copy-done = bf16[2560,256]{1,0:T(8,128)(2,1)S(1)} copy-done((bf16[2560,256]{1,0:T(8,128)(2,1)S(1)}, bf16[2560,256]{1,0:T(8,128)(2,1)}, u32[]{:S(2)}) %copy-start) | copy-done | bytes 1310744
  113.2 0.0 copy-start.1
  113.2 1.2 copy-done.1
  114.5 0.0 copy-start.2
  114.5 1.2 copy-done.2
  115.7 0.0 copy-start.3
  115.7 1.0 copy-done.3
  116.7 0.0 copy-start.4
  116.7 1.0 copy-done.4
  117.8 0.0 copy-start.5
  117.8 0.9 copy-done.5
  118.7 0.0 copy-start.6
  118.7 0.8 copy-done.6
  119.4 2.7 %shard_map.298 = (bf16[8,4,14,1024]{3,2,1,0:T(8,128)(2,1)S(1)}, bf16[8,4,14,1024]{3,2,1,0:T(8,128)(2,1)S(1)}, f32[1024,256]{1,0:T(8,128)}, f32[1,256]{1,0:T(1,12...) custom-call(bf16[8,4,14,1024]{3,2,1,0:T(8,128)(2,1)S(1)} %copy-done., ...), custom_call_target="tpu_custom_call" | custom-call | tf_op jit(solution)/shard_map/pallas_call | solution.py:996
  122.2 1.6 %copy.36 = bf16[8,4,14,1024]{3,1,2,0:T(4,128)(2,1)} copy(bf16[8,4,14,1024]{3,2,1,0:T(8,128)(2,1)S(1)} %get-tuple-element.62) | data formatting | bytes 1835008
  123.8 1.6 %copy.37 = bf16[8,4,14,1024]{3,1,2,0:T(4,128)(2,1)} copy(bf16[8,4,14,1024]{3,2,1,0:T(8,128)(2,1)S(1)} %get-tuple-element.63) | data formatting | bytes 1835008
Async XLA Ops:
  0.6 3.2 %copy-start.7 = (bf16[8,4,14,1024]{3,1,2,0:T(4,128)(2,1)S(1)}, bf16[8,4,14,1024]{3,1,2,0:T(4,128)(2,1)}, u32[]{:S(2)}) copy-start(bf16[8,4,14,1024]{3,1,2,0:T(4,128)(2,1)} %param.35) | copy-start | bytes 2752516
  111.9 1.3 %copy-start = (bf16[2560,256]{1,0:T(8,128)(2,1)S(1)}, bf16[2560,256]{1,0:T(8,128)(2,1)}, u32[]{:S(2)}) copy-start(bf16[2560,256]{1,0:T(8,128)(2,1)} %get-tuple-element.42.big_s) | copy-start | bytes 3932164
  113.2 1.2 copy-start.1
  114.5 1.2 copy-start.2
  115.7 1.0 copy-start.3
  116.7 1.0 copy-start.4
  117.8 0.9 copy-start.5
  118.7 0.8 copy-start.6

commit v2 on v1

v2 whole, which is shorter than its diff:
```python
import functools

import jax
import jax.numpy as jnp
from jax import lax
from jax.experimental import pallas as pl
from jax.experimental.pallas import tpu as pltpu
from jax.sharding import PartitionSpec as P

IMG_H = 14
IMG_W = 14
EPSILON = 1e-05
MESH = pl.DeviceIdType.MESH
F32 = jnp.float32
BF16 = jnp.bfloat16
HIGHEST = lax.Precision.HIGHEST
COLS = 16
GROUP = 8
NN = (((1,), (0,)), ((), ()))
NT = (((1,), (1,)), ((), ()))
TN = (((0,), (0,)), ((), ()))


def dot(lhs, rhs, dims=NN, precision=None):
    return lax.dot_general(lhs, rhs, dims, precision=precision, preferred_element_type=F32)


def sigmoid(values):
    return 0.5 * jnp.tanh(0.5 * values) + 0.5


def swish(values):
    return values * sigmoid(values)


def swish_slope(values):
    sigma = sigmoid(values)
    return sigma + values * sigma * (1.0 - sigma)


def tiled(row, times):
    return jnp.concatenate([row] * times, axis=1) if times > 1 else row


def colsum(values):
    return jnp.sum(values, axis=0, keepdims=True)


def put_rows(ref, at, row):
    for k in range(row.shape[1] // 128):
        ref[at + k : at + k + 1, :] = row[:, k * 128 : (k + 1) * 128]


def get_rows(ref, at, count):
    return jnp.concatenate([ref[at + k : at + k + 1, :] for k in range(count)], axis=1)


def per_slot(values, slots):
    return jnp.sum(values.reshape(slots, COLS, values.shape[1]), axis=1)


def bucket_parts(size, tile):
    unit = 16 * tile
    first = -(-(size // unit) // 2) * unit
    return [(0, first, "yx"), (first, size - first, "xy")][: 2 if size > first else 1]


def main_kernel(n_batch, n_height, sizes, *refs):
    (
        counts, row_valid, gain_one, bias_one, gain_two, bias_two, gain_mid, bias_mid,
        bias_excite, gain_three, bias_three,
        images, cotangent, w_reduce_in, w_split_in, w_squeeze_in, w_excite_in, w_expand_in,
        output, grad_images, big_e, big_a, big_b, big_r, big_q, vectors,
        img4, cot4, out4, w_reduce, w_split, w_squeeze, w_excite, w_expand,
        x, g, pix, to_pad, from_pad, c1, hs, c2, act, slope2, mixed, c3, d3, xo, gc3, gm, d2, gc2, gh, slope1, gc1,
        gc2_own, x_t, mixed_t, hs_t, att, attx, gpx, pooled, sq_all, tot,
        m1, m2, m34, m5, m6, m78, m9, m10, p5, p6, em_src,
        s1, s2, s34, s5, s6, s78, s9, s10, em_all,
        last1, up1, down1, last2, up2, down2, last3, up3, down3,
        local_sem, all_send, all_recv, pair_send, pair_recv, halo_send, halo_recv, em_sems, red_send, red_recv,
        *bucket_refs,
    ) = refs
    slots, cols, rows, width = sizes
    narrow = w_reduce.shape[1]
    split = w_split.shape[1]
    half = split // 2
    cg = w_split.shape[0] // 9
    inner = w_squeeze.shape[1]
    block = slots * COLS
    pixels = rows * block
    total = n_batch * n_height
    area = float(IMG_H * IMG_W)
    b = lax.axis_index("batch")
    h = lax.axis_index("height")
    me = b * n_height + h

    sends = []
    due = {}

    def arrive(key):
        due.pop(key)()

    def move(key, src, dst):
        copy = pltpu.make_async_copy(src, dst, local_sem.at[key])
        copy.start()
        due["move", key] = copy.wait

    for k, (src, dst) in enumerate(
        [
            (images, img4), (w_reduce_in, w_reduce), (w_split_in, w_split), (cotangent, cot4),
            (w_squeeze_in, w_squeeze), (w_excite_in, w_excite), (w_expand_in, w_expand),
        ]
    ):
        move(k, src, dst)

    barrier = pltpu.get_barrier_semaphore()

    def greet(j, carry):
        t = lax.rem(me + j, total)
        pl.semaphore_signal(
            barrier, inc=1, device_id=(t // n_height, lax.rem(t, n_height)), device_id_type=MESH
        )
        return carry

    lax.fori_loop(1, total, greet, 0)


    kh, kq = lax.rem(h, 2), h // 2
    pair_one = (b, h + 1 - 2 * kh)
    pair_two = (b, h + 2 - 4 * kq)

    def circle(dst):
        if dst.shape[0] == total:
            return me, lambda t: (t // n_height, lax.rem(t, n_height))
        pairs = n_height // 2
        return b * pairs + kq, lambda t: (t // pairs, 2 * lax.rem(t, pairs) + kh)

    def send_all(src, dst, k):
        here, device = circle(dst)
        others = dst.shape[0]

        def one(j, carry):
            pltpu.make_async_remote_copy(
                src_ref=src, dst_ref=dst.at[here], send_sem=all_send.at[k], recv_sem=all_recv.at[k],
                device_id=device(lax.rem(here + j, others)), device_id_type=MESH,
            ).start()
            return carry

        lax.fori_loop(1, others, one, 0)
        dst[here] = src[...]
        sends.append(lambda: all_copy(dst, k).wait_send())
        due["all", k] = lambda: all_copy(dst, k).wait_recv()

    def all_copy(dst, k):
        many = dst.at[pl.ds(0, dst.shape[0] - 1)]
        return pltpu.make_async_remote_copy(
            src_ref=many, dst_ref=many,
            send_sem=all_send.at[k], recv_sem=all_recv.at[k], device_id=(b, h), device_id_type=MESH,
        )

    def send_pairs(src, arrived, dst, k):
        copy = pltpu.make_async_remote_copy(
            src_ref=src, dst_ref=arrived, send_sem=pair_send.at[k], recv_sem=pair_recv.at[k],
            device_id=pair_one, device_id_type=MESH,
        )
        copy.start()
        copy.wait()
        src[...] = src[...] + arrived[...]
        send_all(src, dst, k)

    def sum_all(dst, k):
        arrive(("all", k))

        def one(i, acc):
            return acc + jnp.sum(dst[pl.ds(i * 8, 8)], axis=0)

        acc = lax.fori_loop(0, dst.shape[0] // 8, one, jnp.zeros(dst.shape[1:], F32))
        tot[0 : dst.shape[1], :] = acc

    def halo_copies(first, last, up, down, k):
        above = pltpu.make_async_remote_copy(
            src_ref=last, dst_ref=up, send_sem=halo_send.at[2 * k], recv_sem=halo_recv.at[2 * k],
            device_id=(b, lax.rem(h + 1, n_height)), device_id_type=MESH,
        )
        below = pltpu.make_async_remote_copy(
            src_ref=first, dst_ref=down, send_sem=halo_send.at[2 * k + 1],
            recv_sem=halo_recv.at[2 * k + 1],
            device_id=(b, lax.rem(h + n_height - 1, n_height)), device_id_type=MESH,
        )
        return above, below

    def halo_start(first, last, up, down, k):
        above, below = halo_copies(first, last, up, down, k)

        @pl.when(h < n_height - 1)
        def _():
            above.start()

        @pl.when(h > 0)
        def _():
            below.start()

        sends.append(lambda: halo_sent(first, last, up, down, k))
        due["halo", k] = lambda: halo_here(first, last, up, down, k)

        @pl.when(h == 0)
        def _():
            up[...] = jnp.zeros(up.shape, F32)

        @pl.when(h == n_height - 1)
        def _():
            down[...] = jnp.zeros(down.shape, F32)

    def halo_here(first, last, up, down, k):
        above, below = halo_copies(first, last, up, down, k)

        @pl.when(h > 0)
        def _():
            above.wait_recv()

        @pl.when(h < n_height - 1)
        def _():
            below.wait_recv()

    def halo_sent(first, last, up, down, k):
        above, below = halo_copies(first, last, up, down, k)

        @pl.when(h < n_height - 1)
        def _():
            above.wait_send()

        @pl.when(h > 0)
        def _():
            below.wait_send()

    count = counts[0]
    filled = row_valid[0]
    for r in range(1, rows):
        filled = filled + row_valid[r]

    def flag(cond):
        return jnp.where(cond, 1.0, 0.0).astype(F32)

    def own(at):
        return flag((at >= 1) & (at <= filled))

    def ext(at):
        return flag(
            ((at >= 1) & (at <= filled))
            | ((at == 0) & (h > 0))
            | ((at == filled + 1) & (h < n_height - 1))
        )

    def mask(scale, lanes, start=0, size=block):
        return tiled(pix[start : start + size, :] * scale, lanes // 128)

    def block_at(at):
        return pl.ds(at * block if isinstance(at, int) else pl.multiple_of(at * block, block), block)

    def set_last(src, last):
        value = jnp.zeros(last.shape, F32)
        for r in range(rows):
            value = value + src[block_at(r + 1), :] * flag(filled == r + 1)
        last[...] = value

    def patch(ref, up, down):
        ref[block_at(0), :] = up[...]
        ref[block_at(rows + 1), :] = down[...]
        whole = flag(filled == rows)
        ref[block_at(rows), :] = ref[block_at(rows), :] * whole + down[...] * (1.0 - whole)

    iota = lax.broadcasted_iota(jnp.int32, (block, 128), 0)
    pix[...] = jnp.where(((iota >> 4) < count) & ((iota & 15) < cols), 1.0, 0.0)

    def places(shape, dim):
        at = lax.broadcasted_iota(jnp.int32, shape, dim)
        r, s, c = at // block, (at >> 4) & (slots - 1), at & 15
        return r, s, c, (s * cols + c) * rows + r

    def place_in():
        shape = (pixels, slots * cols * rows)
        r, s, c, at = places(shape, 0)
        live = (c < cols) & (s < count) & (r < filled)
        other = lax.broadcasted_iota(jnp.int32, shape, 1)
        to_pad[...] = jnp.where((other == at) & live, 1.0, 0.0).astype(BF16)

    def place_out():
        shape = (slots * cols * rows, pixels)
        r, s, c, at = places(shape, 1)
        other = lax.broadcasted_iota(jnp.int32, shape, 0)
        from_pad[...] = jnp.where((other == at) & (c < cols), 1.0, 0.0).astype(BF16)

    def pad_in(src, dst):
        value = src[...].reshape(slots * cols * rows, width)
        for q in range(rows):
            at = slice(q * block, (q + 1) * block)
            dst[at, :] = dot(to_pad[at, :], value).astype(BF16)

    def pad_out(src, dst):
        for j in range(width // 256):
            lanes = slice(j * 256, (j + 1) * 256)
            value = dot(from_pad[...], src[:, lanes]).astype(BF16)
            dst[:, :, lanes] = value.reshape(slots * cols, rows, 256)

    bx, bz = lax.rem(b, 2), lax.rem(b // 2, 4)
    group, n_groups = b // GROUP, n_batch // GROUP
    peers = {"y": (kq, pair_two), "x": (bx, (b + 1 - 2 * bx, h))}
    bucket_refs = iter(bucket_refs)

    def add(dst, src, src_at, other, count):
        step = 64 if count % 64 == 0 else count

        def one(i, carry):
            at = pl.multiple_of(i * step, step)
            mine = src[pl.ds(pl.multiple_of(src_at + at, 8), step), :].astype(F32)
            dst[pl.ds(at, step), :] = (mine + other[pl.ds(at, step), :].astype(F32)).astype(dst.dtype)
            return carry

        lax.fori_loop(0, count // step, one, 0)

    class Part:
        def __init__(self, bucket, k, at, size, order):
            self.bucket, self.at, self.size = bucket, at, size
            self.sems = bucket.sems + 8 * (k + 1)
            self.in1, self.sum1, self.in2, self.sum2, self.in3, self.in4, self.shard = (
                next(bucket_refs) for _ in range(7)
            )
            (self.i1, self.peer1), (self.i2, self.peer2) = peers[order[0]], peers[order[1]]
            tile = bucket.tile
            self.u1, self.u2, self.u3 = size // 2, size // 4, size // 16
            self.at1 = pl.multiple_of(bucket.base + at + self.i1 * self.u1, tile)
            self.at2 = pl.multiple_of(self.at1 + self.i2 * self.u2, tile)
            self.at3 = pl.multiple_of(self.at2 + bz * self.u3, tile)

        def copy(self, stage, src, dst, device):
            return self.bucket.remote(self.sems + stage, src, dst, device)

        def launch(self, stage, src, dst, device):
            self.copy(stage, src, dst, device).start()
            self.expect(stage, dst)

        def expect(self, stage, many):
            sends.append(lambda: self.copy(stage, many, many, (b, h)).wait_send())
            due[self.sems, stage] = lambda: self.copy(stage, many, many, (b, h)).wait_recv()

        def cut(self, ref, at, size):
            return ref.at[pl.ds(pl.multiple_of(at, self.bucket.tile), size)]

        def s1(self):
            self.launch(0, self.cut(self.bucket.half, self.at + (1 - self.i1) * self.u1, self.u1), self.in1, self.peer1)

        def s2(self):
            arrive((self.sems, 0))
            add(self.sum1, self.bucket.half, self.at + self.i1 * self.u1, self.in1, self.u1)
            self.launch(1, self.cut(self.sum1, (1 - self.i2) * self.u2, self.u2), self.in2, self.peer2)

        def s3(self):
            arrive((self.sems, 1))
            add(self.sum2, self.sum1, self.i2 * self.u2, self.in2, self.u2)
            for j in range(1, 4):
                t = lax.rem(bz + j, 4)
                device = (b + 2 * (t - bz), h)
                self.copy(2, self.cut(self.sum2, t * self.u3, self.u3), self.in3.at[bz], device).start()
            self.expect(2, self.in3.at[pl.ds(0, 3)])
            self.in3[bz] = self.sum2[pl.ds(pl.multiple_of(bz * self.u3, self.bucket.tile), self.u3), :]

        def s4(self):
            arrive((self.sems, 2))
            value = self.in3[0].astype(F32)
            for t in range(1, 4):
                value = value + self.in3[t].astype(F32)
            kind = self.shard.dtype
            if n_groups > 1:
                self.shard[...] = value.astype(kind)

                def send_group(j, carry):
                    t = lax.rem(group + j, n_groups)
                    device = (b + GROUP * (t - group), h)
                    self.copy(3, self.shard, self.in4.at[group], device).start()
                    return carry

                lax.fori_loop(1, n_groups, send_group, 0)
                self.expect(3, self.in4.at[pl.ds(0, n_groups - 1)])
                self.in4[group] = self.shard[...]
                arrive((self.sems, 3))
                value = self.in4[0].astype(F32)
                for t in range(1, n_groups):
                    value = value + self.in4[t].astype(F32)
            done = self.bucket.done
            done[pl.ds(self.at3, self.u3), :] = self.bucket.final(value, self).astype(kind)
            mine = done.at[pl.ds(self.at3, self.u3)]
            for j in range(1, 4):
                t = lax.rem(bz + j, 4)
                self.copy(4, mine, mine, (b + 2 * (t - bz), h)).start()
            self.expect(4, done.at[pl.ds(0, 3 * self.u3)])

        def s5(self):
            arrive((self.sems, 4))
            mine = self.bucket.done.at[pl.ds(self.at2, self.u2)]
            self.launch(5, mine, mine, self.peer2)

        def s6(self):
            arrive((self.sems, 5))
            mine = self.bucket.done.at[pl.ds(self.at1, self.u1)]
            self.launch(6, mine, mine, self.peer1)

        def s7(self):
            arrive((self.sems, 6))

    class Bucket:
        def __init__(self, at):
            self.full, self.in0, self.half, self.done = (next(bucket_refs) for _ in range(4))
            self.tile = 8 if self.full.dtype == F32 else 16
            self.sems = at * 24
            self.size = self.full.shape[0] // 2
            self.base = pl.multiple_of(kh * self.size, self.tile)
            self.final = lambda value, part: value
            self.parts = [Part(self, k, *spec) for k, spec in enumerate(bucket_parts(self.size, self.tile))]

        def remote(self, k, src, dst, device):
            return pltpu.make_async_remote_copy(
                src_ref=src, dst_ref=dst, send_sem=red_send.at[k], recv_sem=red_recv.at[k],
                device_id=device, device_id_type=MESH,
            )

        def launch(self, stage, src, dst):
            copy = self.remote(self.sems + stage, src, dst, pair_one)
            copy.start()
            sends.append(copy.wait_send)
            due[self.sems, stage] = copy.wait_recv

        def s0(self):
            self.launch(0, self.full.at[pl.ds(pl.multiple_of((1 - kh) * self.size, self.tile), self.size)], self.in0)

        def s1(self):
            arrive((self.sems, 0))
            add(self.half, self.full, self.base, self.in0, self.size)
            for part in self.parts:
                part.s1()

        def s2(self):
            for part in self.parts:
                part.s2()

        def s3(self):
            for part in self.parts:
                part.s3()

        def s4(self):
            for part in self.parts:
                part.s4()

        def s5(self):
            for part in self.parts:
                part.s5()

        def s6(self):
            for part in self.parts:
                part.s6()

        def s7(self):
            for part in self.parts:
                part.s7()
            mine = self.done.at[pl.ds(self.base, self.size)]
            self.launch(1, mine, mine)

        def s8(self):
            arrive((self.sems, 1))

    bucket_e, bucket_a, bucket_b, bucket_r, bucket_q = (Bucket(k) for k in range(5))

    place_in()
    arrive(("move", 0))
    pad_in(img4, x)
    arrive(("move", 1))
    sum_one = jnp.zeros((1, narrow), F32)
    square_one = jnp.zeros((1, narrow), F32)
    for q in range(rows // 2):
        value = dot(x[pl.ds(q * 2 * block, 2 * block), :], w_reduce[...])
        c1[pl.ds((1 + 2 * q) * block, 2 * block), :] = value
        sum_one = sum_one + colsum(value)
        square_one = square_one + colsum(value * value)
    m1[...] = jnp.zeros(m1.shape, F32)
    put_rows(m1, 0, sum_one)
    put_rows(m1, narrow // 128, square_one)
    m1[4:5, :] = jnp.zeros((1, 128), F32) + count.astype(F32)
    pl.semaphore_wait(barrier, total - 1)
    send_all(m1, s1, 0)
    set_last(c1, last1)
    first1 = c1.at[block_at(1)]
    halo_start(first1, last1, up1, down1, 0)
    arrive(("move", 3))
    pad_in(cot4, g)

    sum_all(s1, 0)
    slot_total = tot[4:5, :] / n_height
    pix_total = slot_total * area
    m_one = tiled(pix_total, narrow // 128)
    mean = get_rows(tot, 0, narrow // 128) / m_one
    inv_one = lax.rsqrt(get_rows(tot, 2, narrow // 128) / m_one - mean * mean + EPSILON)
    shift_one = mean * inv_one
    scale = inv_one * gain_one[...]
    offset = bias_one[...] - mean * scale
    scale_one, offset_one = scale, offset
    arrive(("halo", 0))
    patch(c1, up1, down1)

    def hide(at, carry):
        value = c1[block_at(at), :] * scale_one + offset_one
        value = swish(value) * mask(ext(at), narrow)
        hs[0, block_at(at), :] = pltpu.roll(value, 1, axis=0).astype(BF16)
        hs[1, block_at(at), :] = value.astype(BF16)
        hs[2, block_at(at), :] = pltpu.roll(value, block - 1, axis=0).astype(BF16)
        return carry

    lax.fori_loop(0, rows + 2, hide, 0)

    arrive(("move", 2))
    for q in range(rows // 2):
        for gr in range(2):
            lhs = jnp.concatenate(
                [
                    hs[bb, (a + 2 * q) * block : (a + 2 * q + 2) * block, gr * cg : (gr + 1) * cg]
                    for a in range(3)
                    for bb in range(3)
                ],
                axis=1,
            )
            c2[(1 + 2 * q) * block : (3 + 2 * q) * block, gr * half : (gr + 1) * half] = dot(
                lhs, w_split[:, gr * half : (gr + 1) * half]
            )
    m2[...] = jnp.zeros(m2.shape, F32)
    for j in range(2):
        lanes = pl.ds(j * half, half)

        def moments(r, carry):
            value = c2[block_at(r), lanes] * mask(own(r), half)
            return carry[0] + colsum(value), carry[1] + colsum(value * value)

        zero = jnp.zeros((1, half), F32)
        sums = lax.fori_loop(1, rows + 1, moments, (zero, zero))
        put_rows(m2, j * (half // 128), sums[0])
        put_rows(m2, split // 128 + j * (half // 128), sums[1])
    send_all(m2, s2, 1)
    set_last(c2, last2)
    first2 = c2.at[block_at(1)]
    halo_start(first2, last2, up2, down2, 1)
    x_t[...] = x[...].T
    place_out()

    sum_all(s2, 1)
    m_two = tiled(pix_total, split // 128)
    mean = get_rows(tot, 0, split // 128) / m_two
    inv_two = lax.rsqrt(get_rows(tot, split // 128, split // 128) / m_two - mean * mean + EPSILON)
    shift_two = mean * inv_two
    scale_two = inv_two * gain_two[...]
    offset_two = bias_two[...] - mean * scale_two
    pool = jnp.zeros((slots, half), F32)
    for j in range(2):
        lanes = pl.ds(j * half, half)
        sc, of = scale_two[:, j * half : (j + 1) * half], offset_two[:, j * half : (j + 1) * half]

        def activate(r, acc):
            value = swish(c2[block_at(r), lanes] * sc + of) * mask(own(r), half)
            act[block_at(r - 1), lanes] = value
            return acc + value

        acc = lax.fori_loop(1, rows + 1, activate, jnp.zeros((block, half), F32))
        pool = pool + per_slot(acc, slots)
    pool = pool / area
    pooled[...] = pool
    arrive(("move", 4))
    m34[...] = dot(pool, w_squeeze[...], precision=HIGHEST)
    send_all(m34, s34, 2)
    for bb in range(3):
        hs_t[bb] = hs[bb].T

    arrive(("move", 5))
    arrive(("all", 2))

    def gather(i, carry):
        value = jnp.sum(s34[pl.ds(i * n_height, n_height)], axis=0)
        sq_all[i] = value
        return carry[0] + colsum(value), carry[1] + colsum(value * value)

    zero = jnp.zeros((1, inner), F32)
    sum_mid, square_mid = lax.fori_loop(0, n_batch, gather, (zero, zero))
    mean = sum_mid / slot_total
    inv_mid = lax.rsqrt(square_mid / slot_total - mean * mean + EPSILON)
    norm_mid = (sq_all[b] - mean) * inv_mid
    pre_mid = norm_mid * gain_mid[...] + bias_mid[...]
    middle = swish(pre_mid)
    logits = dot(middle, w_excite[...], precision=HIGHEST) + bias_excite[...]
    top = jnp.maximum(logits[:, :half], logits[:, half:])
    expo_one = jnp.exp(logits[:, :half] - top)
    expo_two = jnp.exp(logits[:, half:] - top)
    att_one = expo_one / (expo_one + expo_two)
    att_two = expo_two / (expo_one + expo_two)
    att[:, 0:half] = att_one
    att[:, half:split] = att_two
    for s in range(slots):
        attx[s * COLS : (s + 1) * COLS, :] = jnp.broadcast_to(att[s : s + 1, :], (COLS, split))

    def mix(r, carry):
        at = block_at(r)
        mixed[at, :] = (
            attx[:, 0:half] * act[at, 0:half] + attx[:, half:split] * act[at, half:split]
        ).astype(BF16)
        return carry

    lax.fori_loop(0, rows, mix, 0)
    arrive(("move", 6))
    for j in range(width // 256):
        lanes = pl.ds(j * 256, 256)
        sums = jnp.zeros((1, 256), F32)
        squares = jnp.zeros((1, 256), F32)
        for q in range(rows // 2):
            at = pl.ds(q * 2 * block, 2 * block)
            value = dot(mixed[at, :], w_expand[:, lanes])
            c3[at, lanes] = value
            sums = sums + colsum(value)
            squares = squares + colsum(value * value)
        put_rows(m5, j * 2, sums)
        put_rows(m5, width // 128 + j * 2, squares)
    send_pairs(m5, p5, s5, 3)
    mixed_t[...] = mixed[...].T
    arrive(("halo", 1))
    patch(c2, up2, down2)
    for j in range(2):
        lanes = pl.ds(j * half, half)
        sc, of = scale_two[:, j * half : (j + 1) * half], offset_two[:, j * half : (j + 1) * half]

        def slopes(at, carry):
            value = swish_slope(c2[block_at(at), lanes] * sc + of)
            slope2[block_at(at), lanes] = value * mask(ext(at), half)
            return carry

        lax.fori_loop(0, rows + 2, slopes, 0)

    def slopes_one(r, carry):
        value = swish_slope(c1[block_at(r + 1), :] * scale_one + offset_one)
        slope1[block_at(r), :] = value * mask(own(r + 1), narrow)
        return carry

    lax.fori_loop(0, rows, slopes_one, 0)

    sum_all(s5, 3)
    wide = width // 128
    m_three = tiled(pix_total, wide)
    mean = get_rows(tot, 0, wide) / m_three
    inv_three = lax.rsqrt(get_rows(tot, wide, wide) / m_three - mean * mean + EPSILON)
    shift_three = mean * inv_three
    scale_three = inv_three * gain_three[...]
    offset_three = bias_three[...] - mean * scale_three
    part = block // 2
    for j in range(width // 256):
        lanes = pl.ds(j * 256, 256)
        cut = slice(j * 256, (j + 1) * 256)
        sc, of = scale_three[:, cut], offset_three[:, cut]
        iv, sh = inv_three[:, cut], shift_three[:, cut]

        def finish_row(i, carry):
            r, k = i // 2, lax.rem(i, 2)
            at = pl.ds(pl.multiple_of(i * part, part), part)
            conv = c3[at, lanes]
            pre = conv * sc + of + x[at, lanes].astype(F32)
            sigma = sigmoid(pre)
            value = pre * sigma
            live = tiled(pix[pl.ds(pl.multiple_of(k * part, part), part), :] * own(r + 1), 2)
            xo[at, lanes] = (value * live).astype(BF16)
            slope = sigma + value * (1.0 - sigma)
            grad = g[at, lanes].astype(F32) * slope
            d3[at, lanes] = grad
            return carry[0] + colsum(grad), carry[1] + colsum(grad * (conv * iv - sh))

        zero = jnp.zeros((1, 256), F32)
        sums = lax.fori_loop(0, 2 * rows, finish_row, (zero, zero))
        put_rows(m6, j * 2, sums[0])
        put_rows(m6, wide + j * 2, sums[1])
    send_pairs(m6, p6, s6, 4)
    pad_out(xo, out4)
    move(7, out4, output)

    sum_all(s6, 4)
    gb_three = get_rows(tot, 0, wide)
    gg_three = get_rows(tot, wide, wide)
    vectors[0:1, :] = gb_three
    vectors[1:2, :] = gg_three
    gg = gg_three / m_three
    k_one = scale_three
    k_three = k_one * inv_three * gg
    k_two = k_one * (gb_three / m_three - shift_three * gg)
    for j in range(width // 256):
        lanes = pl.ds(j * 256, 256)
        cut = slice(j * 256, (j + 1) * 256)
        ka, kb, kc = k_one[:, cut], k_two[:, cut], k_three[:, cut]

        def back_three(i, carry):
            at = pl.ds(pl.multiple_of(i * part, part), part)
            gc3[at, lanes] = (d3[at, lanes] * ka - kb - c3[at, lanes] * kc).astype(BF16)
            return carry

        lax.fori_loop(0, 2 * rows, back_three, 0)
    for q in range(rows // 2):
        gm[pl.ds((1 + 2 * q) * block, 2 * block), :] = dot(
            gc3[pl.ds(2 * q * block, 2 * block), :], w_expand[...], NT
        )
    set_last(gm, last3)
    first3 = gm.at[block_at(1)]
    halo_start(first3, last3, up3, down3, 2)
    grad_att = []
    for j in range(2):
        lanes = pl.ds(j * half, half)

        def attend(r, acc):
            return acc + gm[block_at(r + 1), :] * act[block_at(r), lanes]

        acc = lax.fori_loop(0, rows, attend, jnp.zeros((block, half), F32))
        grad_att.append(per_slot(acc, slots))
    blend = att_one * grad_att[0] + att_two * grad_att[1]
    grad_logits = jnp.concatenate(
        [att_one * (grad_att[0] - blend), att_two * (grad_att[1] - blend)], axis=1
    )
    em_part = dot(grad_logits, w_excite[...], NT, HIGHEST) * swish_slope(pre_mid)
    em_src[...] = em_part
    m78[0:1, :] = colsum(em_part)
    m78[1:2, :] = colsum(em_part * norm_mid)

    many = em_all.at[pl.ds(0, n_height - 1)]
    em_wait = pltpu.make_async_remote_copy(
        src_ref=many, dst_ref=many, send_sem=em_sems.at[0], recv_sem=em_sems.at[1],
        device_id=(b, h), device_id_type=MESH,
    )

    def em_copy(j):
        return pltpu.make_async_remote_copy(
            src_ref=em_src, dst_ref=em_all.at[h], send_sem=em_sems.at[0], recv_sem=em_sems.at[1],
            device_id=(b, lax.rem(h + j, n_height)), device_id_type=MESH,
        )

    for j in range(1, n_height):
        em_copy(j).start()
    sends.append(lambda: em_wait.wait_send())
    due["em"] = lambda: em_wait.wait_recv()
    em_all[h] = em_src[...]
    send_all(m78, s78, 5)
    for j in range(width // 256):
        bucket_e.full[j * narrow : (j + 1) * narrow, :] = dot(
            mixed_t[...], gc3[:, j * 256 : (j + 1) * 256]
        ).astype(BF16)
    bucket_e.s0()
    grad_excite = dot(middle, grad_logits, TN, HIGHEST)
    last = bucket_b.full.shape[0] - 2 * inner
    bucket_b.full[last : last + inner, :] = grad_excite[:, :half].astype(BF16)
    bucket_b.full[last + inner :, :] = grad_excite[:, half:].astype(BF16)
    bias_part = colsum(grad_logits)
    put_rows(m10, 2 * (narrow // 128), bias_part)
    bucket_e.s1()

    sum_all(s78, 5)
    gb_mid, gg_mid = tot[0:1, :], tot[1:2, :]
    vectors[4:5, 0:128] = gb_mid
    vectors[4:5, 128:256] = gg_mid
    arrive("em")
    em = jnp.sum(em_all[...], axis=0)
    slot_live = jnp.where(lax.broadcasted_iota(jnp.int32, (slots, inner), 0) < count, 1.0, 0.0)
    grad_sq = (
        slot_live * inv_mid * gain_mid[...]
        * (em - gb_mid / slot_total - norm_mid * gg_mid / slot_total)
    )
    grad_pooled = dot(grad_sq, w_squeeze[...], NT, HIGHEST) / area
    pooled_grad = dot(pooled[...], grad_sq, TN, HIGHEST)
    att[:, 0:half] = grad_pooled
    for s in range(slots):
        gpx[s * COLS : (s + 1) * COLS, :] = jnp.broadcast_to(att[s : s + 1, 0:half], (COLS, half))
    arrive(("halo", 2))
    patch(gm, up3, down3)
    for j in range(2):
        lanes = pl.ds(j * half, half)
        iv, sh = inv_two[:, j * half : (j + 1) * half], shift_two[:, j * half : (j + 1) * half]

        def back_act(at, carry):
            value = (attx[:, lanes] * gm[block_at(at), :] + gpx[...]) * slope2[block_at(at), lanes]
            d2[block_at(at), lanes] = value
            value = value * own(at)
            norm = c2[block_at(at), lanes] * iv - sh
            return carry[0] + colsum(value), carry[1] + colsum(value * norm)

        zero = jnp.zeros((1, half), F32)
        sums = lax.fori_loop(0, rows + 2, back_act, (zero, zero))
        put_rows(m9, j * (half // 128), sums[0])
        put_rows(m9, split // 128 + j * (half // 128), sums[1])
    send_all(m9, s9, 6)
    bucket_q.full[...] = pooled_grad
    bucket_q.s0()
    bucket_e.s2()
    bucket_q.s1()

    sum_all(s9, 6)
    gb_two = get_rows(tot, 0, split // 128)
    gg_two = get_rows(tot, split // 128, split // 128)
    vectors[2:3, 0:split] = gb_two
    vectors[2:3, split : 2 * split] = gg_two
    gg = gg_two / m_two
    k_one = scale_two
    k_three = k_one * inv_two * gg
    k_two = k_one * (gb_two / m_two - shift_two * gg)
    for j in range(2):
        lanes = pl.ds(j * half, half)
        cut = slice(j * half, (j + 1) * half)
        ka, kb, kc = k_one[:, cut], k_two[:, cut], k_three[:, cut]

        def back_two(at, carry):
            value = d2[block_at(at), lanes] * ka - kb - c2[block_at(at), lanes] * kc
            gc2[block_at(at), lanes] = (value * mask(ext(at), half)).astype(BF16)
            return carry

        lax.fori_loop(0, rows + 2, back_two, 0)
    gc2_own[...] = (gc2[block_at(rows), :].astype(F32) * own(rows)).astype(BF16)
    bucket_e.s3()
    bucket_q.s2()

    def taps_grad(gr, bb, dst, at):
        lhs = jnp.concatenate(
            [hs_t[bb, gr * cg : (gr + 1) * cg, a * block : a * block + pixels] for a in range(3)], axis=0
        )
        lanes = slice(gr * half, (gr + 1) * half)
        rhs = jnp.concatenate([gc2[block:pixels, lanes], gc2_own[:, lanes]], axis=0)
        dst[at : at + 3 * cg, :] = dot(lhs, rhs).astype(BF16)

    for k in range(6):
        near = k * 3 * cg < bucket_a.full.shape[0]
        bucket = bucket_a if near else bucket_b
        taps_grad(k // 3, k % 3, bucket.full, k * 3 * cg - (0 if near else bucket_a.full.shape[0]))
        if (k + 1) * 3 * cg == bucket_a.full.shape[0]:
            bucket_a.s0()
    bucket_b.s0()
    bucket_a.s1()
    for gr in range(2):
        outs = []
        for bb in range(3):
            lhs = jnp.concatenate(
                [gc2[(2 - a) * block : (2 - a) * block + pixels, gr * half : (gr + 1) * half] for a in range(3)],
                axis=1,
            )
            rhs = jnp.concatenate(
                [
                    w_split[(a * 3 + bb) * cg : (a * 3 + bb + 1) * cg, gr * half : (gr + 1) * half]
                    for a in range(3)
                ],
                axis=1,
            )
            outs.append(dot(lhs, rhs, NT))
        gh[:, gr * cg : (gr + 1) * cg] = (
            outs[1] + pltpu.roll(outs[2], 1, axis=0) + pltpu.roll(outs[0], pixels - 1, axis=0)
        )

    bucket_b.s1()

    def back_hidden(r, carry):
        value = gh[block_at(r), :] * slope1[block_at(r), :]
        gh[block_at(r), :] = value
        norm = c1[block_at(r + 1), :] * inv_one - shift_one
        return carry[0] + colsum(value), carry[1] + colsum(value * norm)

    zero = jnp.zeros((1, narrow), F32)
    sums = lax.fori_loop(0, rows, back_hidden, (zero, zero))
    put_rows(m10, 0, sums[0])
    put_rows(m10, narrow // 128, sums[1])
    send_all(m10, s10, 7)
    bucket_a.s2()
    bucket_e.s4()
    bucket_q.s3()
    bucket_b.s2()
    sum_all(s10, 7)
    gb_one = get_rows(tot, 0, narrow // 128)
    gg_one = get_rows(tot, narrow // 128, narrow // 128)
    vectors[3:4, 0:narrow] = gb_one
    vectors[3:4, narrow : 2 * narrow] = gg_one
    vectors[3:4, 2 * narrow : 2 * narrow + split] = get_rows(tot, 2 * (narrow // 128), split // 128)
    gg = gg_one / m_one
    k_one = scale_one
    k_three = k_one * inv_one * gg
    k_two = k_one * (gb_one / m_one - shift_one * gg)

    def back_one(r, carry):
        value = gh[block_at(r), :] * k_one - k_two - c1[block_at(r + 1), :] * k_three
        gc1[block_at(r), :] = (value * mask(own(r + 1), narrow)).astype(BF16)
        return carry

    lax.fori_loop(0, rows, back_one, 0)
    for q in range(2):
        at = q * (width // 2)
        bucket_r.full[at : at + width // 2, :] = dot(x_t[at : at + width // 2, :], gc1[...]).astype(BF16)
    bucket_r.s0()
    bucket_a.s3()
    bucket_r.s1()
    bucket_b.s3()
    bucket_e.s5()
    bucket_q.s4()
    arrive(("move", 7))

    def back_image(r, carry):
        value = d3[block_at(r), :] + dot(gc1[block_at(r), :], w_reduce[...], NT)
        xo[block_at(r), :] = value.astype(BF16)
        return carry

    lax.fori_loop(0, rows, back_image, 0)
    bucket_r.s2()
    bucket_a.s4()
    bucket_e.s6()
    bucket_b.s4()
    bucket_r.s3()
    pad_out(xo, out4)
    move(7, out4, grad_images)
    bucket_q.s5()
    bucket_a.s5()
    bucket_e.s7()
    bucket_b.s5()
    bucket_r.s4()
    bucket_q.s6()
    bucket_a.s6()
    bucket_e.s8()
    move(0, bucket_e.done, big_e)
    bucket_b.s6()
    bucket_r.s5()
    bucket_q.s7()
    bucket_a.s7()
    bucket_b.s7()
    bucket_r.s6()
    bucket_q.s8()
    move(3, bucket_q.done, big_q)
    bucket_a.s8()
    move(1, bucket_a.done, big_a)
    bucket_b.s8()
    move(4, bucket_b.done, big_b)
    bucket_r.s7()
    bucket_r.s8()
    move(2, bucket_r.done, big_r)

    for wait in sends:
        wait()
    for key in list(due):
        arrive(key)


def unpack_kernel(
    out_a, gimg_a, big_e, big_a, big_b, big_r, big_q, vectors,
    output, grad_images, grad_reduce, grad_split, grad_squeeze, grad_excite, grad_expand,
    grad_gain_one, grad_bias_one, grad_gain_two, grad_bias_two,
    grad_gain_mid, grad_bias_mid, grad_bias_excite, grad_gain_three, grad_bias_three,
    in_e, in_a, in_b, in_r, in_v, in_o, in_g, in_q, out_e, out_s, out_x, out_r, sems,
):
    def move(k, src, dst):
        copy = pltpu.make_async_copy(src, dst, sems.at[k])
        copy.start()
        return copy

    ins = [move(k, src, dst) for k, (src, dst) in enumerate(
        [(big_e, in_e), (big_a, in_a), (big_b, in_b), (big_r, in_r), (vectors, in_v), (out_a, in_o), (gimg_a, in_g),
         (big_q, in_q)]
    )]
    outs = []
    narrow = grad_expand.shape[0]
    taps, split = grad_split.shape
    half = split // 2
    inner = grad_excite.shape[0]
    ins[0].wait()
    for j in range(grad_expand.shape[1] // 256):
        out_e[:, j * 256 : (j + 1) * 256] = in_e[j * narrow : (j + 1) * narrow, :].astype(F32)
    outs.append(move(8, out_e, grad_expand))
    ins[1].wait()
    ins[2].wait()
    cg = taps // 9
    near = in_a.shape[0]
    for k in range(18):
        gr, bb, a = k // 9, k // 3 % 3, k % 3
        ref, at = (in_a, k * cg) if k * cg < near else (in_b, k * cg - near)
        out_s[(a * 3 + bb) * cg : (a * 3 + bb + 1) * cg, gr * half : (gr + 1) * half] = ref[at : at + cg, :].astype(F32)
    last = in_b.shape[0] - 2 * inner
    for gr in range(2):
        out_x[:, gr * half : (gr + 1) * half] = in_b[last + gr * inner : last + (gr + 1) * inner, :].astype(F32)
    outs.append(move(9, out_s, grad_split))
    outs.append(move(10, out_x, grad_excite))
    ins[3].wait()
    out_r[...] = in_r[...].astype(F32)
    outs.append(move(11, out_r, grad_reduce))
    ins[4].wait()
    grad_bias_three[...] = in_v[0:1, :]
    grad_gain_three[...] = in_v[1:2, :]
    grad_bias_two[...] = in_v[2:3, 0:split]
    grad_gain_two[...] = in_v[2:3, split : 2 * split]
    grad_bias_one[...] = in_v[3:4, 0:narrow]
    grad_gain_one[...] = in_v[3:4, narrow : 2 * narrow]
    grad_bias_excite[...] = in_v[3:4, 2 * narrow : 2 * narrow + split]
    grad_bias_mid[...] = in_v[4:5, 0:inner]
    grad_gain_mid[...] = in_v[4:5, inner : 2 * inner]
    for k, (src, dst) in enumerate([(in_o, output), (in_g, grad_images), (in_q, grad_squeeze)]):
        ins[5 + k].wait()
        outs.append(move(12 + k, src, dst))
    for copy in outs:
        copy.wait()


def shards(
    n_batch, n_height,
    images, counts, row_valid, w_reduce, gain_one, bias_one, w_split, gain_two, bias_two, w_squeeze,
    gain_mid, bias_mid, w_excite, bias_excite, w_expand, gain_three, bias_three, cotangent,
):
    slots, rows, cols, width = images.shape
    count = slots * rows * cols
    narrow = w_reduce.shape[1]
    split = w_split.shape[3]
    taps = 9 * w_split.shape[2]
    inner = w_squeeze.shape[1]
    half = split // 2
    total = n_batch * n_height
    block = slots * COLS
    pixels = rows * block
    padded = pixels + 2 * block
    n_groups = n_batch // GROUP

    def row(v):
        return v.reshape(1, -1)

    unit = 4 * GROUP * 16
    size_e = width // 256 * narrow
    size_a = -(-taps // unit) * unit
    size_b = 2 * taps + 2 * inner - size_a
    size_r = width

    def bucket(size, lanes=256, kind=BF16):
        kept = size // 2
        shapes = [(size, lanes), (kept, lanes), (kept, lanes), (size, lanes)]
        for _, rows_, _ in bucket_parts(kept, 8 if kind == F32 else 16):
            cut = rows_ // 16
            shapes += [(rows_ // 2, lanes)] * 2 + [(rows_ // 4, lanes)] * 2
            shapes += [(4, cut, lanes), (n_groups, cut, lanes), (cut, lanes)]
        return [pltpu.VMEM(dims, kind) for dims in shapes]

    heights = [8, 8, 8, 16, 16, 2, 8, 8]
    vm = pltpu.VMEM
    scratch = (
        [vm((slots * cols, rows, width), BF16)] * 3
        + [vm((width, narrow), BF16), vm((taps, split), BF16), vm((narrow, inner), F32), vm((inner, split), F32),
           vm((narrow, width), BF16)]
        + [vm((pixels, width), BF16), vm((pixels, width), BF16), vm((block, 128), F32), vm((pixels, count), BF16),
           vm((count, pixels), BF16)]
        + [vm((padded, narrow), F32), vm((3, padded, narrow), BF16), vm((padded, split), F32), vm((pixels, split), F32),
           vm((padded, split), F32), vm((pixels, half), BF16), vm((pixels, width), F32), vm((pixels, width), F32),
           vm((pixels, width), BF16), vm((pixels, width), BF16), vm((padded, half), F32),
           vm((padded, split), F32), vm((padded, split), BF16), vm((pixels, narrow), F32), vm((pixels, narrow), F32),
           vm((pixels, narrow), BF16), vm((block, split), BF16)]
        + [vm((width, pixels), BF16), vm((half, pixels), BF16), vm((3, narrow, padded), BF16), vm((slots, split), F32),
           vm((block, split), F32), vm((block, half), F32), vm((slots, half), F32), vm((n_batch, slots, inner), F32),
           vm((16, 128), F32)]
        + [vm((k, 128), F32) for k in heights] + [vm((16, 128), F32)] * 2 + [vm((slots, inner), F32)]
        + [vm((total // 2 if k == 16 else total, k, 128), F32) for k in heights] + [vm((n_height, slots, inner), F32)]
        + [vm((block, narrow), F32)] * 3 + [vm((block, split), F32)] * 3 + [vm((block, half), F32)] * 3
        + [pltpu.SemaphoreType.DMA((8,))] * 5
        + [pltpu.SemaphoreType.DMA((6,)), pltpu.SemaphoreType.DMA((6,)), pltpu.SemaphoreType.DMA((2,)),
           pltpu.SemaphoreType.DMA((120,)), pltpu.SemaphoreType.DMA((120,))]
        + bucket(size_e) + bucket(size_a) + bucket(size_b) + bucket(size_r) + bucket(narrow, inner, F32)
    )
    smem = pl.BlockSpec(memory_space=pltpu.SMEM)
    vmem = pl.BlockSpec(memory_space=pltpu.VMEM)
    hbm = pl.BlockSpec(memory_space=pltpu.HBM)
    shape = jax.ShapeDtypeStruct
    flat = (slots * cols, rows, width)

    def by_column(value):
        return value.transpose(0, 2, 1, 3).reshape(flat)

    def by_row(value):
        return value.reshape(slots, cols, rows, width).transpose(0, 2, 1, 3)

    out_a, gimg_a, big_e, big_a, big_b, big_r, big_q, vectors = pl.pallas_call(
        functools.partial(main_kernel, n_batch, n_height, (slots, cols, rows, width)),
        out_shape=(
            shape(flat, BF16), shape(flat, BF16), shape((size_e, 256), BF16),
            shape((size_a, 256), BF16), shape((size_b, 256), BF16), shape((size_r, 256), BF16), shape((narrow, inner), F32),
            shape((8, width), F32),
        ),
        in_specs=[smem, smem] + [vmem] * 9 + [hbm] * 7,
        out_specs=[hbm] * 7 + [vmem],
        scratch_shapes=scratch,
        compiler_params=pltpu.CompilerParams(
            collective_id=0, has_side_effects=True, vmem_limit_bytes=58 * 1024 * 1024
        ),
    )(
        counts, row_valid, row(gain_one), row(bias_one), row(gain_two), row(bias_two), row(gain_mid), row(bias_mid),
        row(bias_excite), row(gain_three), row(bias_three),
        by_column(images), by_column(cotangent), w_reduce, w_split.reshape(taps, split), w_squeeze, w_excite, w_expand,
    )
    (
        output, grad_images, grad_reduce, grad_split, grad_squeeze, grad_excite, grad_expand,
        grad_gain_one, grad_bias_one, grad_gain_two, grad_bias_two,
        grad_gain_mid, grad_bias_mid, grad_bias_excite, grad_gain_three, grad_bias_three,
    ) = pl.pallas_call(
        unpack_kernel,
        out_shape=(
            shape(flat, BF16), shape(flat, BF16), shape((width, narrow), F32), shape((taps, split), F32),
            shape((narrow, inner), F32), shape((inner, split), F32), shape((narrow, width), F32),
            shape((1, narrow), F32), shape((1, narrow), F32), shape((1, split), F32), shape((1, split), F32),
            shape((1, inner), F32), shape((1, inner), F32), shape((1, split), F32), shape((1, width), F32),
            shape((1, width), F32),
        ),
        in_specs=[hbm] * 8,
        out_specs=[hbm] * 7 + [vmem] * 9,
        scratch_shapes=[
            vm((size_e, 256), BF16), vm((size_a, 256), BF16), vm((size_b, 256), BF16), vm((size_r, 256), BF16), vm((8, width), F32),
            vm(flat, BF16), vm(flat, BF16), vm((narrow, inner), F32),
            vm((narrow, width), F32), vm((taps, split), F32), vm((inner, split), F32), vm((width, narrow), F32),
            pltpu.SemaphoreType.DMA((15,)),
        ],
        compiler_params=pltpu.CompilerParams(vmem_limit_bytes=60 * 1024 * 1024),
    )(out_a, gimg_a, big_e, big_a, big_b, big_r, big_q, vectors)

    def like(value, other):
        return value.reshape(other.shape)

    return (
        by_row(output), by_row(grad_images), grad_reduce, like(grad_gain_one, gain_one), like(grad_bias_one, bias_one),
        like(grad_split, w_split), like(grad_gain_two, gain_two), like(grad_bias_two, bias_two), grad_squeeze,
        like(grad_gain_mid, gain_mid), like(grad_bias_mid, bias_mid), grad_excite, like(grad_bias_excite, bias_excite),
        grad_expand, like(grad_gain_three, gain_three), like(grad_bias_three, bias_three),
    )


def solution(mesh):
    axes = mesh.shape
    split_in = P("batch", "height", None, None)
    return jax.shard_map(
        functools.partial(shards, axes["batch"], axes["height"]),
        mesh=mesh,
        in_specs=(split_in, P("batch"), P("height")) + (P(),) * 14 + (split_in,),
        out_specs=(split_in, split_in) + (P(),) * 14,
        check_vma=False,
    )
```

time: 128 us -> 101 us (0.79); the launches traced: 125 us -> 101 us
  local copies, waits for them, and re-layouts: 14.5 us -> 0 us
  Pallas kernels: 109 us -> 99.3 us
    unnamed x20 -> x0, local copies, waits for them, and re-layouts: 14.5 us -> none
    pallas_call x2, Pallas kernels: 109 us -> 99.3 us  [the longest x1 94.5 us: shards(): pl.pallas_call(functools.partial(main_kernel, n_batch, n_height, (slots,...]
where the time goes in v2:
time: 101 us
  Pallas kernels  99.3 us (98%)
  between operations  1.47 us (1%)
    pallas_call x1, Pallas kernels, shards(): pl.pallas_call(functools.partial(main_kernel, n_batch, n_height, (slots,...  94.5 us
    pallas_call x1, Pallas kernels, shards(): pl.pallas_call(unpack_kernel, out_shape=(shape(flat, BF16), shape(flat, B...  4.79 us

profile of v2, /device:TPU:1, one launch (start us, length us, event | category | flops | bytes accessed | tf_op | source)
XLA Modules:
  0.0 100.7 jit_solution(25187211466969799)
XLA Ops:
  1.3 94.5 %shard_map.297 = (bf16[112,4,1024]{2,1,0:T(4,128)(2,1)}, bf16[112,4,1024]{2,1,0:T(4,128)(2,1)}, bf16[1024,256]{1,0:T(8,128)(2,1)}, bf16[1536,256]{1,0:T(8,128)(2...) custom-call(s32[1]{0:T(128)S(6)} %copy.34.refs_0_, ...), custom_call_target="tpu_custom_call" | custom-call | tf_op jit(solution)/shard_map/pallas_call | solution.py:1077
  95.8 4.8 %shard_map.298 = (bf16[112,4,1024]{2,1,0:T(4,128)(2,1)}, bf16[112,4,1024]{2,1,0:T(4,128)(2,1)}, f32[1024,256]{1,0:T(8,128)}, f32[1152,512]{1,0:T(8,128)}, f32[25...) custom-call(bf16[112,4,1024]{2,1,0:T(4,128)(2,1)} %get-tuple-element, ...), custom_call_target="tpu_custom_call" | custom-call | tf_op jit(solution)/shard_map/pallas_call | solution.py:1099

commit v3 on v2

v3 whole, which is shorter than its diff:
```python
import functools

import jax
import jax.numpy as jnp
from jax import lax
from jax.experimental import pallas as pl
from jax.experimental.pallas import tpu as pltpu
from jax.sharding import PartitionSpec as P

IMG_H = 14
IMG_W = 14
EPSILON = 1e-05
MESH = pl.DeviceIdType.MESH
F32 = jnp.float32
BF16 = jnp.bfloat16
HIGHEST = lax.Precision.HIGHEST
COLS = 16
GROUP = 8
NN = (((1,), (0,)), ((), ()))
NT = (((1,), (1,)), ((), ()))
TN = (((0,), (0,)), ((), ()))


def dot(lhs, rhs, dims=NN, precision=None):
    return lax.dot_general(lhs, rhs, dims, precision=precision, preferred_element_type=F32)


def sigmoid(values):
    return 0.5 * jnp.tanh(0.5 * values) + 0.5


def swish(values):
    return values * sigmoid(values)


def swish_slope(values):
    sigma = sigmoid(values)
    return sigma + values * sigma * (1.0 - sigma)


def tiled(row, times):
    return jnp.concatenate([row] * times, axis=1) if times > 1 else row


def colsum(values):
    return jnp.sum(values, axis=0, keepdims=True)


def put_rows(ref, at, row):
    for k in range(row.shape[1] // 128):
        piece = row[:, k * 128 : (k + 1) * 128]
        if len(ref.shape) == 3:
            ref[(at + k) // 2, (at + k) % 2 : (at + k) % 2 + 1, :] = piece
        else:
            ref[at + k : at + k + 1, :] = piece


def get_rows(ref, at, count):
    return jnp.concatenate([ref[at + k : at + k + 1, :] for k in range(count)], axis=1)


def per_slot(values, slots):
    return jnp.sum(values.reshape(slots, COLS, values.shape[1]), axis=1)


def main_kernel(n_batch, n_height, sizes, *refs):
    (
        counts, row_valid, *refs,
    ) = refs
    small_in, refs = refs[:9], refs[9:]
    (
        images, cotangent, w_reduce_in, w_split_in, w_squeeze_in, w_excite_in, w_expand_in,
        output, grad_images, big_e, big_a, big_b, big_c, big_r, big_q, vectors,
        gain_one, bias_one, gain_two, bias_two, gain_mid, bias_mid, bias_excite, gain_three, bias_three,
        img4, cot4, out4, w_reduce, w_split, w_squeeze, w_excite, w_expand,
        x, g, pix, to_pad, from_pad, c1, hs, c2, act, slope2, mixed, c3, d3, xo, gc3, gm, slope2n, gc2, gh, slope1, gc1,
        gc2_own, n1, d1, st_src, st_h, st_sum, st_low, st_b, wns, st_tot, x_t, mixed_t, hs_t, att, attx, gpx, pooled, sq_all, tot,
        m1, m2, m34, m5, m6, m78, m10, mx, mxb, p5, p6, em_src,
        s1, s2, s34, s5, s6, s78, s10, sx, sxb, em_all,
        first1, last1, up1, down1, first2, last2, up2, down2, first3, last3, up3, down3,
        local_sem, all_send, all_recv, pair_send, pair_recv, halo_send, halo_recv, red_send, red_recv,
        *bucket_refs,
    ) = refs
    slots, cols, rows, width = sizes
    narrow = w_reduce.shape[1]
    split = w_split.shape[1]
    half = split // 2
    cg = w_split.shape[0] // 9
    inner = w_squeeze.shape[1]
    block = slots * COLS
    pixels = rows * block
    total = n_batch * n_height
    area = float(IMG_H * IMG_W)
    b = lax.axis_index("batch")
    h = lax.axis_index("height")
    me = b * n_height + h

    sends = []
    due = {}

    def arrive(key):
        due.pop(key)()

    def move(key, src, dst):
        copy = pltpu.make_async_copy(src, dst, local_sem.at[key])
        copy.start()
        due["move", key] = copy.wait

    move(0, images, img4)
    move(1, w_reduce_in, w_reduce)
    barrier = pltpu.get_barrier_semaphore()

    def greet(j, carry):
        t = lax.rem(me + j, total)
        pl.semaphore_signal(
            barrier, inc=1, device_id=(t // n_height, lax.rem(t, n_height)), device_id_type=MESH
        )
        return carry

    lax.fori_loop(1, total, greet, 0)
    small = (gain_one, bias_one, gain_two, bias_two, gain_mid, bias_mid, bias_excite, gain_three, bias_three)
    for k, (src, dst) in enumerate(zip(small_in, small)):
        move(8 + k, src, dst)
    move(2, w_split_in, w_split)
    move(3, cotangent, cot4)
    move(4, w_squeeze_in, w_squeeze)
    move(5, w_excite_in, w_excite)
    move(6, w_expand_in, w_expand)


    kh, kq = lax.rem(h, 2), h // 2
    pair_one = (b, h + 1 - 2 * kh)
    pair_two = (b, h + 2 - 4 * kq)

    def circle(dst):
        if dst.shape[0] == total:
            return me, lambda t: (t // n_height, lax.rem(t, n_height))
        pairs = n_height // 2
        return b * pairs + kq, lambda t: (t // pairs, 2 * lax.rem(t, pairs) + kh)

    def send_all(src, dst, k):
        exchange(src, dst, k, *circle(dst))

    def exchange(src, dst, k, here, device):
        others = dst.shape[0]

        def one(j, carry):
            pltpu.make_async_remote_copy(
                src_ref=src, dst_ref=dst.at[here], send_sem=all_send.at[k], recv_sem=all_recv.at[k],
                device_id=device(lax.rem(here + j, others)), device_id_type=MESH,
            ).start()
            return carry

        lax.fori_loop(1, others, one, 0)
        dst[here] = src[...]
        sends.append(lambda: all_copy(dst, k).wait_send())
        due["all", k] = lambda: all_copy(dst, k).wait_recv()

    def all_copy(dst, k):
        many = dst.at[pl.ds(0, dst.shape[0] - 1)]
        return pltpu.make_async_remote_copy(
            src_ref=many, dst_ref=many,
            send_sem=all_send.at[k], recv_sem=all_recv.at[k], device_id=(b, h), device_id_type=MESH,
        )

    def send_pairs(src, arrived, dst, k):
        copy = pltpu.make_async_remote_copy(
            src_ref=src, dst_ref=arrived, send_sem=pair_send.at[k], recv_sem=pair_recv.at[k],
            device_id=pair_one, device_id_type=MESH,
        )
        copy.start()
        copy.wait()
        src[...] = src[...] + arrived[...]
        send_all(src, dst, k)

    def sum_all(dst, k):
        arrive(("all", k))

        def one(i, acc):
            return acc + jnp.sum(dst[pl.ds(i * 8, 8)], axis=0)

        acc = lax.fori_loop(0, dst.shape[0] // 8, one, jnp.zeros(dst.shape[1:], F32))
        if len(dst.shape) == 4:
            for i in range(dst.shape[1]):
                tot[2 * i : 2 * i + 2, :] = acc[i]
        else:
            tot[0 : dst.shape[1], :] = acc

    def halo_copies(first, last, up, down, k):
        above = pltpu.make_async_remote_copy(
            src_ref=last, dst_ref=up, send_sem=halo_send.at[2 * k], recv_sem=halo_recv.at[2 * k],
            device_id=(b, lax.rem(h + 1, n_height)), device_id_type=MESH,
        )
        below = pltpu.make_async_remote_copy(
            src_ref=first, dst_ref=down, send_sem=halo_send.at[2 * k + 1],
            recv_sem=halo_recv.at[2 * k + 1],
            device_id=(b, lax.rem(h + n_height - 1, n_height)), device_id_type=MESH,
        )
        return above, below

    def halo_start(first, last, up, down, k):
        above, below = halo_copies(first, last, up, down, k)

        @pl.when(h < n_height - 1)
        def _():
            above.start()

        @pl.when(h > 0)
        def _():
            below.start()

        sends.append(lambda: halo_sent(first, last, up, down, k))
        due["halo", k] = lambda: halo_here(first, last, up, down, k)

        @pl.when(h == 0)
        def _():
            up[...] = jnp.zeros(up.shape, up.dtype)

        @pl.when(h == n_height - 1)
        def _():
            down[...] = jnp.zeros(down.shape, down.dtype)

    def halo_here(first, last, up, down, k):
        above, below = halo_copies(first, last, up, down, k)

        @pl.when(h > 0)
        def _():
            above.wait_recv()

        @pl.when(h < n_height - 1)
        def _():
            below.wait_recv()

    def halo_sent(first, last, up, down, k):
        above, below = halo_copies(first, last, up, down, k)

        @pl.when(h < n_height - 1)
        def _():
            above.wait_send()

        @pl.when(h > 0)
        def _():
            below.wait_send()

    count = counts[0]
    filled = row_valid[0]
    for r in range(1, rows):
        filled = filled + row_valid[r]

    def flag(cond):
        return jnp.where(cond, 1.0, 0.0).astype(F32)

    def own(at):
        return flag((at >= 1) & (at <= filled))

    def ext(at):
        return flag(
            ((at >= 1) & (at <= filled))
            | ((at == 0) & (h > 0))
            | ((at == filled + 1) & (h < n_height - 1))
        )

    def mask(scale, lanes, start=0, size=block):
        return tiled(pix[start : start + size, :] * scale, lanes // 128)

    def block_at(at):
        return pl.ds(at * block if isinstance(at, int) else pl.multiple_of(at * block, block), block)

    def set_edges(src, first, last):
        first[...] = src[block_at(1), :].astype(first.dtype)
        value = jnp.zeros(last.shape, F32)
        for r in range(IMG_H // n_height - 1, rows):
            value = value + src[block_at(r + 1), :] * flag(filled == r + 1)
        last[...] = value.astype(last.dtype)

    def patch(ref, up, down):
        below = down[...].astype(F32)
        ref[block_at(0), :] = up[...].astype(F32)
        ref[block_at(rows + 1), :] = below
        whole = flag(filled == rows)
        ref[block_at(rows), :] = ref[block_at(rows), :] * whole + below * (1.0 - whole)

    iota = lax.broadcasted_iota(jnp.int32, (block, 128), 0)
    pix[...] = jnp.where(((iota >> 4) < count) & ((iota & 15) < cols), 1.0, 0.0)

    def places(shape, dim):
        at = lax.broadcasted_iota(jnp.int32, shape, dim)
        r, s, c = at // block, (at >> 4) & (slots - 1), at & 15
        return r, s, c, (s * cols + c) * rows + r

    def place_in():
        shape = (pixels, slots * cols * rows)
        r, s, c, at = places(shape, 0)
        live = (c < cols) & (s < count) & (r < filled)
        other = lax.broadcasted_iota(jnp.int32, shape, 1)
        to_pad[...] = jnp.where((other == at) & live, 1.0, 0.0).astype(BF16)

    def place_out():
        shape = (slots * cols * rows, pixels)
        r, s, c, at = places(shape, 1)
        other = lax.broadcasted_iota(jnp.int32, shape, 0)
        from_pad[...] = jnp.where((other == at) & (c < cols), 1.0, 0.0).astype(BF16)

    def pad_in(src, dst):
        value = src[...].reshape(slots * cols * rows, width)
        for q in range(rows):
            at = slice(q * block, (q + 1) * block)
            dst[at, :] = dot(to_pad[at, :], value).astype(BF16)

    def pad_out(src, dst):
        for j in range(width // 256):
            lanes = slice(j * 256, (j + 1) * 256)
            value = dot(from_pad[...], src[:, lanes]).astype(BF16)
            dst[:, :, lanes] = value.reshape(slots * cols, rows, 256)

    bx, bz = lax.rem(b, 2), lax.rem(b // 2, 4)
    group, n_groups = b // GROUP, n_batch // GROUP
    plane = 2 * kq + bx
    bucket_refs = iter(bucket_refs)

    def in_plane(t):
        return (b - bx + lax.rem(t, 2), 2 * (t // 2) + kh)

    def in_line(t):
        return (b + 2 * (t - bz), h)

    class Bucket:
        def __init__(self, at):
            self.full, self.in0, self.half, self.in1, self.sum1, self.in2, self.in3, self.shard, self.done = (
                next(bucket_refs) for _ in range(9)
            )
            self.kind = self.full.dtype
            self.tile = 8 if self.kind == F32 else 16
            self.sems = at * 8
            self.u0 = self.full.shape[0] // 2
            self.u1, self.u2 = self.u0 // 4, self.u0 // 16
            self.at0 = self.whole(kh * self.u0)
            self.at1 = self.whole(self.at0 + plane * self.u1)
            self.at2 = self.whole(self.at1 + bz * self.u2)
            self.final = lambda value: value

        def whole(self, at):
            return pl.multiple_of(at, self.tile)

        def cut(self, ref, at, size):
            return ref.at[pl.ds(self.whole(at), size)]

        def copy(self, stage, src, dst, device):
            k = self.sems + stage
            return pltpu.make_async_remote_copy(
                src_ref=src, dst_ref=dst, send_sem=red_send.at[k], recv_sem=red_recv.at[k],
                device_id=device, device_id_type=MESH,
            )

        def expect(self, stage, many):
            sends.append(lambda: self.copy(stage, many, many, (b, h)).wait_send())
            due["bucket", self.sems + stage] = lambda: self.copy(stage, many, many, (b, h)).wait_recv()

        def arrived(self, stage):
            arrive(("bucket", self.sems + stage))

        def s0(self):
            self.copy(0, self.cut(self.full, (1 - kh) * self.u0, self.u0), self.in0, pair_one).start()
            self.expect(0, self.in0)

        def s1(self):
            self.arrived(0)
            step = self.u1

            def one(i, carry):
                at = self.whole(i * step)
                mine = self.full[pl.ds(self.whole(self.at0 + at), step), :].astype(F32)
                self.half[pl.ds(at, step), :] = (mine + self.in0[pl.ds(at, step), :].astype(F32)).astype(self.kind)
                return carry

            lax.fori_loop(0, 4, one, 0)
            for j in range(1, 4):
                t = lax.rem(plane + j, 4)
                self.copy(1, self.cut(self.half, t * self.u1, self.u1), self.in1.at[j - 1], in_plane(t)).start()
            self.expect(1, self.in1)

        def s2(self):
            self.arrived(1)
            step = self.u2

            def one(i, carry):
                at = self.whole(i * step)
                value = self.half[pl.ds(self.whole(plane * self.u1 + at), step), :].astype(F32)
                for j in range(3):
                    value = value + self.in1[j, pl.ds(at, step), :].astype(F32)
                self.sum1[pl.ds(at, step), :] = value.astype(self.kind)
                return carry

            lax.fori_loop(0, 4, one, 0)
            for j in range(1, 4):
                t = lax.rem(bz + j, 4)
                self.copy(2, self.cut(self.sum1, t * self.u2, self.u2), self.in2.at[j - 1], in_line(t)).start()
            self.expect(2, self.in2)

        def collect(self):
            self.arrived(2)
            value = self.sum1[pl.ds(self.whole(bz * self.u2), self.u2), :].astype(F32)
            for j in range(3):
                value = value + self.in2[j].astype(F32)
            if n_groups > 1:
                self.shard[...] = value.astype(self.kind)

                def send_group(j, carry):
                    t = lax.rem(group + j, n_groups)
                    self.copy(3, self.shard, self.in3.at[group], (b + GROUP * (t - group), h)).start()
                    return carry

                lax.fori_loop(1, n_groups, send_group, 0)
                self.expect(3, self.in3.at[pl.ds(0, n_groups - 1)])
                self.in3[group] = self.shard[...]
                self.arrived(3)
                value = self.in3[0].astype(F32)
                for t in range(1, n_groups):
                    value = value + self.in3[t].astype(F32)
            return value

        def s3(self):
            self.done[pl.ds(self.at2, self.u2), :] = self.final(self.collect()).astype(self.kind)
            mine = self.done.at[pl.ds(self.at2, self.u2)]
            for j in range(1, 4):
                self.copy(4, mine, mine, in_line(lax.rem(bz + j, 4))).start()
            self.expect(4, self.done.at[pl.ds(0, 3 * self.u2)])

        def s4(self):
            self.arrived(4)
            mine = self.done.at[pl.ds(self.at1, self.u1)]
            for j in range(1, 4):
                self.copy(5, mine, mine, in_plane(lax.rem(plane + j, 4))).start()
            self.expect(5, self.done.at[pl.ds(0, 3 * self.u1)])

        def s5(self):
            self.arrived(5)
            mine = self.done.at[pl.ds(self.at0, self.u0)]
            self.copy(6, mine, mine, pair_one).start()
            self.expect(6, mine)

        def s6(self):
            self.arrived(6)

    buckets = [Bucket(k) for k in range(7)]
    bucket_e, bucket_r, bucket_n, bucket_q = buckets[:4]
    taps_buckets = buckets[4:]
    bucket_a, bucket_b, bucket_c = taps_buckets

    def put_taps(at, value):
        start = 0
        for bucket in taps_buckets:
            size = bucket.full.shape[0]
            low, high = max(at, start), min(at + value.shape[0], start + size)
            if low < high:
                bucket.full[low - start : high - start, :] = value[low - at : high - at].astype(BF16)
            start += size

    place_in()
    arrive(("move", 0))
    pad_in(img4, x)
    arrive(("move", 1))
    sum_one = jnp.zeros((1, narrow), F32)
    square_one = jnp.zeros((1, narrow), F32)
    for q in range(rows // 2):
        value = dot(x[pl.ds(q * 2 * block, 2 * block), :], w_reduce[...])
        c1[pl.ds((1 + 2 * q) * block, 2 * block), :] = value
        sum_one = sum_one + colsum(value)
        square_one = square_one + colsum(value * value)
    put_rows(m1, 0, sum_one)
    put_rows(m1, narrow // 128, square_one)
    put_rows(m1, 4, jnp.zeros((1, 256), F32) + count.astype(F32))
    pl.semaphore_wait(barrier, total - 1)
    send_all(m1, s1, 0)
    set_edges(c1, first1, last1)
    halo_start(first1, last1, up1, down1, 0)
    arrive(("move", 3))
    pad_in(cot4, g)
    for j in range(width // 256):
        put_rows(mx, 2 * j, colsum(x[:, j * 256 : (j + 1) * 256].astype(F32)))
    for k in range(9):
        arrive(("move", 8 + k))

    sum_all(s1, 0)
    slot_total = tot[4:5, :] / n_height
    pix_total = slot_total * area
    m_one = tiled(pix_total, narrow // 128)
    mean = get_rows(tot, 0, narrow // 128) / m_one
    inv_one = lax.rsqrt(get_rows(tot, 2, narrow // 128) / m_one - mean * mean + EPSILON)
    shift_one = mean * inv_one
    scale = inv_one * gain_one[...]
    offset = bias_one[...] - mean * scale
    scale_one, offset_one = scale, offset
    arrive(("halo", 0))
    patch(c1, up1, down1)

    def hide(at, carry):
        value = c1[block_at(at), :] * scale_one + offset_one
        value = swish(value) * mask(ext(at), narrow)
        hs[0, block_at(at), :] = pltpu.roll(value, 1, axis=0).astype(BF16)
        hs[1, block_at(at), :] = value.astype(BF16)
        hs[2, block_at(at), :] = pltpu.roll(value, block - 1, axis=0).astype(BF16)
        return carry

    lax.fori_loop(0, rows + 2, hide, 0)

    arrive(("move", 2))
    for q in range(rows // 2):
        for gr in range(2):
            lhs = jnp.concatenate(
                [
                    hs[bb, (a + 2 * q) * block : (a + 2 * q + 2) * block, gr * cg : (gr + 1) * cg]
                    for a in range(3)
                    for bb in range(3)
                ],
                axis=1,
            )
            c2[(1 + 2 * q) * block : (3 + 2 * q) * block, gr * half : (gr + 1) * half] = dot(
                lhs, w_split[:, gr * half : (gr + 1) * half]
            )
    m2[...] = jnp.zeros(m2.shape, F32)
    for j in range(2):
        lanes = pl.ds(j * half, half)

        def moments(r, carry):
            value = c2[block_at(r), lanes] * mask(own(r), half)
            return carry[0] + colsum(value), carry[1] + colsum(value * value)

        zero = jnp.zeros((1, half), F32)
        sums = lax.fori_loop(1, rows + 1, moments, (zero, zero))
        put_rows(m2, j * (half // 128), sums[0])
        put_rows(m2, split // 128 + j * (half // 128), sums[1])
    send_all(m2, s2, 1)
    set_edges(c2, first2, last2)
    halo_start(first2, last2, up2, down2, 1)
    exchange(mx, sx, 8, h, lambda t: (b, t))
    place_out()
    for bb in range(3):
        hs_t[bb] = hs[bb].T

    def slopes_one(r, carry):
        conv = c1[block_at(r + 1), :]
        live = mask(own(r + 1), narrow)
        slope1[block_at(r), :] = swish_slope(conv * scale_one + offset_one) * live
        n1[block_at(r), :] = ((conv * inv_one - shift_one) * live).astype(BF16)
        return carry

    lax.fori_loop(0, rows, slopes_one, 0)

    sum_all(s2, 1)
    m_two = tiled(pix_total, split // 128)
    mean = get_rows(tot, 0, split // 128) / m_two
    inv_two = lax.rsqrt(get_rows(tot, split // 128, split // 128) / m_two - mean * mean + EPSILON)
    shift_two = mean * inv_two
    scale_two = inv_two * gain_two[...]
    offset_two = bias_two[...] - mean * scale_two
    pool = jnp.zeros((slots, half), F32)
    for j in range(2):
        lanes = pl.ds(j * half, half)
        sc, of = scale_two[:, j * half : (j + 1) * half], offset_two[:, j * half : (j + 1) * half]

        def activate(r, acc):
            value = swish(c2[block_at(r), lanes] * sc + of) * mask(own(r), half)
            act[block_at(r - 1), lanes] = value
            return acc + value

        acc = lax.fori_loop(1, rows + 1, activate, jnp.zeros((block, half), F32))
        pool = pool + per_slot(acc, slots)
    pool = pool / area
    pooled[...] = pool
    arrive(("move", 4))
    m34[...] = dot(pool, w_squeeze[...], precision=HIGHEST)
    send_all(m34, s34, 2)
    arrive(("all", 8))
    mxb[...] = jnp.sum(sx[...], axis=0)
    exchange(mxb, sxb, 12, b, lambda t: (t, h))
    arrive(("move", 5))
    arrive(("all", 2))

    def gather(i, carry):
        value = jnp.sum(s34[pl.ds(i * n_height, n_height)], axis=0)
        sq_all[i] = value
        return carry[0] + colsum(value), carry[1] + colsum(value * value)

    zero = jnp.zeros((1, inner), F32)
    sum_mid, square_mid = lax.fori_loop(0, n_batch, gather, (zero, zero))
    mean_mid = sum_mid / slot_total
    inv_mid = lax.rsqrt(square_mid / slot_total - mean_mid * mean_mid + EPSILON)
    norm_mid = (sq_all[b] - mean_mid) * inv_mid
    pre_mid = norm_mid * gain_mid[...] + bias_mid[...]
    middle = swish(pre_mid)
    logits = dot(middle, w_excite[...], precision=HIGHEST) + bias_excite[...]
    top = jnp.maximum(logits[:, :half], logits[:, half:])
    expo_one = jnp.exp(logits[:, :half] - top)
    expo_two = jnp.exp(logits[:, half:] - top)
    att_one = expo_one / (expo_one + expo_two)
    att_two = expo_two / (expo_one + expo_two)
    att[:, 0:half] = att_one
    att[:, half:split] = att_two
    for s in range(slots):
        attx[s * COLS : (s + 1) * COLS, :] = jnp.broadcast_to(att[s : s + 1, :], (COLS, split))

    def mix(r, carry):
        at = block_at(r)
        mixed[at, :] = (
            attx[:, 0:half] * act[at, 0:half] + attx[:, half:split] * act[at, half:split]
        ).astype(BF16)
        return carry

    lax.fori_loop(0, rows, mix, 0)
    arrive(("move", 6))
    for j in range(width // 256):
        lanes = pl.ds(j * 256, 256)
        sums = jnp.zeros((1, 256), F32)
        squares = jnp.zeros((1, 256), F32)
        for q in range(rows // 2):
            at = pl.ds(q * 2 * block, 2 * block)
            value = dot(mixed[at, :], w_expand[:, lanes])
            c3[at, lanes] = value
            sums = sums + colsum(value)
            squares = squares + colsum(value * value)
        put_rows(m5, j * 2, sums)
        put_rows(m5, width // 128 + j * 2, squares)
    send_pairs(m5, p5, s5, 3)
    mixed_t[...] = mixed[...].T
    arrive(("halo", 1))
    patch(c2, up2, down2)
    for j in range(2):
        lanes = pl.ds(j * half, half)
        cut = slice(j * half, (j + 1) * half)
        sc, of = scale_two[:, cut], offset_two[:, cut]
        iv, sh = inv_two[:, cut], shift_two[:, cut]

        def slopes(at, carry):
            conv = c2[block_at(at), lanes]
            value = swish_slope(conv * sc + of) * mask(ext(at), half)
            slope2[block_at(at), lanes] = value
            value = value * own(at)
            more = value * (conv * iv - sh)
            slope2n[block_at(at), lanes] = more
            return carry[0] + value, carry[1] + more

        zero = jnp.zeros((block, half), F32)
        sums = lax.fori_loop(0, rows + 2, slopes, (zero, zero))
        st_src[0:slots, lanes] = per_slot(sums[0], slots)
        st_src[slots : 2 * slots, lanes] = per_slot(sums[1], slots)
    exchange(st_src, st_h, 10, h, lambda t: (b, t))

    sum_all(s5, 3)
    wide = width // 128
    m_three = tiled(pix_total, wide)
    mean = get_rows(tot, 0, wide) / m_three
    inv_three = lax.rsqrt(get_rows(tot, wide, wide) / m_three - mean * mean + EPSILON)
    shift_three = mean * inv_three
    scale_three = inv_three * gain_three[...]
    offset_three = bias_three[...] - mean * scale_three
    part = block // 2
    for j in range(width // 256):
        lanes = pl.ds(j * 256, 256)
        cut = slice(j * 256, (j + 1) * 256)
        sc, of = scale_three[:, cut], offset_three[:, cut]
        iv, sh = inv_three[:, cut], shift_three[:, cut]

        def finish_row(i, carry):
            r, k = i // 2, lax.rem(i, 2)
            at = pl.ds(pl.multiple_of(i * part, part), part)
            conv = c3[at, lanes]
            pre = conv * sc + of + x[at, lanes].astype(F32)
            sigma = sigmoid(pre)
            value = pre * sigma
            live = tiled(pix[pl.ds(pl.multiple_of(k * part, part), part), :] * own(r + 1), 2)
            xo[at, lanes] = (value * live).astype(BF16)
            slope = sigma + value * (1.0 - sigma)
            grad = g[at, lanes].astype(F32) * slope
            d3[at, lanes] = grad
            return carry[0] + colsum(grad), carry[1] + colsum(grad * (conv * iv - sh))

        zero = jnp.zeros((1, 256), F32)
        sums = lax.fori_loop(0, 2 * rows, finish_row, (zero, zero))
        put_rows(m6, j * 2, sums[0])
        put_rows(m6, wide + j * 2, sums[1])
    send_pairs(m6, p6, s6, 4)
    pad_out(xo, out4)
    move(7, out4, output)
    arrive(("all", 12))
    tot[0:8, :] = jnp.sum(sxb[...], axis=0)
    x_mean = get_rows(tot, 0, width // 128) / tiled(pix_total, width // 128)

    def centre(r, carry):
        value = (x[block_at(r), :].astype(F32) - x_mean) * mask(own(r + 1), width)
        x_t[:, block_at(r)] = value.T.astype(BF16)
        return carry

    lax.fori_loop(0, rows, centre, 0)
    for q in range(2):
        at = slice(q * (width // 2), (q + 1) * (width // 2))
        bucket_n.full[at, :] = dot(x_t[at, :], n1[...]).astype(BF16)
    bucket_n.s0()
    arrive(("all", 10))
    st_sum[...] = jnp.sum(st_h[...], axis=0)
    st_low[...] = st_sum[...].astype(BF16)
    exchange(st_low, st_b, 11, b, lambda t: (t, h))

    sum_all(s6, 4)
    gb_three = get_rows(tot, 0, wide)
    gg_three = get_rows(tot, wide, wide)
    vectors[0:1, :] = gb_three
    vectors[1:2, :] = gg_three
    gg = gg_three / m_three
    k_one = scale_three
    k_three = k_one * inv_three * gg
    k_two = k_one * (gb_three / m_three - shift_three * gg)
    for j in range(width // 256):
        lanes = pl.ds(j * 256, 256)
        cut = slice(j * 256, (j + 1) * 256)
        ka, kb, kc = k_one[:, cut], k_two[:, cut], k_three[:, cut]

        def back_three(i, carry):
            at = pl.ds(pl.multiple_of(i * part, part), part)
            gc3[at, lanes] = (d3[at, lanes] * ka - kb - c3[at, lanes] * kc).astype(BF16)
            return carry

        lax.fori_loop(0, 2 * rows, back_three, 0)
    for q in range(rows // 2):
        gm[pl.ds((1 + 2 * q) * block, 2 * block), :] = dot(
            gc3[pl.ds(2 * q * block, 2 * block), :], w_expand[...], NT
        )
    att_sums = [[], [], []]
    for j in range(2):
        lanes = pl.ds(j * half, half)
        parts = [[], [], []]
        for k in range(2):
            zero = jnp.zeros((part, half), F32)

            def attend(r, acc):
                at = pl.ds(pl.multiple_of(r * block + k * part, part), part)
                up_at = pl.ds(pl.multiple_of((r + 1) * block + k * part, part), part)
                value = gm[up_at, :]
                return (
                    acc[0] + value * act[at, lanes],
                    acc[1] + value * own(r + 1) * slope2[up_at, lanes],
                    acc[2] + value * slope2n[up_at, lanes],
                )

            acc = lax.fori_loop(0, rows, attend, (zero, zero, zero))
            for i in range(3):
                parts[i].append(per_slot(acc[i], slots // 2))
        for i in range(3):
            att_sums[i].append(jnp.concatenate(parts[i], axis=0))
    grad_att = att_sums[0]
    blend = att_one * grad_att[0] + att_two * grad_att[1]
    grad_logits = jnp.concatenate(
        [att_one * (grad_att[0] - blend), att_two * (grad_att[1] - blend)], axis=1
    )
    em_part = dot(grad_logits, w_excite[...], NT, HIGHEST) * swish_slope(pre_mid)
    em_src[...] = em_part
    exchange(em_src, em_all, 9, h, lambda t: (b, t))
    mid_scale = inv_mid * gain_mid[...] / area
    pooled_part = dot(em_part * mid_scale, w_squeeze[...], NT, HIGHEST)
    for j in range(2):
        lanes = pl.ds(j * half, half)
        weight = att_one if j == 0 else att_two
        for i in range(2):
            sums = weight * att_sums[1 + i][j] + pooled_part * st_sum[i * slots : (i + 1) * slots, lanes]
            put_rows(m78, (i * 2 + j) * (half // 128), colsum(sums))
    put_rows(m78, 2 * split // 128, colsum(em_part))
    put_rows(m78, 2 * split // 128 + 1, colsum(em_part * norm_mid))
    send_all(m78, s78, 5)
    set_edges(gm, first3, last3)
    halo_start(first3, last3, up3, down3, 2)
    for j in range(width // 256):
        bucket_e.full[j * narrow : (j + 1) * narrow, :] = dot(
            mixed_t[...], gc3[:, j * 256 : (j + 1) * 256]
        ).astype(BF16)
    bucket_e.s0()
    grad_excite = dot(middle, grad_logits, TN, HIGHEST)
    for gr in range(2):
        put_taps(18 * cg + gr * inner, grad_excite[:, gr * half : (gr + 1) * half])
    bias_part = colsum(grad_logits)
    put_rows(m10, 2 * (narrow // 128), bias_part)
    bucket_n.s1()
    arrive(("all", 11))
    every = n_batch * slots
    mid_all = ((sq_all[...] - mean_mid) * inv_mid).reshape(every, inner)
    st_all = st_b[...].astype(F32)
    w_turned = tiled(w_squeeze[...].T, 2)
    for i in range(2):
        sums = st_all[:, i * slots : (i + 1) * slots, :].reshape(every, split)
        wns[:, i * split : (i + 1) * split] = w_turned * dot(mid_all, sums, TN, HIGHEST)
        st_tot[i : i + 1, :] = colsum(sums)
    bucket_e.s1()

    sum_all(s78, 5)
    rows_mid = 2 * split // 128
    gb_mid, gg_mid = tot[rows_mid : rows_mid + 1, :], tot[rows_mid + 1 : rows_mid + 2, :]
    vectors[4:5, 0:128] = gb_mid
    vectors[4:5, 128:256] = gg_mid
    mid_k = mid_scale / slot_total
    pooled_all = dot(jnp.broadcast_to(mid_k * gb_mid, (8, inner)), w_squeeze[...], NT, HIGHEST)[0:1]
    turned = dot(jnp.broadcast_to(mid_k * gg_mid, (8, inner)), wns[...], precision=HIGHEST)[0:1]
    pooled_all = tiled(pooled_all, 2)
    gb_two = get_rows(tot, 0, split // 128) - pooled_all * st_tot[0:1, :] - turned[:, :split]
    gg_two = get_rows(tot, split // 128, split // 128) - pooled_all * st_tot[1:2, :] - turned[:, split:]
    vectors[2:3, 0:split] = gb_two
    vectors[2:3, split : 2 * split] = gg_two
    arrive(("all", 9))
    em = jnp.sum(em_all[...], axis=0)
    slot_live = jnp.where(lax.broadcasted_iota(jnp.int32, (slots, inner), 0) < count, 1.0, 0.0)
    grad_sq = (
        slot_live * inv_mid * gain_mid[...]
        * (em - gb_mid / slot_total - norm_mid * gg_mid / slot_total)
    )
    grad_pooled = dot(grad_sq, w_squeeze[...], NT, HIGHEST) / area
    att[:, 0:half] = grad_pooled
    for s in range(slots):
        gpx[s * COLS : (s + 1) * COLS, :] = jnp.broadcast_to(att[s : s + 1, 0:half], (COLS, half))
    arrive(("halo", 2))
    patch(gm, up3, down3)
    gg = gg_two / m_two
    k_one = scale_two
    k_three = k_one * inv_two * gg
    k_two = k_one * (gb_two / m_two - shift_two * gg)
    for j in range(2):
        lanes = pl.ds(j * half, half)
        cut = slice(j * half, (j + 1) * half)
        ka, kb, kc = k_one[:, cut], k_two[:, cut], k_three[:, cut]

        def back_two(at, carry):
            value = (attx[:, lanes] * gm[block_at(at), :] + gpx[...]) * slope2[block_at(at), lanes]
            value = value * ka - kb - c2[block_at(at), lanes] * kc
            gc2[block_at(at), lanes] = (value * mask(ext(at), half)).astype(BF16)
            return carry

        lax.fori_loop(0, rows + 2, back_two, 0)
    gc2_own[...] = (gc2[block_at(rows), :].astype(F32) * own(rows)).astype(BF16)

    def taps_grad(k):
        gr, bb = k // 3, k % 3
        lhs = jnp.concatenate(
            [hs_t[bb, gr * cg : (gr + 1) * cg, a * block : a * block + pixels] for a in range(3)], axis=0
        )
        lanes = slice(gr * half, (gr + 1) * half)
        rhs = jnp.concatenate([gc2[block:pixels, lanes], gc2_own[:, lanes]], axis=0)
        put_taps(k * 3 * cg, dot(lhs, rhs))

    begun = []
    for k in range(6):
        taps_grad(k)
        ready = 0
        for bucket in taps_buckets[:2]:
            ready += bucket.full.shape[0]
            if ready <= (k + 1) * 3 * cg and bucket not in begun:
                begun.append(bucket)
                bucket.s0()
    bucket_n.s2()
    for gr in range(2):
        outs = []
        for bb in range(3):
            lhs = jnp.concatenate(
                [gc2[(2 - a) * block : (2 - a) * block + pixels, gr * half : (gr + 1) * half] for a in range(3)],
                axis=1,
            )
            rhs = jnp.concatenate(
                [
                    w_split[(a * 3 + bb) * cg : (a * 3 + bb + 1) * cg, gr * half : (gr + 1) * half]
                    for a in range(3)
                ],
                axis=1,
            )
            outs.append(dot(lhs, rhs, NT))
        gh[:, gr * cg : (gr + 1) * cg] = (
            outs[1] + pltpu.roll(outs[2], 1, axis=0) + pltpu.roll(outs[0], pixels - 1, axis=0)
        )

    bucket_a.s1()
    bucket_b.s1()
    bucket_e.s2()

    def back_hidden(r, carry):
        value = gh[block_at(r), :] * slope1[block_at(r), :]
        gh[block_at(r), :] = value
        d1[block_at(r), :] = value.astype(BF16)
        norm = c1[block_at(r + 1), :] * inv_one - shift_one
        return carry[0] + colsum(value), carry[1] + colsum(value * norm)

    zero = jnp.zeros((1, narrow), F32)
    sums = lax.fori_loop(0, rows, back_hidden, (zero, zero))
    put_rows(m10, 0, sums[0])
    put_rows(m10, narrow // 128, sums[1])
    send_all(m10, s10, 7)
    for q in range(2):
        at = slice(q * (width // 2), (q + 1) * (width // 2))
        bucket_r.full[at, :] = dot(x_t[at, :], d1[...]).astype(BF16)
    bucket_r.s0()
    bucket_c.s0()
    bucket_q.full[...] = dot(pooled[...], grad_sq, TN, HIGHEST)
    bucket_q.s0()
    bucket_r.s1()
    bucket_a.s2()
    bucket_e.s3()
    bucket_c.s1()
    bucket_q.s1()
    bucket_b.s2()
    kept_n = bucket_n.collect()
    sum_all(s10, 7)
    gb_one = get_rows(tot, 0, narrow // 128)
    gg_one = get_rows(tot, narrow // 128, narrow // 128)
    vectors[3:4, 0:narrow] = gb_one
    vectors[3:4, narrow : 2 * narrow] = gg_one
    vectors[3:4, 2 * narrow : 2 * narrow + split] = get_rows(tot, 2 * (narrow // 128), split // 128)
    gg = gg_one / m_one
    k_one = scale_one
    k_three = k_one * inv_one * gg
    k_two = k_one * (gb_one / m_one - shift_one * gg)

    def back_one(r, carry):
        value = gh[block_at(r), :] * k_one - k_two - c1[block_at(r + 1), :] * k_three
        gc1[block_at(r), :] = (value * mask(own(r + 1), narrow)).astype(BF16)
        return carry

    lax.fori_loop(0, rows, back_one, 0)
    bucket_r.final = lambda value: scale_one * (value - kept_n * gg)
    arrive(("move", 7))

    def back_image(r, carry):
        value = d3[block_at(r), :] + dot(gc1[block_at(r), :], w_reduce[...], NT)
        xo[block_at(r), :] = value.astype(BF16)
        return carry

    lax.fori_loop(0, rows, back_image, 0)
    bucket_a.s3()
    bucket_r.s2()
    bucket_e.s4()
    bucket_c.s2()
    bucket_q.s2()
    pad_out(xo, out4)
    move(7, out4, grad_images)
    bucket_b.s3()
    bucket_a.s4()
    bucket_r.s3()
    bucket_c.s3()
    bucket_q.s3()
    bucket_e.s5()
    bucket_b.s4()
    bucket_e.s6()
    move(0, bucket_e.done, big_e)
    bucket_a.s5()
    bucket_r.s4()
    bucket_c.s4()
    bucket_q.s4()
    bucket_a.s6()
    move(1, bucket_a.done, big_a)
    bucket_b.s5()
    bucket_q.s5()
    bucket_b.s6()
    move(4, bucket_b.done, big_b)
    bucket_r.s5()
    bucket_c.s5()
    bucket_q.s6()
    move(3, bucket_q.done, big_q)
    bucket_r.s6()
    move(2, bucket_r.done, big_r)
    bucket_c.s6()
    move(5, bucket_c.done, big_c)

    for wait in sends:
        wait()
    for key in list(due):
        arrive(key)


def unpack_kernel(
    out_a, gimg_a, big_e, big_a, big_b, big_c, big_r, big_q, vectors,
    output, grad_images, grad_reduce, grad_split, grad_squeeze, grad_excite, grad_expand,
    grad_gain_one, grad_bias_one, grad_gain_two, grad_bias_two,
    grad_gain_mid, grad_bias_mid, grad_bias_excite, grad_gain_three, grad_bias_three,
    in_e, in_a, in_b, in_c, in_r, in_v, in_o, in_g, in_q, out_e, out_s, out_x, out_r, sems,
):
    def move(k, src, dst):
        copy = pltpu.make_async_copy(src, dst, sems.at[k])
        copy.start()
        return copy

    ins = [move(k, src, dst) for k, (src, dst) in enumerate([
        (out_a, in_o), (big_e, in_e), (gimg_a, in_g), (big_r, in_r), (big_a, in_a), (big_b, in_b), (big_c, in_c),
        (big_q, in_q), (vectors, in_v),
    ])]
    outs = []
    narrow = grad_expand.shape[0]
    taps, split = grad_split.shape
    half = split // 2
    inner = grad_excite.shape[0]
    ins[0].wait()
    outs.append(move(9, in_o, output))
    ins[1].wait()
    for j in range(grad_expand.shape[1] // 256):
        out_e[:, j * 256 : (j + 1) * 256] = in_e[j * narrow : (j + 1) * narrow, :].astype(F32)
    outs.append(move(10, out_e, grad_expand))
    ins[2].wait()
    outs.append(move(11, in_g, grad_images))
    ins[3].wait()
    out_r[...] = in_r[...].astype(F32)
    outs.append(move(12, out_r, grad_reduce))
    for k in range(4, 7):
        ins[k].wait()

    def put(at, dst, to, lanes, size):
        start = 0
        for ref in (in_a, in_b, in_c):
            low, high = max(at, start), min(at + size, start + ref.shape[0])
            if low < high:
                dst[to + low - at : to + high - at, lanes] = ref[low - start : high - start, :].astype(F32)
            start += ref.shape[0]

    cg = taps // 9
    for k in range(18):
        gr, bb, a = k // 9, k // 3 % 3, k % 3
        put(k * cg, out_s, (a * 3 + bb) * cg, slice(gr * half, (gr + 1) * half), cg)
    outs.append(move(13, out_s, grad_split))
    for gr in range(2):
        put(18 * cg + gr * inner, out_x, 0, slice(gr * half, (gr + 1) * half), inner)
    outs.append(move(14, out_x, grad_excite))
    ins[7].wait()
    outs.append(move(15, in_q, grad_squeeze))
    ins[8].wait()
    grad_bias_three[...] = in_v[0:1, :]
    grad_gain_three[...] = in_v[1:2, :]
    grad_bias_two[...] = in_v[2:3, 0:split]
    grad_gain_two[...] = in_v[2:3, split : 2 * split]
    grad_bias_one[...] = in_v[3:4, 0:narrow]
    grad_gain_one[...] = in_v[3:4, narrow : 2 * narrow]
    grad_bias_excite[...] = in_v[3:4, 2 * narrow : 2 * narrow + split]
    grad_bias_mid[...] = in_v[4:5, 0:inner]
    grad_gain_mid[...] = in_v[4:5, inner : 2 * inner]
    for copy in outs:
        copy.wait()


def shards(
    n_batch, n_height,
    images, counts, row_valid, w_reduce, gain_one, bias_one, w_split, gain_two, bias_two, w_squeeze,
    gain_mid, bias_mid, w_excite, bias_excite, w_expand, gain_three, bias_three, cotangent,
):
    slots, rows, cols, width = images.shape
    count = slots * rows * cols
    narrow = w_reduce.shape[1]
    split = w_split.shape[3]
    taps = 9 * w_split.shape[2]
    inner = w_squeeze.shape[1]
    half = split // 2
    total = n_batch * n_height
    block = slots * COLS
    pixels = rows * block
    padded = pixels + 2 * block
    n_groups = n_batch // GROUP

    def row(v):
        return v.reshape(1, -1)

    unit = 4 * GROUP * 16
    size_e = width // 256 * narrow
    size_r = width
    taps_rows = 2 * taps + 2 * inner
    size_a = -(-taps_rows // (5 * unit)) * 2 * unit
    size_c = taps_rows - 2 * size_a

    def bucket(size, lanes=256, kind=BF16):
        kept = size // 2
        shapes = [
            (size, lanes), (kept, lanes), (kept, lanes), (3, kept // 4, lanes), (kept // 4, lanes),
            (3, kept // 16, lanes), (n_groups, kept // 16, lanes), (kept // 16, lanes), (size, lanes),
        ]
        return [pltpu.VMEM(dims, kind) for dims in shapes]

    messages = [(3, 2, 128), (8, 128), (8, 128), (16, 128), (16, 128), (5, 2, 128), (8, 128), (8, 128), (8, 128)]
    vm = pltpu.VMEM
    scratch = (
        [vm((1, k), F32) for k in (narrow, narrow, split, split, inner, inner, split, width, width)]
        + [vm((slots * cols, rows, width), BF16)] * 3
        + [vm((width, narrow), BF16), vm((taps, split), BF16), vm((narrow, inner), F32), vm((inner, split), F32),
           vm((narrow, width), BF16)]
        + [vm((pixels, width), BF16), vm((pixels, width), BF16), vm((block, 128), F32), vm((pixels, count), BF16),
           vm((count, pixels), BF16)]
        + [vm((padded, narrow), F32), vm((3, padded, narrow), BF16), vm((padded, split), F32), vm((pixels, split), F32),
           vm((padded, split), F32), vm((pixels, half), BF16), vm((pixels, width), F32), vm((pixels, width), F32),
           vm((pixels, width), BF16), vm((pixels, width), BF16), vm((padded, half), F32),
           vm((padded, split), F32), vm((padded, split), BF16), vm((pixels, narrow), F32), vm((pixels, narrow), F32),
           vm((pixels, narrow), BF16), vm((block, split), BF16), vm((pixels, narrow), BF16), vm((pixels, narrow), BF16)]
        + [vm((2 * slots, split), F32), vm((n_height, 2 * slots, split), F32), vm((2 * slots, split), F32),
           vm((2 * slots, split), BF16), vm((n_batch, 2 * slots, split), BF16), vm((inner, 2 * split), F32),
           vm((8, split), F32)]
        + [vm((width, pixels), BF16), vm((half, pixels), BF16), vm((3, narrow, padded), BF16), vm((slots, split), F32),
           vm((block, split), F32), vm((block, half), F32), vm((slots, half), F32), vm((n_batch, slots, inner), F32),
           vm((16, 128), F32)]
        + [vm(dims, F32) for dims in messages] + [vm((16, 128), F32)] * 2 + [vm((slots, inner), F32)]
        + [vm((total // 2 if dims[0] == 16 else total,) + dims, F32) for dims in messages[:-2]]
        + [vm((n_height,) + messages[-1], F32), vm((n_batch,) + messages[-1], F32)] + [vm((n_height, slots, inner), F32)]
        + [vm((block, narrow), F32)] * 4 + [vm((block, split), BF16)] * 4 + [vm((block, half), BF16)] * 4
        + [pltpu.SemaphoreType.DMA((k,)) for k in (17, 13, 13, 8, 8, 6, 6, 56, 56)]
        + bucket(size_e) + bucket(size_r) * 2 + bucket(narrow, inner, F32) + bucket(size_a) * 2 + bucket(size_c)
    )
    smem = pl.BlockSpec(memory_space=pltpu.SMEM)
    vmem = pl.BlockSpec(memory_space=pltpu.VMEM)
    hbm = pl.BlockSpec(memory_space=pltpu.HBM)
    shape = jax.ShapeDtypeStruct
    flat = (slots * cols, rows, width)

    def by_column(value):
        return value.transpose(0, 2, 1, 3).reshape(flat)

    def by_row(value):
        return value.reshape(slots, cols, rows, width).transpose(0, 2, 1, 3)

    out_a, gimg_a, big_e, big_a, big_b, big_c, big_r, big_q, vectors = pl.pallas_call(
        functools.partial(main_kernel, n_batch, n_height, (slots, cols, rows, width)),
        out_shape=(
            shape(flat, BF16), shape(flat, BF16), shape((size_e, 256), BF16),
            shape((size_a, 256), BF16), shape((size_a, 256), BF16), shape((size_c, 256), BF16), shape((size_r, 256), BF16),
            shape((narrow, inner), F32),
            shape((8, width), F32),
        ),
        in_specs=[smem, smem] + [hbm] * 16,
        out_specs=[hbm] * 8 + [vmem],
        scratch_shapes=scratch,
        compiler_params=pltpu.CompilerParams(
            collective_id=0, has_side_effects=True, vmem_limit_bytes=58 * 1024 * 1024
        ),
    )(
        counts, row_valid, row(gain_one), row(bias_one), row(gain_two), row(bias_two), row(gain_mid), row(bias_mid),
        row(bias_excite), row(gain_three), row(bias_three),
        by_column(images), by_column(cotangent), w_reduce, w_split.reshape(taps, split), w_squeeze, w_excite, w_expand,
    )
    (
        output, grad_images, grad_reduce, grad_split, grad_squeeze, grad_excite, grad_expand,
        grad_gain_one, grad_bias_one, grad_gain_two, grad_bias_two,
        grad_gain_mid, grad_bias_mid, grad_bias_excite, grad_gain_three, grad_bias_three,
    ) = pl.pallas_call(
        unpack_kernel,
        out_shape=(
            shape(flat, BF16), shape(flat, BF16), shape((width, narrow), F32), shape((taps, split), F32),
            shape((narrow, inner), F32), shape((inner, split), F32), shape((narrow, width), F32),
            shape((1, narrow), F32), shape((1, narrow), F32), shape((1, split), F32), shape((1, split), F32),
            shape((1, inner), F32), shape((1, inner), F32), shape((1, split), F32), shape((1, width), F32),
            shape((1, width), F32),
        ),
        in_specs=[hbm] * 9,
        out_specs=[hbm] * 7 + [vmem] * 9,
        scratch_shapes=[
            vm((size_e, 256), BF16), vm((size_a, 256), BF16), vm((size_a, 256), BF16), vm((size_c, 256), BF16), vm((size_r, 256), BF16),
            vm((8, width), F32),
            vm(flat, BF16), vm(flat, BF16), vm((narrow, inner), F32),
            vm((narrow, width), F32), vm((taps, split), F32), vm((inner, split), F32), vm((width, narrow), F32),
            pltpu.SemaphoreType.DMA((16,)),
        ],
        compiler_params=pltpu.CompilerParams(vmem_limit_bytes=60 * 1024 * 1024),
    )(out_a, gimg_a, big_e, big_a, big_b, big_c, big_r, big_q, vectors)

    def like(value, other):
        return value.reshape(other.shape)

    return (
        by_row(output), by_row(grad_images), grad_reduce, like(grad_gain_one, gain_one), like(grad_bias_one, bias_one),
        like(grad_split, w_split), like(grad_gain_two, gain_two), like(grad_bias_two, bias_two), grad_squeeze,
        like(grad_gain_mid, gain_mid), like(grad_bias_mid, bias_mid), grad_excite, like(grad_bias_excite, bias_excite),
        grad_expand, like(grad_gain_three, gain_three), like(grad_bias_three, bias_three),
    )


def solution(mesh):
    axes = mesh.shape
    split_in = P("batch", "height", None, None)
    return jax.shard_map(
        functools.partial(shards, axes["batch"], axes["height"]),
        mesh=mesh,
        in_specs=(split_in, P("batch"), P("height")) + (P(),) * 14 + (split_in,),
        out_specs=(split_in, split_in) + (P(),) * 14,
        check_vma=False,
    )
```

time: 101 us -> 95.8 us (0.949)
  Pallas kernels: 99.3 us -> 94.1 us
    pallas_call x1, Pallas kernels: 94.5 us -> 89.4 us  [shards(): pl.pallas_call(functools.partial(main_kernel, n_batch, n_height, (slots,...]
where the time goes in v3:
time: 95.8 us; the launch traced here: 95.6 us
  Pallas kernels  94.1 us (98%)
  between operations  1.47 us (2%)
    pallas_call x1, Pallas kernels, shards(): pl.pallas_call(functools.partial(main_kernel, n_batch, n_height, (slots,...  89.4 us
    pallas_call x1, Pallas kernels, shards(): pl.pallas_call(unpack_kernel, out_shape=(shape(flat, BF16), shape(flat, B...  4.76 us

profile of v3, /device:TPU:1, one launch (start us, length us, event | category | flops | bytes accessed | tf_op | source)
XLA Modules:
  0.0 95.6 jit_solution(16162895875460806188)
XLA Ops:
  1.3 89.4 %shard_map.297 = (bf16[112,4,1024]{2,1,0:T(4,128)(2,1)}, bf16[112,4,1024]{2,1,0:T(4,128)(2,1)}, bf16[1024,256]{1,0:T(8,128)(2,1)}, bf16[1024,256]{1,0:T(8,128)(2...) custom-call(s32[1]{0:T(128)S(6)} %copy.34.refs_0_, ...), custom_call_target="tpu_custom_call" | custom-call | tf_op jit(solution)/shard_map/pallas_call | solution.py:1114
  90.7 4.8 %shard_map.298 = (bf16[112,4,1024]{2,1,0:T(4,128)(2,1)}, bf16[112,4,1024]{2,1,0:T(4,128)(2,1)}, f32[1024,256]{1,0:T(8,128)}, f32[1152,512]{1,0:T(8,128)}, f32[25...) custom-call(bf16[112,4,1024]{2,1,0:T(4,128)(2,1)} %get-tuple-element, ...), custom_call_target="tpu_custom_call" | custom-call | tf_op jit(solution)/shard_map/pallas_call | solution.py:1137

commit v4 on v3

--- a/solution.py
+++ b/solution.py
@@ -65,20 +65,20 @@
 
 def main_kernel(n_batch, n_height, sizes, *refs):
     (
-        counts, row_valid, *refs,
+        counts_in, row_valid_in, *refs,
     ) = refs
     small_in, refs = refs[:9], refs[9:]
     (
         images, cotangent, w_reduce_in, w_split_in, w_squeeze_in, w_excite_in, w_expand_in,
-        output, grad_images, big_e, big_a, big_b, big_c, big_r, big_q, vectors,
+        output, grad_images, big_e, big_a, big_b, big_c, big_r, big_q, vectors_out,
         gain_one, bias_one, gain_two, bias_two, gain_mid, bias_mid, bias_excite, gain_three, bias_three,
         img4, cot4, out4, w_reduce, w_split, w_squeeze, w_excite, w_expand,
         x, g, pix, to_pad, from_pad, c1, hs, c2, act, slope2, mixed, c3, d3, xo, gc3, gm, slope2n, gc2, gh, slope1, gc1,
         gc2_own, n1, d1, st_src, st_h, st_sum, st_low, st_b, wns, st_tot, x_t, mixed_t, hs_t, att, attx, gpx, pooled, sq_all, tot,
-        m1, m2, m34, m5, m6, m78, m10, mx, mxb, p5, p6, em_src,
+        m1, m2, m34, m5, m6, m78, m10, mx, mxb, p5, p6, vectors, pool_h, pool_sum, pool_b, em_sum, em_b, squeeze_grad, em_src,
         s1, s2, s34, s5, s6, s78, s10, sx, sxb, em_all,
         first1, last1, up1, down1, first2, last2, up2, down2, first3, last3, up3, down3,
-        local_sem, all_send, all_recv, pair_send, pair_recv, halo_send, halo_recv, red_send, red_recv,
+        counts, row_valid, local_sem, all_send, all_recv, pair_send, pair_recv, halo_send, halo_recv, red_send, red_recv,
         *bucket_refs,
     ) = refs
     slots, cols, rows, width = sizes
@@ -106,6 +106,8 @@
         copy.start()
         due["move", key] = copy.wait
 
+    move(17, counts_in, counts)
+    move(18, row_valid_in, row_valid)
     move(0, images, img4)
     move(1, w_reduce_in, w_reduce)
     barrier = pltpu.get_barrier_semaphore()
@@ -145,13 +147,18 @@
         others = dst.shape[0]
 
         def one(j, carry):
-            pltpu.make_async_remote_copy(
-                src_ref=src, dst_ref=dst.at[here], send_sem=all_send.at[k], recv_sem=all_recv.at[k],
-                device_id=device(lax.rem(here + j, others)), device_id_type=MESH,
-            ).start()
+            t = jnp.where(2 * here < others, others - 1 - j, j)
+
+            @pl.when(t != here)
+            def _():
+                pltpu.make_async_remote_copy(
+                    src_ref=src, dst_ref=dst.at[here], send_sem=all_send.at[k], recv_sem=all_recv.at[k],
+                    device_id=device(t), device_id_type=MESH,
+                ).start()
+
             return carry
 
-        lax.fori_loop(1, others, one, 0)
+        lax.fori_loop(0, others, one, 0)
         dst[here] = src[...]
         sends.append(lambda: all_copy(dst, k).wait_send())
         due["all", k] = lambda: all_copy(dst, k).wait_recv()
@@ -177,7 +184,7 @@
         arrive(("all", k))
 
         def one(i, acc):
-            return acc + jnp.sum(dst[pl.ds(i * 8, 8)], axis=0)
+            return acc + jnp.sum(dst[pl.ds(i * 8, 8)].astype(F32), axis=0)
 
         acc = lax.fori_loop(0, dst.shape[0] // 8, one, jnp.zeros(dst.shape[1:], F32))
         if len(dst.shape) == 4:
@@ -242,6 +249,8 @@
         def _():
             below.wait_send()
 
+    arrive(("move", 17))
+    arrive(("move", 18))
     count = counts[0]
     filled = row_valid[0]
     for r in range(1, rows):
@@ -442,9 +451,9 @@
         def s6(self):
             self.arrived(6)
 
-    buckets = [Bucket(k) for k in range(7)]
-    bucket_e, bucket_r, bucket_n, bucket_q = buckets[:4]
-    taps_buckets = buckets[4:]
+    buckets = [Bucket(k) for k in range(6)]
+    bucket_e, bucket_r, bucket_n = buckets[:3]
+    taps_buckets = buckets[3:]
     bucket_a, bucket_b, bucket_c = taps_buckets
 
     def put_taps(at, value):
@@ -478,6 +487,7 @@
     pad_in(cot4, g)
     for j in range(width // 256):
         put_rows(mx, 2 * j, colsum(x[:, j * 256 : (j + 1) * 256].astype(F32)))
+    exchange(mx, sx, 8, h, lambda t: (b, t))
     for k in range(9):
         arrive(("move", 8 + k))
 
@@ -533,7 +543,9 @@
     send_all(m2, s2, 1)
     set_edges(c2, first2, last2)
     halo_start(first2, last2, up2, down2, 1)
-    exchange(mx, sx, 8, h, lambda t: (b, t))
+    arrive(("all", 8))
+    mxb[...] = jnp.sum(sx[...], axis=0)
+    exchange(mxb, sxb, 12, b, lambda t: (t, h))
     place_out()
     for bb in range(3):
         hs_t[bb] = hs[bb].T
@@ -571,9 +583,21 @@
     arrive(("move", 4))
     m34[...] = dot(pool, w_squeeze[...], precision=HIGHEST)
     send_all(m34, s34, 2)
-    arrive(("all", 8))
-    mxb[...] = jnp.sum(sx[...], axis=0)
-    exchange(mxb, sxb, 12, b, lambda t: (t, h))
+    exchange(pooled, pool_h, 13, h, lambda t: (b, t))
+    arrive(("all", 12))
+    tot[0:8, :] = jnp.sum(sxb[...], axis=0)
+    x_mean = get_rows(tot, 0, width // 128) / tiled(pix_total, width // 128)
+
+    def centre(r, carry):
+        value = (x[block_at(r), :].astype(F32) - x_mean) * mask(own(r + 1), width)
+        x_t[:, block_at(r)] = value.T.astype(BF16)
+        return carry
+
+    lax.fori_loop(0, rows, centre, 0)
+    for q in range(2):
+        at = slice(q * (width // 2), (q + 1) * (width // 2))
+        bucket_n.full[at, :] = dot(x_t[at, :], n1[...]).astype(BF16)
+    bucket_n.s0()
     arrive(("move", 5))
     arrive(("all", 2))
 
@@ -623,6 +647,10 @@
         put_rows(m5, width // 128 + j * 2, squares)
     send_pairs(m5, p5, s5, 3)
     mixed_t[...] = mixed[...].T
+    bucket_n.s1()
+    arrive(("all", 13))
+    pool_sum[...] = jnp.sum(pool_h[...], axis=0)
+    exchange(pool_sum, pool_b, 14, b, lambda t: (t, h))
     arrive(("halo", 1))
     patch(c2, up2, down2)
     for j in range(2):
@@ -677,25 +705,13 @@
 
         zero = jnp.zeros((1, 256), F32)
         sums = lax.fori_loop(0, 2 * rows, finish_row, (zero, zero))
-        put_rows(m6, j * 2, sums[0])
-        put_rows(m6, wide + j * 2, sums[1])
-    send_pairs(m6, p6, s6, 4)
+        put_rows(p6, j * 2, sums[0])
+        put_rows(p6, wide + j * 2, sums[1])
+    m6[...] = p6[...].astype(BF16)
+    send_all(m6, s6, 4)
     pad_out(xo, out4)
     move(7, out4, output)
-    arrive(("all", 12))
-    tot[0:8, :] = jnp.sum(sxb[...], axis=0)
-    x_mean = get_rows(tot, 0, width // 128) / tiled(pix_total, width // 128)
-
-    def centre(r, carry):
-        value = (x[block_at(r), :].astype(F32) - x_mean) * mask(own(r + 1), width)
-        x_t[:, block_at(r)] = value.T.astype(BF16)
-        return carry
-
-    lax.fori_loop(0, rows, centre, 0)
-    for q in range(2):
-        at = slice(q * (width // 2), (q + 1) * (width // 2))
-        bucket_n.full[at, :] = dot(x_t[at, :], n1[...]).astype(BF16)
-    bucket_n.s0()
+    bucket_n.s2()
     arrive(("all", 10))
     st_sum[...] = jnp.sum(st_h[...], axis=0)
     st_low[...] = st_sum[...].astype(BF16)
@@ -754,7 +770,6 @@
     )
     em_part = dot(grad_logits, w_excite[...], NT, HIGHEST) * swish_slope(pre_mid)
     em_src[...] = em_part
-    exchange(em_src, em_all, 9, h, lambda t: (b, t))
     mid_scale = inv_mid * gain_mid[...] / area
     pooled_part = dot(em_part * mid_scale, w_squeeze[...], NT, HIGHEST)
     for j in range(2):
@@ -766,6 +781,7 @@
     put_rows(m78, 2 * split // 128, colsum(em_part))
     put_rows(m78, 2 * split // 128 + 1, colsum(em_part * norm_mid))
     send_all(m78, s78, 5)
+    exchange(em_src, em_all, 9, h, lambda t: (b, t))
     set_edges(gm, first3, last3)
     halo_start(first3, last3, up3, down3, 2)
     for j in range(width // 256):
@@ -778,7 +794,7 @@
         put_taps(18 * cg + gr * inner, grad_excite[:, gr * half : (gr + 1) * half])
     bias_part = colsum(grad_logits)
     put_rows(m10, 2 * (narrow // 128), bias_part)
-    bucket_n.s1()
+    bucket_e.s1()
     arrive(("all", 11))
     every = n_batch * slots
     mid_all = ((sq_all[...] - mean_mid) * inv_mid).reshape(every, inner)
@@ -788,7 +804,6 @@
         sums = st_all[:, i * slots : (i + 1) * slots, :].reshape(every, split)
         wns[:, i * split : (i + 1) * split] = w_turned * dot(mid_all, sums, TN, HIGHEST)
         st_tot[i : i + 1, :] = colsum(sums)
-    bucket_e.s1()
 
     sum_all(s78, 5)
     rows_mid = 2 * split // 128
@@ -805,6 +820,7 @@
     vectors[2:3, split : 2 * split] = gg_two
     arrive(("all", 9))
     em = jnp.sum(em_all[...], axis=0)
+    em_sum[...] = em
     slot_live = jnp.where(lax.broadcasted_iota(jnp.int32, (slots, inner), 0) < count, 1.0, 0.0)
     grad_sq = (
         slot_live * inv_mid * gain_mid[...]
@@ -852,7 +868,8 @@
             if ready <= (k + 1) * 3 * cg and bucket not in begun:
                 begun.append(bucket)
                 bucket.s0()
-    bucket_n.s2()
+    bucket_e.s2()
+    exchange(em_sum, em_b, 15, b, lambda t: (t, h))
     for gr in range(2):
         outs = []
         for bb in range(3):
@@ -874,7 +891,6 @@
 
     bucket_a.s1()
     bucket_b.s1()
-    bucket_e.s2()
 
     def back_hidden(r, carry):
         value = gh[block_at(r), :] * slope1[block_at(r), :]
@@ -893,13 +909,10 @@
         bucket_r.full[at, :] = dot(x_t[at, :], d1[...]).astype(BF16)
     bucket_r.s0()
     bucket_c.s0()
-    bucket_q.full[...] = dot(pooled[...], grad_sq, TN, HIGHEST)
-    bucket_q.s0()
     bucket_r.s1()
     bucket_a.s2()
     bucket_e.s3()
     bucket_c.s1()
-    bucket_q.s1()
     bucket_b.s2()
     kept_n = bucket_n.collect()
     sum_all(s10, 7)
@@ -908,6 +921,7 @@
     vectors[3:4, 0:narrow] = gb_one
     vectors[3:4, narrow : 2 * narrow] = gg_one
     vectors[3:4, 2 * narrow : 2 * narrow + split] = get_rows(tot, 2 * (narrow // 128), split // 128)
+    move(6, vectors, vectors_out)
     gg = gg_one / m_one
     k_one = scale_one
     k_three = k_one * inv_one * gg
@@ -920,6 +934,13 @@
 
     lax.fori_loop(0, rows, back_one, 0)
     bucket_r.final = lambda value: scale_one * (value - kept_n * gg)
+    arrive(("all", 14))
+    arrive(("all", 15))
+    sq_grads = (inv_mid * gain_mid[...]) * (
+        em_b[...].reshape(every, inner) - gb_mid / slot_total - mid_all * gg_mid / slot_total
+    )
+    squeeze_grad[...] = dot(pool_b[...].reshape(every, half), sq_grads, TN, HIGHEST)
+    move(3, squeeze_grad, big_q)
     arrive(("move", 7))
 
     def back_image(r, carry):
@@ -932,14 +953,12 @@
     bucket_r.s2()
     bucket_e.s4()
     bucket_c.s2()
-    bucket_q.s2()
     pad_out(xo, out4)
     move(7, out4, grad_images)
     bucket_b.s3()
     bucket_a.s4()
     bucket_r.s3()
     bucket_c.s3()
-    bucket_q.s3()
     bucket_e.s5()
     bucket_b.s4()
     bucket_e.s6()
@@ -947,17 +966,13 @@
     bucket_a.s5()
     bucket_r.s4()
     bucket_c.s4()
-    bucket_q.s4()
     bucket_a.s6()
     move(1, bucket_a.done, big_a)
     bucket_b.s5()
-    bucket_q.s5()
     bucket_b.s6()
     move(4, bucket_b.done, big_b)
     bucket_r.s5()
     bucket_c.s5()
-    bucket_q.s6()
-    move(3, bucket_q.done, big_q)
     bucket_r.s6()
     move(2, bucket_r.done, big_r)
     bucket_c.s6()
@@ -985,11 +1000,11 @@
         (out_a, in_o), (big_e, in_e), (gimg_a, in_g), (big_r, in_r), (big_a, in_a), (big_b, in_b), (big_c, in_c),
         (big_q, in_q), (vectors, in_v),
     ])]
-    outs = []
     narrow = grad_expand.shape[0]
     taps, split = grad_split.shape
     half = split // 2
     inner = grad_excite.shape[0]
+    outs = []
     ins[0].wait()
     outs.append(move(9, in_o, output))
     ins[1].wait()
@@ -1023,15 +1038,12 @@
     ins[7].wait()
     outs.append(move(15, in_q, grad_squeeze))
     ins[8].wait()
-    grad_bias_three[...] = in_v[0:1, :]
-    grad_gain_three[...] = in_v[1:2, :]
-    grad_bias_two[...] = in_v[2:3, 0:split]
-    grad_gain_two[...] = in_v[2:3, split : 2 * split]
-    grad_bias_one[...] = in_v[3:4, 0:narrow]
-    grad_gain_one[...] = in_v[3:4, narrow : 2 * narrow]
-    grad_bias_excite[...] = in_v[3:4, 2 * narrow : 2 * narrow + split]
-    grad_bias_mid[...] = in_v[4:5, 0:inner]
-    grad_gain_mid[...] = in_v[4:5, inner : 2 * inner]
+    for dst, line, at in [
+        (grad_bias_three, 0, 0), (grad_gain_three, 1, 0), (grad_bias_two, 2, 0), (grad_gain_two, 2, split),
+        (grad_bias_one, 3, 0), (grad_gain_one, 3, narrow), (grad_bias_excite, 3, 2 * narrow),
+        (grad_bias_mid, 4, 0), (grad_gain_mid, 4, inner),
+    ]:
+        dst[...] = in_v[line : line + 1, at : at + dst.shape[1]]
     for copy in outs:
         copy.wait()
 
@@ -1073,6 +1085,7 @@
         return [pltpu.VMEM(dims, kind) for dims in shapes]
 
     messages = [(3, 2, 128), (8, 128), (8, 128), (16, 128), (16, 128), (5, 2, 128), (8, 128), (8, 128), (8, 128)]
+    kinds = [BF16 if k == 4 else F32 for k in range(len(messages))]
     vm = pltpu.VMEM
     scratch = (
         [vm((1, k), F32) for k in (narrow, narrow, split, split, inner, inner, split, width, width)]
@@ -1092,14 +1105,16 @@
         + [vm((width, pixels), BF16), vm((half, pixels), BF16), vm((3, narrow, padded), BF16), vm((slots, split), F32),
            vm((block, split), F32), vm((block, half), F32), vm((slots, half), F32), vm((n_batch, slots, inner), F32),
            vm((16, 128), F32)]
-        + [vm(dims, F32) for dims in messages] + [vm((16, 128), F32)] * 2 + [vm((slots, inner), F32)]
-        + [vm((total // 2 if dims[0] == 16 else total,) + dims, F32) for dims in messages[:-2]]
+        + [vm(dims, kinds[k]) for k, dims in enumerate(messages)] + [vm((16, 128), F32)] * 2 + [vm((8, width), F32)]
+        + [vm((n_height, slots, half), F32), vm((slots, half), F32), vm((n_batch, slots, half), F32), vm((slots, inner), F32),
+           vm((n_batch, slots, inner), F32), vm((narrow, inner), F32), vm((slots, inner), F32)]
+        + [vm((total // 2 if k == 3 else total,) + dims, kinds[k]) for k, dims in enumerate(messages[:-2])]
         + [vm((n_height,) + messages[-1], F32), vm((n_batch,) + messages[-1], F32)] + [vm((n_height, slots, inner), F32)]
         + [vm((block, narrow), F32)] * 4 + [vm((block, split), BF16)] * 4 + [vm((block, half), BF16)] * 4
-        + [pltpu.SemaphoreType.DMA((k,)) for k in (17, 13, 13, 8, 8, 6, 6, 56, 56)]
-        + bucket(size_e) + bucket(size_r) * 2 + bucket(narrow, inner, F32) + bucket(size_a) * 2 + bucket(size_c)
+        + [pltpu.SMEM((1,), jnp.int32), pltpu.SMEM((rows,), jnp.int32)]
+        + [pltpu.SemaphoreType.DMA((k,)) for k in (19, 16, 16, 8, 8, 6, 6, 48, 48)]
+        + bucket(size_e) + bucket(size_r) * 2 + bucket(size_a) * 2 + bucket(size_c)
     )
-    smem = pl.BlockSpec(memory_space=pltpu.SMEM)
     vmem = pl.BlockSpec(memory_space=pltpu.VMEM)
     hbm = pl.BlockSpec(memory_space=pltpu.HBM)
     shape = jax.ShapeDtypeStruct
@@ -1119,8 +1134,8 @@
             shape((narrow, inner), F32),
             shape((8, width), F32),
         ),
-        in_specs=[smem, smem] + [hbm] * 16,
-        out_specs=[hbm] * 8 + [vmem],
+        in_specs=[hbm] * 18,
+        out_specs=[hbm] * 9,
         scratch_shapes=scratch,
         compiler_params=pltpu.CompilerParams(
             collective_id=0, has_side_effects=True, vmem_limit_bytes=58 * 1024 * 1024

time: 95.8 us -> 92.5 us (0.966)
  Pallas kernels: 94.1 us -> 90.8 us
    pallas_call x1, Pallas kernels: 89.4 us -> 86.1 us  [shards(): pl.pallas_call(functools.partial(main_kernel, n_batch, n_height, (slots,...]
where the time goes in v4:
time: 92.5 us; the launch traced here: 92.3 us
  Pallas kernels  90.8 us (98%)
  between operations  1.47 us (2%)
    pallas_call x1, Pallas kernels, shards(): pl.pallas_call(functools.partial(main_kernel, n_batch, n_height, (slots,...  86.1 us
    pallas_call x1, Pallas kernels, shards(): pl.pallas_call(unpack_kernel, out_shape=(shape(flat, BF16), shape(flat, B...  4.76 us

profile of v4, /device:TPU:1, one launch (start us, length us, event | category | flops | bytes accessed | tf_op | source)
XLA Modules:
  0.0 92.3 jit_solution(4154547876563338002)
XLA Ops:
  1.3 86.1 %shard_map.297 = (bf16[112,4,1024]{2,1,0:T(4,128)(2,1)}, bf16[112,4,1024]{2,1,0:T(4,128)(2,1)}, bf16[1024,256]{1,0:T(8,128)(2,1)}, bf16[1024,256]{1,0:T(8,128)(2...) custom-call(s32[1]{0:T(128)S(6)} %copy.34.refs_0_, ...), custom_call_target="tpu_custom_call" | custom-call | tf_op jit(solution)/shard_map/pallas_call | solution.py:1129
  87.4 4.8 %shard_map.298 = (bf16[112,4,1024]{2,1,0:T(4,128)(2,1)}, bf16[112,4,1024]{2,1,0:T(4,128)(2,1)}, f32[1024,256]{1,0:T(8,128)}, f32[1152,512]{1,0:T(8,128)}, f32[25...) custom-call(bf16[112,4,1024]{2,1,0:T(4,128)(2,1)} %get-tuple-element, ...), custom_call_target="tpu_custom_call" | custom-call | tf_op jit(solution)/shard_map/pallas_call | solution.py:1152

commit v5 on v4

--- a/solution.py
+++ b/solution.py
@@ -859,17 +859,15 @@
         rhs = jnp.concatenate([gc2[block:pixels, lanes], gc2_own[:, lanes]], axis=0)
         put_taps(k * 3 * cg, dot(lhs, rhs))
 
-    begun = []
-    for k in range(6):
+    for k in range(3):
         taps_grad(k)
-        ready = 0
-        for bucket in taps_buckets[:2]:
-            ready += bucket.full.shape[0]
-            if ready <= (k + 1) * 3 * cg and bucket not in begun:
-                begun.append(bucket)
-                bucket.s0()
+    bucket_a.s0()
+    for k in range(3, 6):
+        taps_grad(k)
+    exchange(em_sum, em_b, 15, b, lambda t: (t, h))
+    bucket_a.s1()
     bucket_e.s2()
-    exchange(em_sum, em_b, 15, b, lambda t: (t, h))
+    bucket_b.s0()
     for gr in range(2):
         outs = []
         for bb in range(3):
@@ -888,17 +886,13 @@
         gh[:, gr * cg : (gr + 1) * cg] = (
             outs[1] + pltpu.roll(outs[2], 1, axis=0) + pltpu.roll(outs[0], pixels - 1, axis=0)
         )
-
-    bucket_a.s1()
     bucket_b.s1()
-
     def back_hidden(r, carry):
         value = gh[block_at(r), :] * slope1[block_at(r), :]
         gh[block_at(r), :] = value
         d1[block_at(r), :] = value.astype(BF16)
         norm = c1[block_at(r + 1), :] * inv_one - shift_one
         return carry[0] + colsum(value), carry[1] + colsum(value * norm)
-
     zero = jnp.zeros((1, narrow), F32)
     sums = lax.fori_loop(0, rows, back_hidden, (zero, zero))
     put_rows(m10, 0, sums[0])
@@ -926,12 +920,10 @@
     k_one = scale_one
     k_three = k_one * inv_one * gg
     k_two = k_one * (gb_one / m_one - shift_one * gg)
-
     def back_one(r, carry):
         value = gh[block_at(r), :] * k_one - k_two - c1[block_at(r + 1), :] * k_three
         gc1[block_at(r), :] = (value * mask(own(r + 1), narrow)).astype(BF16)
         return carry
-
     lax.fori_loop(0, rows, back_one, 0)
     bucket_r.final = lambda value: scale_one * (value - kept_n * gg)
     arrive(("all", 14))
@@ -942,14 +934,12 @@
     squeeze_grad[...] = dot(pool_b[...].reshape(every, half), sq_grads, TN, HIGHEST)
     move(3, squeeze_grad, big_q)
     arrive(("move", 7))
-
+    bucket_a.s3()
     def back_image(r, carry):
         value = d3[block_at(r), :] + dot(gc1[block_at(r), :], w_reduce[...], NT)
         xo[block_at(r), :] = value.astype(BF16)
         return carry
-
     lax.fori_loop(0, rows, back_image, 0)
-    bucket_a.s3()
     bucket_r.s2()
     bucket_e.s4()
     bucket_c.s2()

time: 92.5 us -> 90.6 us (0.979)
  Pallas kernels: 90.8 us -> 88.9 us
    pallas_call x1, Pallas kernels: 86.1 us -> 84.2 us  [shards(): pl.pallas_call(functools.partial(main_kernel, n_batch, n_height, (slots,...]
where the time goes in v5:
time: 90.6 us; the launch traced here: 90.4 us
  Pallas kernels  88.9 us (98%)
  between operations  1.47 us (2%)
    pallas_call x1, Pallas kernels, shards(): pl.pallas_call(functools.partial(main_kernel, n_batch, n_height, (slots,...  84.2 us
    pallas_call x1, Pallas kernels, shards(): pl.pallas_call(unpack_kernel, out_shape=(shape(flat, BF16), shape(flat, B...  4.76 us

profile of v5, /device:TPU:1, one launch (start us, length us, event | category | flops | bytes accessed | tf_op | source)
XLA Modules:
  0.0 90.4 jit_solution(6673855784325896653)
XLA Ops:
  1.3 84.2 %shard_map.297 = (bf16[112,4,1024]{2,1,0:T(4,128)(2,1)}, bf16[112,4,1024]{2,1,0:T(4,128)(2,1)}, bf16[1024,256]{1,0:T(8,128)(2,1)}, bf16[1024,256]{1,0:T(8,128)(2...) custom-call(s32[1]{0:T(128)S(6)} %copy.34.refs_0_, ...), custom_call_target="tpu_custom_call" | custom-call | tf_op jit(solution)/shard_map/pallas_call | solution.py:1119
  85.5 4.8 %shard_map.298 = (bf16[112,4,1024]{2,1,0:T(4,128)(2,1)}, bf16[112,4,1024]{2,1,0:T(4,128)(2,1)}, f32[1024,256]{1,0:T(8,128)}, f32[1152,512]{1,0:T(8,128)}, f32[25...) custom-call(bf16[112,4,1024]{2,1,0:T(4,128)(2,1)} %get-tuple-element, ...), custom_call_target="tpu_custom_call" | custom-call | tf_op jit(solution)/shard_map/pallas_call | solution.py:1142

commit v6 on v5

--- a/solution.py
+++ b/solution.py
@@ -711,13 +711,12 @@
     send_all(m6, s6, 4)
     pad_out(xo, out4)
     move(7, out4, output)
-    bucket_n.s2()
+
+    sum_all(s6, 4)
     arrive(("all", 10))
     st_sum[...] = jnp.sum(st_h[...], axis=0)
     st_low[...] = st_sum[...].astype(BF16)
     exchange(st_low, st_b, 11, b, lambda t: (t, h))
-
-    sum_all(s6, 4)
     gb_three = get_rows(tot, 0, wide)
     gg_three = get_rows(tot, wide, wide)
     vectors[0:1, :] = gb_three
@@ -782,6 +781,7 @@
     put_rows(m78, 2 * split // 128 + 1, colsum(em_part * norm_mid))
     send_all(m78, s78, 5)
     exchange(em_src, em_all, 9, h, lambda t: (b, t))
+    bucket_n.s2()
     set_edges(gm, first3, last3)
     halo_start(first3, last3, up3, down3, 2)
     for j in range(width // 256):

time: 90.6 us -> 90.2 us (level)
  no operation moved by 1% of the time
where the time goes in v6:
time: 90.2 us; the launch traced here: 90 us
  Pallas kernels  88.6 us (98%)
  between operations  1.47 us (2%)
    pallas_call x1, Pallas kernels, shards(): pl.pallas_call(functools.partial(main_kernel, n_batch, n_height, (slots,...  83.8 us
    pallas_call x1, Pallas kernels, shards(): pl.pallas_call(unpack_kernel, out_shape=(shape(flat, BF16), shape(flat, B...  4.76 us

profile of v6, /device:TPU:1, one launch (start us, length us, event | category | flops | bytes accessed | tf_op | source)
XLA Modules:
  0.0 90.0 jit_solution(9621946607128790060)
XLA Ops:
  1.3 83.8 %shard_map.297 = (bf16[112,4,1024]{2,1,0:T(4,128)(2,1)}, bf16[112,4,1024]{2,1,0:T(4,128)(2,1)}, bf16[1024,256]{1,0:T(8,128)(2,1)}, bf16[1024,256]{1,0:T(8,128)(2...) custom-call(s32[1]{0:T(128)S(6)} %copy.34.refs_0_, ...), custom_call_target="tpu_custom_call" | custom-call | tf_op jit(solution)/shard_map/pallas_call | solution.py:1119
  85.1 4.8 %shard_map.298 = (bf16[112,4,1024]{2,1,0:T(4,128)(2,1)}, bf16[112,4,1024]{2,1,0:T(4,128)(2,1)}, f32[1024,256]{1,0:T(8,128)}, f32[1152,512]{1,0:T(8,128)}, f32[25...) custom-call(bf16[112,4,1024]{2,1,0:T(4,128)(2,1)} %get-tuple-element, ...), custom_call_target="tpu_custom_call" | custom-call | tf_op jit(solution)/shard_map/pallas_call | solution.py:1142
